TPU v7x, 32 devices: a whole 2x2x4 slice. The times are simulated.
32 devices in a mesh: dp: 4 (over z), seq: 8 (over y, x, core).
Axes of the slice: x: 2, y: 2, z: 4, core: 2. Of those that a mesh axis runs over, the one named last changes fastest.
Arguments:
- inputs: float32 [8, 2048, 512], P('dp', 'seq'), may hold values from -6 to 6
- out_grad: float32 [8, 2048, 512], P('dp', 'seq'), may hold values from -6 to 6
- ln_gain: float32 [2, 512], P(None, 'dp'), may hold values from 0.1 to 1.9
- ln_bias: float32 [2, 512], P(None, 'dp'), may hold values from -3 to 3
- nu_log: float32 [2, 256], P(None, 'dp'), may hold values from -12 to -3
- theta_log: float32 [2, 256], P(None, 'dp'), may hold values from -5 to 0
- gamma_log: float32 [2, 256], P(None, 'dp'), may hold values from -7 to -1
- in_map: float32 [2, 512, 512], P(None, 'dp'), may hold values from -0.25 to 0.25
- out_map: float32 [2, 512, 512], P(None, 'dp'), may hold values from -0.25 to 0.25
- skip_gain: float32 [2, 512], P(None, 'dp'), may hold values from -4 to 4
- glu_weight: float32 [2, 512, 1024], P(None, 'dp'), may hold values from -0.25 to 0.25
- glu_bias: float32 [2, 1024], P(None, 'dp'), may hold values from -3 to 3
Outputs:
- output: float32 [8, 2048, 512], P('dp', 'seq')
- input_grad: float32 [8, 2048, 512], P('dp', 'seq')
- grad_ln_gain: float32 [2, 512], P(None, 'dp')
- grad_ln_bias: float32 [2, 512], P(None, 'dp')
- grad_nu_log: float32 [2, 256], P(None, 'dp')
- grad_theta_log: float32 [2, 256], P(None, 'dp')
- grad_gamma_log: float32 [2, 256], P(None, 'dp')
- grad_in_map: float32 [2, 512, 512], P(None, 'dp')
- grad_out_map: float32 [2, 512, 512], P(None, 'dp')
- grad_skip_gain: float32 [2, 512], P(None, 'dp')
- grad_glu_weight: float32 [2, 512, 1024], P(None, 'dp')
- grad_glu_bias: float32 [2, 1024], P(None, 'dp')
All inputs are finite; a program needn't handle non-finite values.
Results may differ from a plain program's by a relative error of at most 0.0004.
Values sent between devices are 32-bit elements; how exact they have to be, the bound alone decides.
No kernel may reach another device: no remote copies, remote signals or barrier semaphores. Data moves between devices by JAX's collectives and lax.ppermute only.
A program may use at most 192 MiB of HBM per device.

v0:
```python
import jax
import jax.numpy as jnp
from jax import lax
from jax.sharding import PartitionSpec as P

norm_eps = 1e-05


def carried_in(part, axis, combine, identity, reverse):
    count = lax.axis_size(axis)
    place = lax.axis_index(axis)
    ahead = count - 1 - place if reverse else place
    gathered = jax.tree.map(lambda a: lax.all_gather(a, axis), part)
    state = jax.tree.map(lambda a, e: jnp.zeros_like(a) + jnp.asarray(e, a.dtype), part, identity)

    def one(lap, state):
        source = count - 1 - lap if reverse else lap
        return combine(
            state, jax.tree.map(lambda a: lax.dynamic_index_in_dim(a, source, 0, False), gathered)
        )

    return lax.fori_loop(0, ahead, one, state)


def matmul(left_side, right_side):
    return jnp.dot(
        left_side, right_side, precision=lax.Precision.HIGHEST, preferred_element_type=jnp.float32
    )


def table_product(table, values):
    return jnp.einsum(
        "tsn,bsn->btn",
        table,
        values,
        precision=lax.Precision.HIGHEST,
        preferred_element_type=jnp.float32,
    )


def layer_norm(activation, norm_gain, norm_bias):
    centred = activation - jnp.mean(activation, -1, keepdims=True)
    spread = jnp.mean(centred * centred, -1, keepdims=True)
    return centred * lax.rsqrt(spread + norm_eps) * norm_gain + norm_bias


def decay_powers(nu_part, theta_part, step_counts, turn=1.0):
    rate = jnp.exp(nu_part)
    angle = jnp.exp(theta_part)
    modulus = jnp.exp(-step_counts * rate)
    return (modulus * jnp.cos(step_counts * angle), turn * modulus * jnp.sin(step_counts * angle))


def combine_pairs(earlier, later_pair):
    early_ar, early_ai, early_br, early_bi = earlier
    late_ar, late_ai, late_br, late_bi = later_pair
    return (
        early_ar * late_ar - early_ai * late_ai,
        early_ar * late_ai + early_ai * late_ar,
        late_ar * early_br - late_ai * early_bi + late_br,
        late_ar * early_bi + late_ai * early_br + late_bi,
    )


def front_half(activation, norm_gain, norm_bias, in_weight, gamma_part):
    normed = layer_norm(activation, norm_gain, norm_bias)
    gamma = jnp.exp(gamma_part)
    return (normed, matmul(normed, in_weight) * jnp.concatenate([gamma, gamma]))


def stretch_states(driven, nu_part, theta_part, turn):
    stretch_len = driven.shape[0]
    half_width = driven.shape[1] // 2
    span_len = min(16, stretch_len)
    span_count = stretch_len // span_len
    drive_re = driven[:, :half_width].reshape(span_count, span_len, half_width)
    drive_im = driven[:, half_width:].reshape(span_count, span_len, half_width)
    inner = jnp.arange(span_len)
    inner_gap = inner[:, None] - inner[None, :]
    inner_mask = (inner_gap >= 0).astype(jnp.float32)[:, :, None]
    table_re, table_im = decay_powers(
        nu_part, theta_part, jnp.maximum(inner_gap, 0).astype(jnp.float32)[:, :, None], turn
    )
    table_re = table_re * inner_mask
    table_im = table_im * inner_mask
    local_re = table_product(table_re, drive_re) - table_product(table_im, drive_im)
    local_im = table_product(table_re, drive_im) + table_product(table_im, drive_re)
    final_re = local_re[:, -1][None]
    final_im = local_im[:, -1][None]
    outer = jnp.arange(span_count)
    outer_gap = outer[:, None] - outer[None, :] - 1
    outer_mask = (outer_gap >= 0).astype(jnp.float32)[:, :, None]
    cross_re, cross_im = decay_powers(
        nu_part,
        theta_part,
        (jnp.maximum(outer_gap, 0) * span_len).astype(jnp.float32)[:, :, None],
        turn,
    )
    cross_re = cross_re * outer_mask
    cross_im = cross_im * outer_mask
    enter_re = (table_product(cross_re, final_re) - table_product(cross_im, final_im))[0]
    enter_im = (table_product(cross_re, final_im) + table_product(cross_im, final_re))[0]
    lift_re, lift_im = decay_powers(
        nu_part, theta_part, (inner + 1).astype(jnp.float32)[:, None], turn
    )
    state_re = local_re + lift_re[None] * enter_re[:, None] - lift_im[None] * enter_im[:, None]
    state_im = local_im + lift_re[None] * enter_im[:, None] + lift_im[None] * enter_re[:, None]
    return jnp.concatenate(
        [state_re.reshape(stretch_len, half_width), state_im.reshape(stretch_len, half_width)], 1
    )


def add_entry(local_states, power_re, power_im, entry_re, entry_im):
    return local_states + jnp.concatenate(
        [power_re * entry_re - power_im * entry_im, power_re * entry_im + power_im * entry_re], 1
    )


def back_half(activation, normed, states, out_weight, skip_part, glu_part, glu_shift):
    mixed = matmul(states, out_weight) + skip_part * normed
    active = jax.nn.gelu(mixed)
    both = matmul(active, glu_part) + glu_shift
    width_now = activation.shape[1]
    return activation + both[:, :width_now] * jax.nn.sigmoid(both[:, width_now:])


def body(
    inputs,
    out_grad,
    ln_gain,
    ln_bias,
    nu_log,
    theta_log,
    gamma_log,
    in_map,
    out_map,
    skip_gain,
    glu_weight,
    glu_bias,
):
    layer_count = in_map.shape[0]
    stretch_len = inputs.shape[1]
    state_width = nu_log.shape[1] * lax.axis_size("dp")
    unit_one = jnp.ones((state_width,), jnp.float32)
    unit_zero = jnp.zeros((state_width,), jnp.float32)
    identity = (unit_one, unit_zero, unit_zero, unit_zero)
    step_counts = jnp.arange(1, stretch_len + 1, dtype=jnp.float32)[:, None]
    running = None
    outputs = []
    input_grads = []
    for micro_num in range(inputs.shape[0]):
        fwd_weights = (
            lax.all_gather(ln_gain, "dp", axis=1, tiled=True),
            lax.all_gather(ln_bias, "dp", axis=1, tiled=True),
            lax.all_gather(nu_log, "dp", axis=1, tiled=True),
            lax.all_gather(theta_log, "dp", axis=1, tiled=True),
            lax.all_gather(gamma_log, "dp", axis=1, tiled=True),
            lax.all_gather(in_map, "dp", axis=1, tiled=True),
            lax.all_gather(out_map, "dp", axis=1, tiled=True),
            lax.all_gather(skip_gain, "dp", axis=1, tiled=True),
            lax.all_gather(glu_weight, "dp", axis=1, tiled=True),
            lax.all_gather(glu_bias, "dp", axis=1, tiled=True),
        )
        activation = inputs[micro_num]
        kept_layers = []
        for layer_num in range(layer_count):
            weights = tuple((item[layer_num] for item in fwd_weights))
            normed, driven = front_half(activation, weights[0], weights[1], weights[5], weights[4])
            local_states = stretch_states(driven, weights[2], weights[3], 1.0)
            power_re, power_im = decay_powers(weights[2], weights[3], step_counts)
            carry_pair = (
                power_re[-1],
                power_im[-1],
                local_states[-1, :state_width],
                local_states[-1, state_width:],
            )
            entry_sum = carried_in(carry_pair, "seq", combine_pairs, identity, False)
            entry_re, entry_im = (entry_sum[2], entry_sum[3])
            states = add_entry(local_states, power_re, power_im, entry_re, entry_im)
            kept_layers.append((activation, entry_re, entry_im))
            activation = back_half(
                activation, normed, states, weights[6], weights[7], weights[8], weights[9]
            )
        outputs.append(activation)
        behind = (
            lax.all_gather(ln_gain, "dp", axis=1, tiled=True),
            lax.all_gather(ln_bias, "dp", axis=1, tiled=True),
            lax.all_gather(nu_log, "dp", axis=1, tiled=True),
            lax.all_gather(theta_log, "dp", axis=1, tiled=True),
            lax.all_gather(gamma_log, "dp", axis=1, tiled=True),
            lax.all_gather(in_map, "dp", axis=1, tiled=True),
            lax.all_gather(out_map, "dp", axis=1, tiled=True),
            lax.all_gather(skip_gain, "dp", axis=1, tiled=True),
            lax.all_gather(glu_weight, "dp", axis=1, tiled=True),
            lax.all_gather(glu_bias, "dp", axis=1, tiled=True),
        )
        adjoint = out_grad[micro_num]
        layer_grads = [None] * layer_count
        for layer_num in reversed(range(layer_count)):
            weights = tuple((item[layer_num] for item in behind))
            layer_input, entry_re, entry_im = kept_layers[layer_num]
            (normed, driven), front_pull = jax.vjp(
                front_half, layer_input, weights[0], weights[1], weights[5], weights[4]
            )
            power_re, power_im = decay_powers(weights[2], weights[3], step_counts)
            states = add_entry(
                stretch_states(driven, weights[2], weights[3], 1.0),
                power_re,
                power_im,
                entry_re,
                entry_im,
            )
            _, tail_pull = jax.vjp(
                back_half,
                layer_input,
                normed,
                states,
                weights[6],
                weights[7],
                weights[8],
                weights[9],
            )
            d_resid, d_normed, d_states, d_out_map, d_skip, d_glu_w, d_glu_b = tail_pull(adjoint)
            flipped = jnp.flip(d_states, 0)
            local_adj = stretch_states(flipped, weights[2], weights[3], -1.0)
            carry_pair = (
                power_re[-1],
                -power_im[-1],
                local_adj[-1, :state_width],
                local_adj[-1, state_width:],
            )
            later_sum = carried_in(carry_pair, "seq", combine_pairs, identity, True)
            later_re, later_im = (later_sum[2], later_sum[3])
            adj_full = jnp.flip(add_entry(local_adj, power_re, -power_im, later_re, later_im), 0)
            adj_re = adj_full[:, :state_width]
            adj_im = adj_full[:, state_width:]
            entry_row = jnp.concatenate([entry_re, entry_im])[None, :]
            before = jnp.concatenate([entry_row, states[:-1]], 0)
            before_re = before[:, :state_width]
            before_im = before[:, state_width:]
            dlam_re = jnp.sum(adj_re * before_re + adj_im * before_im, 0)
            dlam_im = jnp.sum(adj_im * before_re - adj_re * before_im, 0)
            lam_re, lam_im = decay_powers(weights[2], weights[3], 1.0)
            rate = jnp.exp(weights[2])
            angle = jnp.exp(weights[3])
            d_nu = -rate * (dlam_re * lam_re + dlam_im * lam_im)
            d_theta = angle * (dlam_im * lam_re - dlam_re * lam_im)
            d_activ, d_gain, d_bias, d_in_map, d_gamma = front_pull((d_normed, adj_full))
            adjoint = d_resid + d_activ
            layer_grads[layer_num] = (
                d_gain,
                d_bias,
                d_nu,
                d_theta,
                d_gamma,
                d_in_map,
                d_out_map,
                d_skip,
                d_glu_w,
                d_glu_b,
            )
        input_grads.append(adjoint)
        stacked = tuple(
            (
                jnp.stack([layer_grads[layer_num][member] for layer_num in range(layer_count)])
                for member in range(10)
            )
        )
        if running is None:
            running = stacked
        else:
            running = tuple((old_sum + new_sum for old_sum, new_sum in zip(running, stacked)))
    g_gain, g_bias, g_nu, g_theta, g_gamma, g_in_map, g_out_map, g_skip, g_glu_w, g_glu_b = running
    summed = lax.psum(
        (g_gain, g_bias, g_nu, g_theta, g_gamma, g_in_map, g_out_map, g_skip, g_glu_w, g_glu_b),
        "seq",
    )
    s_gain, s_bias, s_nu, s_theta, s_gamma, s_in_map, s_out_map, s_skip, s_glu_w, s_glu_b = summed
    shares = (
        lax.psum_scatter(s_gain, "dp", scatter_dimension=1, tiled=True),
        lax.psum_scatter(s_bias, "dp", scatter_dimension=1, tiled=True),
        lax.psum_scatter(s_nu, "dp", scatter_dimension=1, tiled=True),
        lax.psum_scatter(s_theta, "dp", scatter_dimension=1, tiled=True),
        lax.psum_scatter(s_gamma, "dp", scatter_dimension=1, tiled=True),
        lax.psum_scatter(s_in_map, "dp", scatter_dimension=1, tiled=True),
        lax.psum_scatter(s_out_map, "dp", scatter_dimension=1, tiled=True),
        lax.psum_scatter(s_skip, "dp", scatter_dimension=1, tiled=True),
        lax.psum_scatter(s_glu_w, "dp", scatter_dimension=1, tiled=True),
        lax.psum_scatter(s_glu_b, "dp", scatter_dimension=1, tiled=True),
    )
    output = jnp.stack(outputs)
    input_grad = jnp.stack(input_grads)
    return (
        output,
        input_grad,
        shares[0],
        shares[1],
        shares[2],
        shares[3],
        shares[4],
        shares[5],
        shares[6],
        shares[7],
        shares[8],
        shares[9],
    )


def solution(mesh):
    in_specs = (
        P("dp", "seq", None),
        P("dp", "seq", None),
        P(None, "dp"),
        P(None, "dp"),
        P(None, "dp"),
        P(None, "dp"),
        P(None, "dp"),
        P(None, "dp", None),
        P(None, "dp", None),
        P(None, "dp"),
        P(None, "dp", None),
        P(None, "dp"),
    )
    out_specs = (
        P("dp", "seq", None),
        P("dp", "seq", None),
        P(None, "dp"),
        P(None, "dp"),
        P(None, "dp"),
        P(None, "dp"),
        P(None, "dp"),
        P(None, "dp", None),
        P(None, "dp", None),
        P(None, "dp"),
        P(None, "dp", None),
        P(None, "dp"),
    )
    return jax.shard_map(body, mesh=mesh, in_specs=in_specs, out_specs=out_specs, check_vma=False)
```

profile of v0, /device:TPU:9, one launch (start us, length us, event | category | flops | bytes accessed | tf_op | source)
XLA Modules:
  0.0 1748.3 jit_solution(4369832243427333768)
XLA Ops:
  58.4 20.1 %all-gather.3 = f32[8,1,256]{2,1,0:T(1,128)S(1)} all-gather(f32[1,1,256]{2,1,0:T(1,128)S(1)} %slice_bitcast_fusion.111), channel_id=1, replica_groups=mesh['dp'=4,'seq'=8] {'seq'}, dimensions={0}, use_global_device_ids=true | all-gather | bytes 9216 | tf_op jit(solution)/shard_map/all_gather | solution.py:13
  120.2 13.9 fusion.134
  238.9 13.6 fusion.128
  454.0 13.6 fusion.68
  561.8 13.6 fusion.64
  731.4 13.8 fusion.86
  751.5 13.8 fusion.84
  776.0 13.4 fusion.52
  849.5 13.8 fusion.82
  869.7 14.0 fusion.80
  1050.8 13.8 fusion.146
  1071.3 13.8 fusion.144
  1095.8 13.4 fusion.112
  1169.0 13.8 fusion.150
  1189.2 14.0 fusion.148
  1448.4 80.7 %reduce-scatter.29.cloned.1.call-done = f32[2,128,1024]{2,1,0:T(8,128)} async-done(((f32[2,512,1024]{2,1,0:T(8,128)}), f32[2,128,1024]{2,1,0:T(8,128)}) %reduce-scatter.29.cloned.1.call-update) | async-done | bytes 1048592 | tf_op jit(solution)/shard_map/reduce_scatter | solution.py:288
  1532.9 13.6 reduce-scatter.35.cloned.1.call-done
  1547.4 18.8 %reduce-scatter.37.cloned.1.call-done = f32[64,2]{1,0:T(8,128)} async-done(((f32[256,2]{1,0:T(8,128)}), f32[64,2]{1,0:T(8,128)}) %reduce-scatter.37.cloned.1.call-update) | async-done | bytes 528
  1567.0 18.8 %reduce-scatter.39.cloned.1.call-done = f32[64,2]{1,0:T(8,128)} async-done(((f32[256,2]{1,0:T(8,128)}), f32[64,2]{1,0:T(8,128)}) %reduce-scatter.39.cloned.1.call-update) | async-done | bytes 528
  1586.6 20.2 %reduce-scatter.31.cloned.1.call-done = f32[128,2]{1,0:T(8,128)} async-done(((f32[512,2]{1,0:T(8,128)}), f32[128,2]{1,0:T(8,128)}) %reduce-scatter.31.cloned.1.call-update) | async-done | bytes 1040
  1607.7 19.0 %reduce-scatter.33.cloned.1.call-done = f32[128,2]{1,0:T(8,128)} async-done(((f32[512,2]{1,0:T(8,128)}), f32[128,2]{1,0:T(8,128)}) %reduce-scatter.33.cloned.1.call-update) | async-done | bytes 1040
  1627.6 19.4 %reduce-scatter.41.cloned.1.call-done = f32[128,2]{1,0:T(8,128)} async-done(((f32[512,2]{1,0:T(8,128)}), f32[128,2]{1,0:T(8,128)}) %reduce-scatter.41.cloned.1.call-update) | async-done | bytes 1040
  1648.0 22.2 %reduce-scatter.43.cloned.1.call-done = f32[256,2]{1,0:T(8,128)} async-done(((f32[1024,2]{1,0:T(8,128)}), f32[256,2]{1,0:T(8,128)}) %reduce-scatter.43.cloned.1.call-update) | async-done | bytes 2064
  1684.4 52.4 %all-reduce.12.cloned.1.call-done = (f32[2,128,512]{2,1,0:T(8,128)}, f32[2,128,512]{2,1,0:T(8,128)}, f32[2,128,1024]{2,1,0:T(8,128)}) async-done(((f32[2,128,512]{2,1,0:T(8,128)}, f32[2,128,512]{2,1,0:T(8,128)}, f32[2,128,1024]{2,1,0:T(8,128)}), (f32[2,128,512]{2,1,0:T(8,128)}, f32[2,128,512]{2,1,0:T(8,128)}, f32[2,128,1024]{2,1,0:T(8,128)})) %all-reduce.12.cloned.1.call-update) | async-done | bytes 2097168 | tf_op jit(solution)/shard_map/psum | solution.py:274
  (942 shorter events, 1264.7 us)
Async XLA Ops:
  7.3 100.6 %all-gather.29.cloned.1.call-start = ((), (), s32[]{:S(2)}) async-start(), calls=%async_computation.10 | async-start | bytes 2621440 | tf_op jit(solution)/shard_map/all_gather | solution.py:158
  8.0 406.5 %all-gather.31.cloned.1.call-start = ((), (), s32[]{:S(2)}) async-start(), calls=%async_computation.11 | async-start | bytes 2621440 | tf_op jit(solution)/shard_map/all_gather | solution.py:159
  8.7 78.6 %copy-start.218 = (f32[2,128]{1,0:T(2,128)S(1)}, f32[2,128]{1,0:T(2,128)}, u32[]{:S(2)}) copy-start(f32[2,128]{1,0:T(2,128)} %param.37) | copy-start | bytes 3076
  8.7 411.1 %all-gather.33.cloned.1.call-start = ((), (), s32[]{:S(2)}) async-start(), calls=%async_computation.12 | async-start | bytes 5242880 | tf_op jit(solution)/shard_map/all_gather | solution.py:161
  9.5 1427.6 %reduce-scatter.25.cloned.1.call-start = ((), (), s32[]{:S(2)}) async-start(), calls=%async_computation.13 | async-start | bytes 2621440 | tf_op jit(solution)/shard_map/reduce_scatter | solution.py:285
  9.6 301.5 %copy-start.196 = (f32[16,16]{1,0:T(8,128)}, f32[16,16]{1,0:T(8,128)S(1)}, u32[]{:S(2)}) copy-start(f32[16,16]{1,0:T(8,128)S(1)} %fusion.645) | copy-start | bytes 3076
  9.6 301.5 %copy-start.200 = (f32[16,16]{1,0:T(8,128)}, f32[16,16]{1,0:T(8,128)S(1)}, u32[]{:S(2)}) copy-start(f32[16,16]{1,0:T(8,128)S(1)} %multiply_convert_fusion) | copy-start | bytes 3076
  10.2 369.5 %copy-start.178 = (f32[256]{0:T(256)}, f32[256]{0:T(256)S(1)}, u32[]{:S(2)}) copy-start(f32[256]{0:T(256)S(1)} %iota_add_fusion) | copy-start | bytes 3076
  10.3 369.5 %copy-start.181 = (f32[256]{0:T(256)}, f32[256]{0:T(256)S(1)}, u32[]{:S(2)}) copy-start(f32[256]{0:T(256)S(1)} %fusion.657) | copy-start | bytes 3076
  27.0 83.3 %copy-start.161 = (f32[512]{0:T(512)}, f32[512]{0:T(512)S(1)}, u32[]{:S(2)}) copy-start(f32[512]{0:T(512)S(1)} %pad_maximum_fusion.6) | copy-start | bytes 6148
  56.3 56.2 %copy-start.176 = (f32[256,2]{0,1:T(2,128)}, f32[256,2]{0,1:T(2,128)S(1)}, u32[]{:S(2)}) copy-start(f32[256,2]{0,1:T(2,128)S(1)} %reshape.1131) | copy-start | bytes 6148
  95.4 322.6 %copy-start.163 = (f32[1,512]{1,0:T(1,128)}, f32[1,512]{1,0:T(1,128)S(1)}, u32[]{:S(2)}) copy-start(f32[1,512]{1,0:T(1,128)S(1)} %get-tuple-element.1174) | copy-start | bytes 6148
  970.4 44.4 %copy-start.179 = (f32[256]{0:T(256)S(1)}, f32[256]{0:T(256)}, u32[]{:S(2)}) copy-start(f32[256]{0:T(256)} %copy-done.178) | copy-start | bytes 3076
  970.4 44.4 %copy-start.182 = (f32[256]{0:T(256)S(1)}, f32[256]{0:T(256)}, u32[]{:S(2)}) copy-start(f32[256]{0:T(256)} %copy-done.181) | copy-start | bytes 3076
  1363.5 84.8 %reduce-scatter.27.cloned.1.call-start = ((), (), s32[]{:S(2)}) async-start(), calls=%async_computation.14 | async-start | bytes 2621440 | tf_op jit(solution)/shard_map/reduce_scatter | solution.py:286
  1371.0 158.0 %reduce-scatter.29.cloned.1.call-start = ((), (), s32[]{:S(2)}) async-start(), calls=%async_computation.15 | async-start | bytes 5242880 | tf_op jit(solution)/shard_map/reduce_scatter | solution.py:288
  1384.1 162.4 %reduce-scatter.35.cloned.1.call-start = ((), (), s32[]{:S(2)}) async-start(), calls=%async_computation.18 | async-start | bytes 163840
  1425.1 141.1 %reduce-scatter.37.cloned.1.call-start = ((), (), s32[]{:S(2)}) async-start(), calls=%async_computation.19 | async-start | bytes 163840
  1427.4 158.4 %reduce-scatter.39.cloned.1.call-start = ((), (), s32[]{:S(2)}) async-start(), calls=%async_computation.20 | async-start | bytes 163840
  1428.3 178.5 %reduce-scatter.31.cloned.1.call-start = ((), (), s32[]{:S(2)}) async-start(), calls=%async_computation.16 | async-start | bytes 327680
  1431.1 195.6 %reduce-scatter.33.cloned.1.call-start = ((), (), s32[]{:S(2)}) async-start(), calls=%async_computation.17 | async-start | bytes 327680
  1433.6 213.5 %reduce-scatter.41.cloned.1.call-start = ((), (), s32[]{:S(2)}) async-start(), calls=%async_computation.21 | async-start | bytes 327680
  1435.9 234.2 %reduce-scatter.43.cloned.1.call-start = ((), (), s32[]{:S(2)}) async-start(), calls=%async_computation.22 | async-start | bytes 655360
  1437.0 299.8 %all-reduce.12.cloned.1.call-start = ((), (), s32[]{:S(2)}) async-start(), calls=%async_computation.23 | async-start | bytes 4194304 | tf_op jit(solution)/shard_map/psum | solution.py:274
  (209 other events, 1793.5 us)
Sparse Core Ops, SparseCore 0:
  9.7 45.5 all-gather.28
  56.8 44.6 all-gather.30
  103.1 78.8 all-gather.32
  1363.6 39.2 reduce-scatter.24
  1405.2 43.1 reduce-scatter.26
  1450.5 78.5 reduce-scatter.28
  1531.4 15.0 reduce-scatter.34
  1548.8 17.3 reduce-scatter.36
  1568.5 17.2 reduce-scatter.38
  1588.5 18.2 reduce-scatter.30
  1609.2 17.5 reduce-scatter.32
  1628.9 18.1 reduce-scatter.40
  1650.0 20.0 reduce-scatter.42
  1673.8 62.9 all-reduce.11
where the time goes:
time: 1760 us; the launch traced here: 1750 us
  matrix products  863 us (49%)
  waiting for transfers between devices  279 us (16%)
  blocking collectives  277 us (16%)
  local copies, waits for them, and re-layouts  238 us (14%)
  other arithmetic  71.8 us (4%)
  between operations  17.8 us (1%)
    dot_general x64, matrix products, table_product(): jnp.einsum('tsn,bsn->btn', table, values, precision=lax.Precision.HIGHEST...  793 us
    all_gather x22, blocking collectives, carried_in(): gathered = jax.tree.map(lambda a: lax.all_gather(a, axis), part)  211 us
    unnamed x21, waiting for transfers between devices  134 us
    reduce_scatter x1, waiting for transfers between devices, body(): lax.psum_scatter(s_glu_w, 'dp', scatter_dimension=1, tiled=True)  80.7 us
    dot_general x36, matrix products, matmul(): jnp.dot(left_side, right_side, precision=lax.Precision.HIGHEST, preferred...  70.5 us
    psum x1, waiting for transfers between devices, body(): lax.psum((g_gain, g_bias, g_nu, g_theta, g_gamma, g_in_map, g_out_map, g_...  52.4 us
    unnamed x498, local copies, waits for them, and re-layouts  37 us
  transfers between devices with their start and end apart: 14, of which 10 were waited for; matrix products, arithmetic and copies ran while one was open for 19% of the time, Pallas kernels for 0%

commit v1 on v0

v1 whole, which is shorter than its diff:
```python
import functools
import math

import jax
import jax.numpy as jnp
from jax import lax
from jax.experimental import pallas as pl
from jax.experimental.pallas import tpu as pltpu
from jax.sharding import PartitionSpec as P

NORM_EPS = 1e-05
GROUPS = 8
WIDE = 256
SMALL = 8
TABLE = 16
F32 = jnp.float32
BF16 = jnp.bfloat16
GELU_C = math.sqrt(2.0 / math.pi)

GAIN, BIAS, SKIP, BIAS_V, BIAS_G, GAMMA, LAM, LAM1, LAM2, LAM4, LAM8, RATES = range(12)


class Dims:
    def __init__(self, inputs, in_map, dp, seq):
        self.B, self.Tb, self.H = inputs.shape
        self.layers, self.Hd = in_map.shape[:2]
        self.N = self.H // 2
        self.T = self.B * self.Tb
        self.R = self.B * GROUPS
        self.L = self.Tb // GROUPS
        self.D, self.S = dp, seq
        self.q = max(16, self.Hd // seq)
        self.used = self.Hd // self.q


def cmul(ar, ai, br, bi):
    return ar * br - ai * bi, ar * bi + ai * br


def split(x):
    hi = x.astype(BF16)
    return hi, (x - hi.astype(F32)).astype(BF16)


def dot3(ah, al, bh, bl, dims):
    def one(a, b):
        return lax.dot_general(a, b, (dims, ((), ())), preferred_element_type=F32)

    return one(ah, bh) + (one(ah, bl) + one(al, bh))


def product(ah, al, wh, wl, dst, transposed=False, add=False):
    for n in range(dst.shape[1] // WIDE):
        cols = slice(n * WIDE, (n + 1) * WIDE)
        if transposed:
            res = dot3(ah[...], al[...], wh[cols, :], wl[cols, :], ((1,), (1,)))
        else:
            res = dot3(ah[...], al[...], wh[:, cols], wl[:, cols], ((1,), (0,)))
        dst[:, cols] = dst[:, cols] + res if add else res


def each_step(dim, fn, unroll=2, reverse=False, init=0):
    def one(i, carry):
        j = dim.L - 1 - i if reverse else i
        rows = pl.ds(pl.multiple_of(j * dim.R, dim.R), dim.R)
        return fn(j, rows, carry)

    return lax.fori_loop(0, dim.L, one, init, unroll=unroll)


def row(table, index, n=1):
    return table[index : index + n, :]


def lam_of(dim, table, index, reverse):
    pair = table[index : index + 1, :]
    real, imag = pair[:, : dim.N], pair[:, dim.N :]
    return real, -imag if reverse else imag


def chunk_scan(dim, table, yr, yi, reverse):
    place = lax.broadcasted_iota(jnp.int32, yr.shape, 0)
    for dist, index in ((1, LAM1), (2, LAM2), (4, LAM4)):
        pr, pi = lam_of(dim, table, index, reverse)
        if reverse:
            shift, seen = GROUPS - dist, place < GROUPS - dist
        else:
            shift, seen = dist, place >= dist
        sr = jnp.where(seen, pltpu.roll(yr, shift, 0), 0.0)
        si = jnp.where(seen, pltpu.roll(yi, shift, 0), 0.0)
        mr, mi = cmul(pr, pi, sr, si)
        yr, yi = yr + mr, yi + mi
    return yr, yi


def local_finals(dim, table, drive_ref, cf_ref, f_ref, reverse):
    lr, li = lam_of(dim, table, LAM, reverse)
    lr = jnp.broadcast_to(lr, (dim.R, dim.N))
    li = jnp.broadcast_to(li, (dim.R, dim.N))

    def step(j, rows, carry):
        d = drive_ref[rows, :]
        mr, mi = cmul(lr, li, *carry)
        return mr + d[:, : dim.N], mi + d[:, dim.N :]

    zero = jnp.zeros((dim.R, dim.N), F32)
    fr, fi = each_step(dim, step, 4, reverse, (zero, zero))
    cf_ref[:, : dim.N] = fr
    cf_ref[:, dim.N :] = fi
    last = 0 if reverse else GROUPS - 1
    for b in range(dim.B):
        rows = slice(b * GROUPS, (b + 1) * GROUPS)
        yr, yi = chunk_scan(dim, table, fr[rows], fi[rows], reverse)
        f_ref[b : b + 1, : dim.N] = yr[last : last + 1]
        f_ref[b : b + 1, dim.N :] = yi[last : last + 1]


def entries_of(dim, table, cf_ref, g_ref, en_ref, reverse):
    me = lax.axis_index("seq")
    lr, li = lam_of(dim, table, LAM8, reverse)
    xr = jnp.zeros((dim.B, dim.N), F32)
    xi = xr
    order = reversed(range(dim.S)) if reverse else range(dim.S)
    for other in order:
        ahead = other > me if reverse else other < me
        g = g_ref[other]
        mr, mi = cmul(lr, li, xr, xi)
        xr = jnp.where(ahead, mr + g[:, : dim.N], xr)
        xi = jnp.where(ahead, mi + g[:, dim.N :], xi)
    for b in range(dim.B):
        rows = slice(b * GROUPS, (b + 1) * GROUPS)
        f = cf_ref[rows, :]
        place = lax.broadcasted_iota(jnp.int32, f.shape, 0)
        x = jnp.concatenate([xr[b : b + 1], xi[b : b + 1]], 1)
        if reverse:
            y = jnp.where(place == GROUPS - 1, x, pltpu.roll(f, GROUPS - 1, 0))
        else:
            y = jnp.where(place == 0, x, pltpu.roll(f, 1, 0))
        yr, yi = chunk_scan(dim, table, y[:, : dim.N], y[:, dim.N :], reverse)
        en_ref[rows, : dim.N] = yr
        en_ref[rows, dim.N :] = yi


def norm_step(dim, x, table):
    mean = jnp.mean(x, -1, keepdims=True)
    centred = x - mean
    var = jnp.mean(centred * centred, -1, keepdims=True)
    rstd = lax.rsqrt(var + NORM_EPS)
    xhat = centred * rstd
    return xhat, rstd, xhat * row(table, GAIN) + row(table, BIAS)


def front(dim, load_act, table, w_in, xhat, rstd, drive, cf, fin, ah, al, wh, wl):
    def norm(j, rows, _):
        xh, rs, normed = norm_step(dim, load_act(j, rows), table)
        xhat[rows, :] = xh
        rstd[rows, :] = jnp.broadcast_to(rs, (dim.R, 128))
        ah[rows, :], al[rows, :] = split(normed)
        return 0

    each_step(dim, norm, 4)
    w_in.fill(wh, wl)
    product(ah, al, wh, wl, drive)

    def scale(j, rows, _):
        drive[rows, :] = drive[rows, :] * row(table, GAMMA)
        return 0

    each_step(dim, scale, 4)
    local_finals(dim, table, drive, cf, fin, False)


def gelu_parts(m):
    inner = GELU_C * (m + 0.044715 * (m * m * m))
    th = jnp.tanh(inner)
    return th


def back(dim, table, drive, cf, g, xhat, w_out, w_gv, w_gg, en, states, mixed, active, v, s, ah, al, wh, wl):
    entries_of(dim, table, cf, g, en, False)
    lr, li = lam_of(dim, table, LAM, False)
    lr = jnp.broadcast_to(lr, (dim.R, dim.N))
    li = jnp.broadcast_to(li, (dim.R, dim.N))

    def scan(j, rows, carry):
        d = drive[rows, :]
        mr, mi = cmul(lr, li, *carry)
        both = jnp.concatenate([mr + d[:, : dim.N], mi + d[:, dim.N :]], 1)
        states[rows, :] = both
        ah[rows, :], al[rows, :] = split(both)
        return both[:, : dim.N], both[:, dim.N :]

    each_step(dim, scan, 4, False, (en[:, : dim.N], en[:, dim.N :]))
    w_out.fill(wh, wl)
    product(ah, al, wh, wl, mixed)

    def gelu(j, rows, _):
        normed = xhat[rows, :] * row(table, GAIN) + row(table, BIAS)
        m = mixed[rows, :] + row(table, SKIP) * normed
        mixed[rows, :] = m
        a = (0.5 * m) * (1.0 + gelu_parts(m))
        active[rows, :] = a
        ah[rows, :], al[rows, :] = split(a)
        return 0

    each_step(dim, gelu, 2)
    w_gv.fill(wh, wl)
    product(ah, al, wh, wl, v)
    w_gg.fill(wh, wl)
    product(ah, al, wh, wl, s)


def gate(dim, table, v, s, rows):
    vv = v[rows, :] + row(table, BIAS_V)
    ss = jax.nn.sigmoid(s[rows, :] + row(table, BIAS_G))
    v[rows, :] = vv
    s[rows, :] = ss
    return vv * ss


def top(dim, table, load_dact, v, s, mixed, xhat, w_gv, w_gg, w_out, dv, dg, dmixed, ds, rcf, rfin, sums, ah, al, bh, bl, wh, wl):
    def dgate(j, rows, carry):
        dact = load_dact(j, rows)
        ss, vv = s[rows, :], v[rows, :]
        a = dact * ss
        b = a * vv * (1.0 - ss)
        dv[rows, :] = a
        dg[rows, :] = b
        ah[rows, :], al[rows, :] = split(a)
        bh[rows, :], bl[rows, :] = split(b)
        return carry[0] + a, carry[1] + b

    zero = jnp.zeros((dim.R, dim.H), F32)
    sv, sg = each_step(dim, dgate, 2, False, (zero, zero))
    sums[BIAS_V : BIAS_V + 1, :] = jnp.sum(sv, 0, keepdims=True)
    sums[BIAS_G : BIAS_G + 1, :] = jnp.sum(sg, 0, keepdims=True)
    w_gv.fill(wh, wl)
    product(ah, al, wh, wl, dmixed, True)
    w_gg.fill(wh, wl)
    product(bh, bl, wh, wl, dmixed, True, True)

    def dgelu(j, rows, carry):
        m = mixed[rows, :]
        th = gelu_parts(m)
        slope = 0.5 * (1.0 + th) + (0.5 * m) * (1.0 - th * th) * (GELU_C * (1.0 + (3 * 0.044715) * (m * m)))
        d = dmixed[rows, :] * slope
        dmixed[rows, :] = d
        ah[rows, :], al[rows, :] = split(d)
        normed = xhat[rows, :] * row(table, GAIN) + row(table, BIAS)
        return carry + d * normed

    sums[SKIP : SKIP + 1, :] = jnp.sum(each_step(dim, dgelu, 2, False, zero), 0, keepdims=True)
    w_out.fill(wh, wl)
    product(ah, al, wh, wl, ds, True)
    local_finals(dim, table, ds, rcf, rfin, True)


def bottom(dim, table, ds, rcf, gr, states, en, drive, xhat, rstd, dmixed, w_in, load_dact, store, dproj, buf, adj_en, sums, ah, al, wh, wl):
    entries_of(dim, table, rcf, gr, adj_en, True)
    lr, li = lam_of(dim, table, LAM, True)
    lr = jnp.broadcast_to(lr, (dim.R, dim.N))
    li = jnp.broadcast_to(li, (dim.R, dim.N))
    zero = jnp.zeros((dim.R, dim.N), F32)

    def scan(j, rows, carry):
        ar, ai, dr, di, dgam = carry
        d = ds[rows, :]
        mr, mi = cmul(lr, li, ar, ai)
        ar, ai = mr + d[:, : dim.N], mi + d[:, dim.N :]
        earlier = pl.ds(pl.multiple_of(jnp.maximum(j - 1, 0) * dim.R, dim.R), dim.R)
        before = jnp.where(j == 0, en[...], states[earlier, :])
        br, bi = before[:, : dim.N], before[:, dim.N :]
        dr = dr + (ar * br + ai * bi)
        di = di + (ai * br - ar * bi)
        u = drive[rows, :]
        dgam = dgam + (ar * u[:, : dim.N] + ai * u[:, dim.N :])
        dp = jnp.concatenate([ar, ai], 1) * row(table, GAMMA)
        dproj[rows, :] = dp
        ah[rows, :], al[rows, :] = split(dp)
        return ar, ai, dr, di, dgam

    start = (adj_en[:, : dim.N], adj_en[:, dim.N :], zero, zero, zero)
    _, _, dr, di, dgam = each_step(dim, scan, 2, True, start)
    dr, di, dgam = (jnp.sum(x, 0, keepdims=True) for x in (dr, di, dgam))
    fr, fi = lam_of(dim, table, LAM, False)
    rates = row(table, RATES)
    rate, angle = rates[:, : dim.N], rates[:, dim.N :]
    sums[5:6, : dim.N] = -rate * (dr * fr + di * fi)
    sums[5:6, dim.N :] = angle * (di * fr - dr * fi)
    sums[6:7, : dim.N] = dgam
    sums[6:7, dim.N :] = jnp.zeros_like(dgam)
    sums[7:8, :] = jnp.zeros((1, dim.H), F32)

    w_in.fill(wh, wl)
    product(ah, al, wh, wl, buf, True)
    wide = jnp.zeros((dim.R, dim.H), F32)

    def dnorm(j, rows, carry):
        dn = buf[rows, :] + dmixed[rows, :] * row(table, SKIP)
        xh = xhat[rows, :]
        dx = dn * row(table, GAIN)
        m1 = jnp.mean(dx, -1, keepdims=True)
        m2 = jnp.mean(dx * xh, -1, keepdims=True)
        store(j, rows, load_dact(j, rows) + rstd[rows, 0:1] * (dx - m1 - xh * m2))
        return carry[0] + dn * xh, carry[1] + dn

    sgain, sbias = each_step(dim, dnorm, 2, False, (wide, wide))
    sums[GAIN : GAIN + 1, :] = jnp.sum(sgain, 0, keepdims=True)
    sums[BIAS : BIAS + 1, :] = jnp.sum(sbias, 0, keepdims=True)


def split_rows(dim, load, xh, xl):
    def one(j, rows, _):
        xh[rows, :], xl[rows, :] = split(load(rows))
        return 0

    each_step(dim, one, 4)


class Share:
    def __init__(self, dim, nm, extra=0):
        self.nm = nm
        self.q = -(-nm * dim.Hd // (8 * dim.S)) * 8
        self.extra = extra
        self.rows = self.q + extra
        self.step = math.gcd(self.q, dim.Hd)
        self.shape = (dim.S // 2, dim.D, self.rows, dim.H)


def weight_grad(dim, share, m, ah, al, bh, bl, tile, keep, send):
    me = lax.axis_index("seq")
    my = lax.axis_index("dp")
    for h0 in range(0, dim.H, WIDE):
        tile[...] = dot3(ah[:, h0 : h0 + WIDE], al[:, h0 : h0 + WIDE], bh[...], bl[...], ((0,), (0,)))

        def put(odd):
            for r0 in range(0, WIDE, share.step):
                h = h0 + r0
                d, p = h // dim.Hd, m * dim.Hd + h % dim.Hd
                s, off = p // share.q, p % share.q
                dst = keep if (s & 1) == odd else send
                dst[(s ^ me) >> 1, d ^ my, off : off + share.step, :] = tile[r0 : r0 + share.step, :]

        for odd in range(2):
            pl.when(me & 1 == odd)(functools.partial(put, odd))


def call(fn, outs, scratch, *args, flops=0, anywhere=0):
    nbytes = sum(4 * math.prod(x.shape) for x in (*args, *outs))
    spaces = [pl.ANY] * anywhere + [pltpu.VMEM] * (len(args) - anywhere)
    return pl.pallas_call(
        fn,
        out_shape=[jax.ShapeDtypeStruct(s.shape, F32) for s in outs],
        in_specs=[pl.BlockSpec(memory_space=space) for space in spaces],
        out_specs=[pl.BlockSpec(memory_space=pltpu.VMEM)] * len(outs),
        scratch_shapes=scratch,
        compiler_params=pltpu.CompilerParams(vmem_limit_bytes=56 * 1024 * 1024),
        cost_estimate=pl.CostEstimate(flops=flops, bytes_accessed=nbytes, transcendentals=0),
    )(*args)


def f32(*shape):
    return jax.ShapeDtypeStruct(shape, F32)


def halves(dim, n):
    return [pltpu.VMEM((dim.T, dim.H), BF16)] * (2 * n) + [pltpu.VMEM((dim.H, dim.H), BF16)] * 2


def prep_kernel(dim, small, table):
    for layer in range(dim.layers):
        s = small[layer]
        nu, theta, gam = s[5:6, : dim.N], s[5:6, dim.N :], s[6:7, : dim.N]
        rate, angle = jnp.exp(nu), jnp.exp(theta)
        mod = jnp.exp(-rate)
        re, im = mod * jnp.cos(angle), mod * jnp.sin(angle)
        gamma = jnp.exp(gam)

        def put(index, a, b):
            table[layer, index : index + 1, : dim.N] = a
            table[layer, index : index + 1, dim.N :] = b

        table[layer] = jnp.zeros((TABLE, dim.H), F32)
        table[layer, :5, :] = s[:5]
        put(GAMMA, gamma, gamma)
        put(LAM, re, im)
        put(RATES, rate, angle)
        power = 1
        while power < dim.L:
            re, im = cmul(re, im, re, im)
            power *= 2
        for index in (LAM1, LAM2, LAM4, LAM8):
            put(index, re, im)
            re, im = cmul(re, im, re, im)


class Weight:
    def __init__(self, dim, layer, m, sources, own, buf, sem):
        self.dim, self.layer, self.m = dim, layer, m
        self.sources, self.own, self.buf, self.sem = sources, own, buf, sem
        self.here = False

    def moves(self):
        in_map, out_map, glu = self.sources[:3]
        lo = max(self.m - 2, 0) * self.dim.H
        shard = (in_map, out_map, glu, glu)[self.m].at[self.layer, :, pl.ds(lo, self.dim.H)]
        yield pltpu.make_async_copy(shard, self.own, self.sem.at[self.dim.S])
        for k, piece in enumerate(self.sources[3:]):
            yield pltpu.make_async_copy(piece.at[self.m], self.buf.at[k], self.sem.at[k])

    def start(self):
        for move in self.moves():
            move.start()

    def fill(self, wh, wl):
        dim, q = self.dim, self.dim.q
        if not self.here:
            for move in self.moves():
                move.wait()
        self.here = True
        me, my = lax.axis_index("seq"), lax.axis_index("dp")

        def put(start, n, value):
            rows = pl.ds(pl.multiple_of(start, 16), n)
            wh[rows, :], wl[rows, :] = split(value)

        def mine(i, _):
            put(my * dim.Hd + i * 32, 32, self.own[pl.ds(pl.multiple_of(i * 32, 32), 32), :])
            return 0

        lax.fori_loop(0, dim.Hd // 32, mine, 0)

        def one(k, _):
            s = k ^ me

            def block():
                for kz in range(1, dim.D):
                    put((kz ^ my) * dim.Hd + s * q, q, self.buf[k, kz - 1])

            if dim.used < dim.S:
                pl.when(s < dim.used)(block)
            else:
                block()
            return 0

        lax.fori_loop(0, dim.S, one, 0)


def weights_in(dim, names, fn):
    layers = sorted({layer for layer, _ in names})
    first = 3 + len(layers) * dim.S

    def kernel(*refs):
        sources = {layer: refs[:3] + refs[3 + i * dim.S : 3 + (i + 1) * dim.S] for i, layer in enumerate(layers)}
        spare = refs[len(refs) - 3 * len(names) :]
        weights = [
            Weight(dim, layer, m, sources[layer], *spare[3 * i : 3 * i + 3]) for i, (layer, m) in enumerate(names)
        ]
        for w in weights:
            w.start()
        fn(dim, weights, *refs[first : len(refs) - 3 * len(names)])

    scratch = [
        pltpu.VMEM((dim.Hd, dim.H), F32),
        pltpu.VMEM((dim.S, dim.D - 1, dim.q, dim.H), F32),
        pltpu.SemaphoreType.DMA((dim.S + 1,)),
    ] * len(names)
    return kernel, first, scratch


def strided(dim, ref):
    return lambda j, rows: ref[:, j, :]


def plain(ref):
    return lambda j, rows: ref[rows, :]


def k_a0(dim, weights, x, table, xhat, rstd, drive, cf, fin, ah, al, wh, wl):
    front(dim, strided(dim, x), table.at[0], weights[0], xhat, rstd, drive, cf, fin, ah, al, wh, wl)


def k_b0(dim, weights, x, table, drive, cf, g, xhat,
         en, states, mixed, active, v, s, act1, xhat1, rstd1, drive1, cf1, fin1, ah, al, wh, wl):
    t = table.at[0]
    w_out, w_gv, w_gg, w_in1 = weights
    back(dim, t, drive, cf, g, xhat, w_out, w_gv, w_gg, en, states, mixed, active, v, s, ah, al, wh, wl)
    load = strided(dim, x)

    def residual(j, rows):
        act = load(j, rows) + gate(dim, t, v, s, rows)
        act1[rows, :] = act
        return act

    front(dim, residual, table.at[1], w_in1, xhat1, rstd1, drive1, cf1, fin1, ah, al, wh, wl)


def k_b1(dim, weights, act1, out_grad, table, drive, cf, g, xhat,
         out, en, states, active, dv, dg, dmixed, ds, rcf, rfin, sums, ah, al, bh, bl, wh, wl, mixed, v, s):
    t = table.at[1]
    w_out, w_gv, w_gg = weights
    back(dim, t, drive, cf, g, xhat, w_out, w_gv, w_gg, en, states, mixed, active, v, s, ah, al, wh, wl)

    def residual(j, rows, _):
        out[:, j, :] = act1[rows, :] + gate(dim, t, v, s, rows)
        return 0

    each_step(dim, residual, 2)
    sums[...] = jnp.zeros((SMALL, dim.H), F32)
    top(dim, t, strided(dim, out_grad), v, s, mixed, xhat, w_gv, w_gg, w_out, dv, dg, dmixed, ds, rcf, rfin, sums,
        ah, al, bh, bl, wh, wl)


def k_w1(dim, share, active, dv, dg, states, dmixed, keep, send, ah, al, bh, bl, tile):
    split_rows(dim, lambda rows: active[rows, :], ah, al)
    for m, ref in ((0, dv), (1, dg)):
        split_rows(dim, lambda rows: ref[rows, :], bh, bl)
        weight_grad(dim, share, m, ah, al, bh, bl, tile, keep, send)
    split_rows(dim, lambda rows: states[rows, :], ah, al)
    split_rows(dim, lambda rows: dmixed[rows, :], bh, bl)
    weight_grad(dim, share, 2, ah, al, bh, bl, tile, keep, send)


def k_c1(dim, weights, out_grad, table, ds, rcf, gr, states, en, drive, xhat, rstd, dmixed,
         xhat0, mixed0, v0, s0,
         dproj, dmid, dv0, dg0, dmixed0, ds0, rcf0, rfin0, sums1, sums0, ah, al, bh, bl, wh, wl, adj_en):
    w_in, w_gv, w_gg, w_out = weights

    def store(j, rows, value):
        dmid[rows, :] = value

    bottom(dim, table.at[1], ds, rcf, gr, states, en, drive, xhat, rstd, dmixed, w_in, strided(dim, out_grad), store,
           dproj, ds0, adj_en, sums1, ah, al, wh, wl)
    sums0[...] = jnp.zeros((SMALL, dim.H), F32)
    top(dim, table.at[0], plain(dmid), v0, s0, mixed0, xhat0, w_gv, w_gg, w_out, dv0, dg0, dmixed0, ds0, rcf0, rfin0,
        sums0, ah, al, bh, bl, wh, wl)


def k_w2(dim, share, active, dv, dg, states, dmixed, xhat1, dproj1, table, keep, send, ah, al, bh, bl, tile):
    k_w1(dim, share, active, dv, dg, states, dmixed, keep, send, ah, al, bh, bl, tile)
    t = table.at[1]
    split_rows(dim, lambda rows: xhat1[rows, :] * row(t, GAIN) + row(t, BIAS), ah, al)
    split_rows(dim, lambda rows: dproj1[rows, :], bh, bl)
    weight_grad(dim, share, 3, ah, al, bh, bl, tile, keep, send)


def k_c0(share, dim, weights, table, ds, rcf, gr, states, en, drive, xhat, rstd, dmixed, dmid, sums1a, sums1b, sums0a,
         input_grad, keep, send, ah, al, bh, bl, wh, wl, adj_en, dproj, buf, sums0, tile):
    t = table.at[0]

    def store(j, rows, value):
        input_grad[:, j, :] = value

    bottom(dim, t, ds, rcf, gr, states, en, drive, xhat, rstd, dmixed, weights[0], plain(dmid), store, dproj, buf, adj_en,
           sums0, ah, al, wh, wl)
    split_rows(dim, lambda rows: xhat[rows, :] * row(t, GAIN) + row(t, BIAS), bh, bl)
    weight_grad(dim, share, 0, bh, bl, ah, al, tile, keep, send)
    place = lax.broadcasted_iota(jnp.int32, (SMALL, dim.H), 0)
    upper = (place >= SKIP) & (place <= BIAS_G)
    tile[0:SMALL, :] = jnp.where(upper, sums0a[...], sums0[...])
    tile[SMALL : 2 * SMALL, :] = jnp.where(upper, sums1a[...], sums1b[...])
    me = lax.axis_index("seq")
    n = -(-2 * SMALL // dim.S)

    def put(odd):
        for s in range(dim.S):
            dst = keep if (s & 1) == odd else send
            lo = min(s * n, 2 * SMALL - n)
            for d in range(dim.D):
                dst[(s ^ me) >> 1, d, share.q : share.q + n, :] = tile[lo : lo + n, :]

    for odd in range(2):
        pl.when(me & 1 == odd)(functools.partial(put, odd))


def swap(x, axis, mask):
    count = lax.axis_size(axis)
    return lax.ppermute(x, axis, [(i, i ^ mask) for i in range(count)])


def plane_gather(dim, x):
    pieces = [None] * dim.S
    pieces[0] = x
    for k in range(2, dim.S, 2):
        pieces[k] = swap(x, "seq", k)
    for k in range(0, dim.S, 2):
        pieces[k + 1] = swap(pieces[k], "seq", 1)
    return pieces


def reduce_share(dim, keep, send):
    got = swap(send, "seq", 1)
    half = [keep[k] + got[k] for k in range(dim.S // 2)]
    total = half[0]
    for k in range(1, dim.S // 2):
        total = total + swap(half[k], "seq", 2 * k)
    out = total[0]
    for k in range(1, dim.D):
        out = out + swap(total[k], "dp", k)
    return out


def unpack_kernel(dim, shares, *refs):
    count = len(shares) * dim.S
    pieces, (g_in, g_out, g_glu, vectors) = refs[:count], refs[count:]
    me = lax.axis_index("seq")
    n = -(-2 * SMALL // dim.S)

    def place(layer, kind, rows, value):
        if kind == "in":
            g_in[layer, rows, :] = value
        elif kind == "out":
            g_out[layer, rows, :] = value
        elif kind == "gv":
            g_glu[layer, rows, 0 : dim.H] = value
        else:
            g_glu[layer, rows, dim.H : 2 * dim.H] = value

    for i, (share, kinds) in enumerate(shares):
        for k in range(dim.S):
            src = pieces[i * dim.S + k]
            s = k ^ me

            def one(known):
                for off in range(0, share.q, share.step):
                    p = known * share.q + off
                    m = p // dim.Hd
                    if m < share.nm:
                        layer, kind = kinds[m]
                        r = p % dim.Hd
                        place(layer, kind, slice(r, r + share.step), src[off : off + share.step, :])
                if share.extra:
                    lo = min(known * n, 2 * SMALL - n)
                    vectors[lo : lo + n, :] = src[share.q : share.q + n, :]

            for known in range(dim.S):
                pl.when(s == known)(functools.partial(one, known))


def unpack(dim, shares, pieces):
    args = [p for group in pieces for p in group]
    outs = [f32(dim.layers, dim.Hd, dim.H), f32(dim.layers, dim.Hd, dim.H), f32(dim.layers, dim.Hd, 2 * dim.H),
            f32(2 * SMALL, dim.H)]
    return call(functools.partial(unpack_kernel, dim, shares), outs, [], *args)


def spread(vec, width, my):
    count = width // vec.shape[1]
    lane = lax.broadcasted_iota(jnp.int32, (vec.shape[0], width), 1)
    return jnp.where(lane // vec.shape[1] == my, jnp.tile(vec, (1, count)), 0.0)


def body(inputs, out_grad, ln_gain, ln_bias, nu_log, theta_log, gamma_log, in_map, out_map, skip_gain, glu_weight, glu_bias):
    dim = Dims(inputs, in_map, lax.axis_size("dp"), lax.axis_size("seq"))
    T, H, N, R, B, D, S = dim.T, dim.H, dim.N, dim.R, dim.B, dim.D, dim.S
    me, my = lax.axis_index("seq"), lax.axis_index("dp")
    x = inputs.reshape(R, dim.L, H)
    og = out_grad.reshape(R, dim.L, H)

    both = spread(glu_bias, 2 * H, my)
    small = jnp.stack(
        [
            spread(ln_gain, H, my),
            spread(ln_bias, H, my),
            spread(skip_gain, H, my),
            both[:, :H],
            both[:, H:],
            jnp.concatenate([spread(nu_log, N, my), spread(theta_log, N, my)], 1),
            spread(gamma_log, H, my),
            jnp.zeros_like(ln_gain, shape=(dim.layers, H)),
        ],
        1,
    )
    pieces = []
    table = None
    start = jnp.minimum(me, dim.used - 1) * dim.q
    for layer in range(dim.layers):

        def cut(w, lo):
            return lax.dynamic_slice(w, (layer, start, lo), (1, dim.q, H))[0]

        mine = jnp.concatenate([cut(in_map, 0), cut(out_map, 0), cut(glu_weight, 0), cut(glu_weight, H)], 0)
        if layer == 0:
            mine = jnp.concatenate([small.reshape(-1, H), mine], 0)
        others = [swap(mine, "dp", k) for k in range(1, D)]
        if layer == 0:
            first = dim.layers * SMALL
            total = mine[:first]
            for other in others:
                total = total + other[:first]
            table = call(
                functools.partial(prep_kernel, dim), [f32(dim.layers, TABLE, H)], [], total.reshape(small.shape)
            )[0]
            others = [other[first:] for other in others]
        joined = jnp.stack([other.reshape(4, dim.q, H) for other in others], 1)
        pieces.append(plane_gather(dim, joined))

    unit = 2 * T * H * H
    big, ent, fins = f32(T, H), f32(R, H), f32(B, H)
    stat = f32(T, 128)
    vec = f32(SMALL, H)

    def k(fn, names, outs, scratch, *args, n):
        kernel, count, own = weights_in(dim, names, fn)
        layers = sorted({layer for layer, _ in names})
        sources = [in_map, out_map, glu_weight] + [p for layer in layers for p in pieces[layer]]
        return call(kernel, outs, scratch + own, *sources, *args, flops=3 * n * unit, anywhere=count)

    def carried(fin):
        return lax.all_gather(fin, "seq")

    xhat0, rstd0, drive0, cf0, fin0 = k(
        k_a0, [(0, 0)], [big, stat, big, ent, fins], halves(dim, 1), x, table, n=1
    )
    g0 = carried(fin0)
    en0, states0, mixed0, active0, v0, s0, act1, xhat1, rstd1, drive1, cf1, fin1 = k(
        k_b0,
        [(0, 1), (0, 2), (0, 3), (1, 0)],
        [ent, big, big, big, big, big, big, big, stat, big, ent, fins],
        halves(dim, 1),
        x, table, drive0, cf0, g0, xhat0,
        n=4,
    )
    g1 = carried(fin1)
    spare = [pltpu.VMEM((T, H), F32)]
    out, en1, states1, active1, dv1, dg1, dmixed1, ds1, rcf1, rfin1, sums1a = k(
        k_b1,
        [(1, 1), (1, 2), (1, 3)],
        [f32(R, dim.L, H), ent, big, big, big, big, big, big, ent, fins, vec],
        halves(dim, 2) + spare * 3,
        act1, og, table, drive1, cf1, g1, xhat1,
        n=6,
    )
    gr1 = carried(rfin1)
    share1, share2, share3 = Share(dim, 3), Share(dim, 4), Share(dim, 1, 8)
    tile = [pltpu.VMEM((WIDE, H), F32)]
    pair = [pltpu.VMEM((T, H), BF16)] * 4
    keep1, send1 = call(
        functools.partial(k_w1, dim, share1), [f32(*share1.shape)] * 2, pair + tile,
        active1, dv1, dg1, states1, dmixed1, flops=9 * unit,
    )
    dproj1, dmid, dv0, dg0, dmixed0, ds0, rcf0, rfin0, sums1b, sums0a = k(
        k_c1,
        [(1, 0), (0, 2), (0, 3), (0, 1)],
        [big, big, big, big, big, big, ent, fins, vec, vec],
        halves(dim, 2) + [pltpu.VMEM((R, H), F32)],
        og, table, ds1, rcf1, gr1, states1, en1, drive1, xhat1, rstd1, dmixed1,
        xhat0, mixed0, v0, s0,
        n=4,
    )
    gr0 = carried(rfin0)
    keep2, send2 = call(
        functools.partial(k_w2, dim, share2), [f32(*share2.shape)] * 2, pair + tile,
        active0, dv0, dg0, states0, dmixed0, xhat1, dproj1, table, flops=12 * unit,
    )
    input_grad, keep3, send3 = k(
        functools.partial(k_c0, share3),
        [(0, 0)],
        [f32(R, dim.L, H)] + [f32(*share3.shape)] * 2,
        halves(dim, 2) + [pltpu.VMEM((R, H), F32)] + spare * 2 + [pltpu.VMEM((SMALL, H), F32)] + tile,
        table, ds0, rcf0, gr0, states0, en0, drive0, xhat0, rstd0, dmixed0, dmid, sums1a, sums1b, sums0a,
        n=2,
    )
    shared = [plane_gather(dim, reduce_share(dim, a, b)) for a, b in ((keep1, send1), (keep2, send2), (keep3, send3))]
    kinds1 = [(1, "gv"), (1, "gg"), (1, "out")]
    kinds2 = [(0, "gv"), (0, "gg"), (0, "out"), (1, "in")]
    kinds3 = [(0, "in")]
    g_in, g_out, g_glu, vectors = unpack(
        dim, [(share1, kinds1), (share2, kinds2), (share3, kinds3)], shared
    )
    vectors = vectors.reshape(2, SMALL, H)

    def own(index, lo, width, total):
        rows = vectors[:, index, lo : lo + width]
        part = width // D if total is None else total
        return lax.dynamic_slice_in_dim(rows, my * part, part, 1)

    glu_rows = jnp.concatenate([vectors[:, BIAS_V], vectors[:, BIAS_G]], 1)
    part = 2 * H // D
    return (
        out.reshape(inputs.shape),
        input_grad.reshape(inputs.shape),
        own(GAIN, 0, H, None),
        own(BIAS, 0, H, None),
        own(5, 0, N, None),
        own(5, N, N, None),
        own(6, 0, N, None),
        g_in,
        g_out,
        own(SKIP, 0, H, None),
        g_glu,
        lax.dynamic_slice_in_dim(glu_rows, my * part, part, 1),
    )


def solution(mesh):
    act, vec, mat = P("dp", "seq", None), P(None, "dp"), P(None, "dp", None)
    in_specs = (act, act, vec, vec, vec, vec, vec, mat, mat, vec, mat, vec)
    out_specs = (act, act, vec, vec, vec, vec, vec, mat, mat, vec, mat, vec)
    return jax.shard_map(body, mesh=mesh, in_specs=in_specs, out_specs=out_specs, check_vma=False)
```

time: 1760 us -> 307 us (0.17)
  matrix products: 863 us -> 0 us
  blocking collectives: 277 us -> 39.5 us
  waiting for transfers between devices: 279 us -> 48.6 us
  local copies, waits for them, and re-layouts: 238 us -> 17.6 us
  starting transfers between devices: 1.15 us -> 100 us
  Pallas kernels: 0 us -> 93.2 us
  other arithmetic: 71.8 us -> 4.78 us
    dot_general x100 -> x0, matrix products: 863 us -> none  [the longest x64 793 us: table_product(): jnp.einsum('tsn,bsn->btn', table, values, precision=lax.Precision.HIGHEST...]
    all_gather x29 -> x4, blocking collectives: 263 us -> 39.5 us  [carried(): return lax.all_gather(fin, 'seq')]
    unnamed x21 -> x0, waiting for transfers between devices: 134 us -> none
    ppermute x0 -> x62, starting transfers between devices: none -> 100 us  [swap(): return lax.ppermute(x, axis, [(i, i ^ mask) for i in range(count)])]
    pallas_call x0 -> x9, Pallas kernels: none -> 93.2 us  [call(): pl.pallas_call(fn, out_shape=[jax.ShapeDtypeStruct(s.shape, F32) for s in...]
    reduce_scatter x3 -> x0, waiting for transfers between devices: 92 us -> none  [the longest x1 80.7 us: body(): lax.psum_scatter(s_glu_w, 'dp', scatter_dimension=1, tiled=True)]
    slice x32 -> x6, local copies, waits for them, and re-layouts: 61.5 us -> 1.8 us  [the longest x1 0.96 us: body(): glu_rows = jnp.concatenate([vectors[:, BIAS_V], vectors[:, BIAS_G]], 1)]
    reshape x16 -> x0, local copies, waits for them, and re-layouts: 54.8 us -> none  [the longest x8 27.4 us: stretch_states(): drive_re = driven[:, :half_width].reshape(span_count, span_len, half_width)]
  transfers between devices with their start and end apart: 14 -> 62, of which waited for: 10 -> 19; matrix products, arithmetic and copies ran while one was open for 19% -> 4% of each run, Pallas kernels for 0% -> 9%
where the time goes in v1:
time: 307 us; the launch traced here: 305 us
  starting transfers between devices  100 us (33%)
  Pallas kernels  93.2 us (30%)
  waiting for transfers between devices  48.6 us (16%)
  blocking collectives  39.5 us (13%)
  local copies, waits for them, and re-layouts  17.6 us (6%)
  other arithmetic  4.78 us (2%)
    ppermute x62, starting transfers between devices, swap(): return lax.ppermute(x, axis, [(i, i ^ mask) for i in range(count)])  100 us
    pallas_call x9, Pallas kernels, call(): pl.pallas_call(fn, out_shape=[jax.ShapeDtypeStruct(s.shape, F32) for s in...  93.2 us
    ppermute x62, waiting for transfers between devices, swap(): return lax.ppermute(x, axis, [(i, i ^ mask) for i in range(count)])  48.6 us
    all_gather x4, blocking collectives, carried(): return lax.all_gather(fin, 'seq')  39.5 us
  transfers between devices with their start and end apart: 62, of which 19 were waited for; matrix products, arithmetic and copies ran while one was open for 4% of the time, Pallas kernels for 9%

profile of v1, /device:TPU:9, one launch (start us, length us, event | category | flops | bytes accessed | tf_op | source)
XLA Modules:
  0.0 305.2 jit_solution(7424110717551388830)
XLA Ops:
  18.8 6.7 %collective-permute-done.11 = f32[80,512]{1,0:T(8,128)S(1)} collective-permute-done((f32[80,512]{1,0:T(8,128)S(1)}, f32[80,512]{1,0:T(8,128)S(1)}, u32[]{:S(2)}, u32[]{:S(2)}) %collective-permute-start.11) | collective-permute-done | bytes 163872 | tf_op jit(solution)/shard_map/ppermute | solution.py:578
  25.5 4.4 %collective-permute-done.12 = f32[80,512]{1,0:T(8,128)S(1)} collective-permute-done((f32[80,512]{1,0:T(8,128)S(1)}, f32[80,512]{1,0:T(8,128)S(1)}, u32[]{:S(2)}, u32[]{:S(2)}) %collective-permute-start.12) | collective-permute-done | bytes 163872 | tf_op jit(solution)/shard_map/ppermute | solution.py:578
  38.6 5.5 %collective-permute-start.15 = (f32[4,3,16,512]{3,2,1,0:T(8,128)S(1)}, f32[4,3,16,512]{3,2,1,0:T(8,128)S(1)}, u32[]{:S(2)}, u32[]{:S(2)}) collective-permute-start(f32[4,3,16,512]{3,2,1,0:T(8,128)S(1)} %collective-permute-done.14.refs_5_), channel_id=1, source_target_pairs={{0,1},{1,0},{2,3},{3,2},{4,5},{5,4},{6,7},{7,6},{8,9},{9,8},{10,11... | collective-permute-start | bytes 1179656 | tf_op jit(solution)/shard_map/ppermute | solution.py:578
  44.2 15.5 %collective-permute-start.17 = (f32[4,3,16,512]{3,2,1,0:T(8,128)S(1)}, f32[4,3,16,512]{3,2,1,0:T(8,128)S(1)}, u32[]{:S(2)}, u32[]{:S(2)}) collective-permute-start(f32[4,3,16,512]{3,2,1,0:T(8,128)S(1)} %collective-permute-done.16.refs_7_), channel_id=1, source_target_pairs={{0,1},{1,0},{2,3},{3,2},{4,5},{5,4},{6,7},{7,6},{8,9},{9,8},{10,11... | collective-permute-start | bytes 1179656 | tf_op jit(solution)/shard_map/ppermute | solution.py:578
  64.3 5.9 %shard_map.212 = (f32[512,512]{1,0:T(8,128)}, f32[512,128]{1,0:T(8,128)}, f32[512,512]{1,0:T(8,128)}, f32[16,512]{1,0:T(8,128)}, f32[2,512]{1,0:T(2,128)}) custom-call(f32[2,128,512]{2,1,0:T(8,128)} %refs_0_.9, f32[2,128,512]{2,1,0:T(8,128)} %refs_1_.9, f32[2,128,1024]{2,1,0:T(8,128)} %refs_2_.9, f32[4,3,16,512]{3,2,1,0:T(8,128)} %copy-done.1, ...), custom_call_target="tpu_custom_call" | custom-call | flops 805306368 | bytes 8753152 | tf_op jit(solution)/shard_map/pallas_call | solution.py:351
  70.2 10.0 %all-gather.4.refs_23_ = f32[8,2,512]{2,1,0:T(2,128)} all-gather(f32[1,2,512]{2,1,0:T(2,128)} %bitcast.167), channel_id=2, replica_groups=mesh['dp'=4,'seq'=8] {'seq'}, dimensions={0}, use_global_device_ids=true | all-gather | bytes 36864 | tf_op jit(solution)/shard_map/all_gather | solution.py:710
  81.4 15.4 %shard_map.213 = (f32[16,512]{1,0:T(8,128)}, f32[512,512]{1,0:T(8,128)}, f32[512,512]{1,0:T(8,128)}, f32[512,512]{1,0:T(8,128)}, f32[512,512]{1,0:T(8,128)}, /*i...) custom-call(f32[2,128,512]{2,1,0:T(8,128)} %refs_0_.9, ...), custom_call_target="tpu_custom_call" | custom-call | flops 3221225472 | bytes 20385792 | tf_op jit(solution)/shard_map/pallas_call | solution.py:351
  96.7 9.8 %all-gather.5.refs_16_ = f32[8,2,512]{2,1,0:T(2,128)} all-gather(f32[1,2,512]{2,1,0:T(2,128)} %bitcast.165), channel_id=3, replica_groups=mesh['dp'=4,'seq'=8] {'seq'}, dimensions={0}, use_global_device_ids=true | all-gather | bytes 36864 | tf_op jit(solution)/shard_map/all_gather | solution.py:710
  106.5 17.7 %shard_map.214 = (f32[16,32,512]{2,1,0:T(8,128)}, f32[16,512]{1,0:T(8,128)}, f32[512,512]{1,0:T(8,128)}, f32[512,512]{1,0:T(8,128)}, f32[512,512]{1,0:T(8,128)},...) custom-call(f32[2,128,512]{2,1,0:T(8,128)} %refs_0_.9, ...), custom_call_target="tpu_custom_call" | custom-call | flops 4831838208 | bytes 16994304 | tf_op jit(solution)/shard_map/pallas_call | solution.py:351
  124.2 10.0 %all-gather.6.refs_23_ = f32[8,2,512]{2,1,0:T(2,128)} all-gather(f32[1,2,512]{2,1,0:T(2,128)} %bitcast.166), channel_id=4, replica_groups=mesh['dp'=4,'seq'=8] {'seq'}, dimensions={0}, use_global_device_ids=true | all-gather | bytes 36864 | tf_op jit(solution)/shard_map/all_gather | solution.py:710
  134.2 17.7 %shard_map.215 = (f32[512,512]{1,0:T(8,128)}, f32[512,512]{1,0:T(8,128)}, f32[512,512]{1,0:T(8,128)}, f32[512,512]{1,0:T(8,128)}, f32[512,512]{1,0:T(8,128)}, /*...) custom-call(f32[2,128,512]{2,1,0:T(8,128)} %refs_0_.9, ...), custom_call_target="tpu_custom_call" | custom-call | flops 3221225472 | bytes 25661440 | tf_op jit(solution)/shard_map/pallas_call | solution.py:351
  151.9 9.7 %all-gather.7.refs_14_ = f32[8,2,512]{2,1,0:T(2,128)} all-gather(f32[1,2,512]{2,1,0:T(2,128)} %bitcast.164), channel_id=5, replica_groups=mesh['dp'=4,'seq'=8] {'seq'}, dimensions={0}, use_global_device_ids=true | all-gather | bytes 36864 | tf_op jit(solution)/shard_map/all_gather | solution.py:710
  161.6 11.5 %shard_map.218 = (f32[4,4,64,512]{3,2,1,0:T(8,128)}, f32[4,4,64,512]{3,2,1,0:T(8,128)}) custom-call(f32[512,512]{1,0:T(8,128)} %get-tuple-element.98.active, f32[512,512]{1,0:T(8,128)} %get-tuple-element.99.dv, f32[512,512]{1,0:T(8,128)} %get-tuple-element.100.dg, f32[512,512]{1,0:T(8,128)} %get-tuple-element.84.refs_15_.states, ...), custom_call_target="tpu_custom_call" | custom-call | flops 3221225472 | bytes 11599872 | tf_op jit(solution)/shard_map/pallas_call | solution.py:351
  173.3 8.9 %shard_map.217 = (f32[4,4,48,512]{3,2,1,0:T(8,128)}, f32[4,4,48,512]{3,2,1,0:T(8,128)}) custom-call(f32[512,512]{1,0:T(8,128)} %get-tuple-element.93.active, f32[512,512]{1,0:T(8,128)} %get-tuple-element.94.dv, f32[512,512]{1,0:T(8,128)} %get-tuple-element.95.dg, f32[512,512]{1,0:T(8,128)} %get-tuple-element.74.refs_24_.states, ...), custom_call_target="tpu_custom_call" | custom-call | flops 2415919104 | bytes 8388608 | tf_op jit(solution)/shard_map/pallas_call | solution.py:351
  182.4 10.9 %shard_map.216 = (f32[16,32,512]{2,1,0:T(8,128)}, f32[4,4,24,512]{3,2,1,0:T(8,128)}, f32[4,4,24,512]{3,2,1,0:T(8,128)}) custom-call(f32[2,128,512]{2,1,0:T(8,128)} %refs_0_.9, f32[2,128,512]{2,1,0:T(8,128)} %refs_1_.9, f32[2,128,1024]{2,1,0:T(8,128)} %refs_2_.9, f32[4,3,16,512]{3,2,1,0:T(8,128)} %copy-done.1, f32[4,3,16,512]{3,2,1,0:T(8,128)} %copy-done.5, ...), custom_call_target="tpu_custom_call" | custom-call | flops 1610612736 | bytes 14630912 | tf_op jit(solution)/shard_map/pallas_call | solution.py:351
  199.8 3.7 %collective-permute-done.49 = f32[4,24,512]{2,1,0:T(8,128)S(1)} collective-permute-done((f32[4,24,512]{2,1,0:T(8,128)S(1)}, f32[4,24,512]{2,1,0:T(8,128)S(1)}, u32[]{:S(2)}, u32[]{:S(2)}) %collective-permute-start.49) | collective-permute-done | bytes 196640 | tf_op jit(solution)/shard_map/ppermute | solution.py:578
  203.8 4.7 %collective-permute-done.51 = f32[4,24,512]{2,1,0:T(8,128)S(1)} collective-permute-done((f32[4,24,512]{2,1,0:T(8,128)S(1)}, f32[4,24,512]{2,1,0:T(8,128)S(1)}, u32[]{:S(2)}, u32[]{:S(2)}) %collective-permute-start.51) | collective-permute-done | bytes 196640 | tf_op jit(solution)/shard_map/ppermute | solution.py:578
  219.6 3.4 %collective-permute-done.22 = f32[4,48,512]{2,1,0:T(8,128)S(1)} collective-permute-done((f32[4,48,512]{2,1,0:T(8,128)S(1)}, f32[4,48,512]{2,1,0:T(8,128)S(1)}, u32[]{:S(2)}, u32[]{:S(2)}) %collective-permute-start.22) | collective-permute-done | bytes 393248 | tf_op jit(solution)/shard_map/ppermute | solution.py:578
  223.0 6.7 %collective-permute-start.56 = (f32[24,512]{1,0:T(8,128)S(1)}, f32[24,512]{1,0:T(8,128)S(1)}, u32[]{:S(2)}, u32[]{:S(2)}) collective-permute-start(f32[24,512]{1,0:T(8,128)S(1)} %fusion.29.refs_16_), channel_id=1, source_target_pairs={{0,2},{1,3},{2,0},{3,1},{4,6},{5,7},{6,4},{7,5},{8,10},{9,11},{10,... | collective-permute-start | bytes 147464 | tf_op jit(solution)/shard_map/ppermute | solution.py:578
  230.0 9.2 %collective-permute-done.35 = f32[4,64,512]{2,1,0:T(8,128)S(1)} collective-permute-done((f32[4,64,512]{2,1,0:T(8,128)S(1)}, f32[4,64,512]{2,1,0:T(8,128)S(1)}, u32[]{:S(2)}, u32[]{:S(2)}) %collective-permute-start.35) | collective-permute-done | bytes 524320 | tf_op jit(solution)/shard_map/ppermute | solution.py:578
  239.3 3.4 %collective-permute-done.36 = f32[4,64,512]{2,1,0:T(8,128)S(1)} collective-permute-done((f32[4,64,512]{2,1,0:T(8,128)S(1)}, f32[4,64,512]{2,1,0:T(8,128)S(1)}, u32[]{:S(2)}, u32[]{:S(2)}) %collective-permute-start.36) | collective-permute-done | bytes 524320 | tf_op jit(solution)/shard_map/ppermute | solution.py:578
  242.7 14.7 %collective-permute-start.55 = (f32[24,512]{1,0:T(8,128)S(1)}, f32[24,512]{1,0:T(8,128)S(1)}, u32[]{:S(2)}, u32[]{:S(2)}) collective-permute-start(f32[24,512]{1,0:T(8,128)S(1)} %fusion.29.refs_16_), channel_id=1, source_target_pairs={{0,1},{1,0},{2,3},{3,2},{4,5},{5,4},{6,7},{7,6},{8,9},{9,8},{10,11... | collective-permute-start | bytes 147464 | tf_op jit(solution)/shard_map/ppermute | solution.py:578
  272.6 5.7 %collective-permute-start.61 = (f32[24,512]{1,0:T(8,128)S(1)}, f32[24,512]{1,0:T(8,128)S(1)}, u32[]{:S(2)}, u32[]{:S(2)}) collective-permute-start(f32[24,512]{1,0:T(8,128)S(1)} %collective-permute-done.60.refs_22_), channel_id=1, source_target_pairs={{0,1},{1,0},{2,3},{3,2},{4,5},{5,4},{6,7},{7,6},{8,9},{9,8},{10,11... | collective-permute-start | bytes 147464 | tf_op jit(solution)/shard_map/ppermute | solution.py:578
  295.4 3.8 %shard_map.219 = (f32[2,128,512]{2,1,0:T(8,128)}, f32[2,128,512]{2,1,0:T(8,128)}, f32[2,128,1024]{2,1,0:T(8,128)}, f32[16,512]{1,0:T(8,128)}) custom-call(f32[48,512]{1,0:T(8,128)} %copy-done.13, f32[48,512]{1,0:T(8,128)} %copy-done.32, f32[48,512]{1,0:T(8,128)} %copy-done.29, f32[48,512]{1,0:T(8,128)} %copy-done.33, f32[48,512]{1,0:T(8,128)} %copy-done.30, ...), custom_call_target="tpu_custom_call" | custom-call | bytes 4358144 | tf_op jit(solution)/shard_map/pallas_call | solution.py:351
  (265 shorter events, 88.8 us)
Async XLA Ops:
  15.9 14.0 %collective-permute-start.12 = (f32[80,512]{1,0:T(8,128)S(1)}, f32[80,512]{1,0:T(8,128)S(1)}, u32[]{:S(2)}, u32[]{:S(2)}) collective-permute-start(f32[80,512]{1,0:T(8,128)S(1)} %bitcast_dynamic-update-slice_fusion), channel_id=1, source_target_pairs={{0,24},{8,16},{16,8},{24,0},{1,25},{9,17},{17,9},{25,1},{2,26},{10... | collective-permute-start | bytes 491528 | tf_op jit(solution)/shard_map/ppermute | solution.py:578
  16.2 16.5 %collective-permute-start.4 = (f32[4,3,16,512]{3,2,1,0:T(8,128)S(1)}, f32[4,3,16,512]{3,2,1,0:T(8,128)S(1)}, u32[]{:S(2)}, u32[]{:S(2)}) collective-permute-start(f32[4,3,16,512]{3,2,1,0:T(8,128)S(1)} %pad_maximum_fusion.refs_11_.refs_3_), channel_id=1, source_target_pairs={{0,2},{1,3},{2,0},{3,1},{4,6},{5,7},{6,4},{7,5},{8,10},{9,11},{10,... | collective-permute-start | bytes 1179656 | tf_op jit(solution)/shard_map/ppermute | solution.py:578
  17.5 17.4 %collective-permute-start.6 = (f32[4,3,16,512]{3,2,1,0:T(8,128)S(1)}, f32[4,3,16,512]{3,2,1,0:T(8,128)S(1)}, u32[]{:S(2)}, u32[]{:S(2)}) collective-permute-start(f32[4,3,16,512]{3,2,1,0:T(8,128)S(1)} %pad_maximum_fusion.refs_11_.refs_3_), channel_id=1, source_target_pairs={{0,4},{1,5},{2,6},{3,7},{4,0},{5,1},{6,2},{7,3},{8,12},{9,13},{10,... | collective-permute-start | bytes 1179656 | tf_op jit(solution)/shard_map/ppermute | solution.py:578
  32.5 27.1 %collective-permute-start.18 = (f32[4,3,16,512]{3,2,1,0:T(8,128)S(1)}, f32[4,3,16,512]{3,2,1,0:T(8,128)S(1)}, u32[]{:S(2)}, u32[]{:S(2)}) collective-permute-start(f32[4,3,16,512]{3,2,1,0:T(8,128)S(1)} %pad_maximum_fusion.1.refs_3_), channel_id=1, source_target_pairs={{0,6},{1,7},{2,4},{3,5},{4,2},{5,3},{6,0},{7,1},{8,14},{9,15},{10,... | collective-permute-start | bytes 1179656 | tf_op jit(solution)/shard_map/ppermute | solution.py:578
  32.7 27.0 %collective-permute-start.8 = (f32[4,3,16,512]{3,2,1,0:T(8,128)S(1)}, f32[4,3,16,512]{3,2,1,0:T(8,128)S(1)}, u32[]{:S(2)}, u32[]{:S(2)}) collective-permute-start(f32[4,3,16,512]{3,2,1,0:T(8,128)S(1)} %pad_maximum_fusion.refs_11_.refs_3_), channel_id=1, source_target_pairs={{0,6},{1,7},{2,4},{3,5},{4,2},{5,3},{6,0},{7,1},{8,14},{9,15},{10,... | collective-permute-start | bytes 1179656 | tf_op jit(solution)/shard_map/ppermute | solution.py:578
  34.9 25.3 %collective-permute-start.13 = (f32[4,3,16,512]{3,2,1,0:T(8,128)S(1)}, f32[4,3,16,512]{3,2,1,0:T(8,128)S(1)}, u32[]{:S(2)}, u32[]{:S(2)}) collective-permute-start(f32[4,3,16,512]{3,2,1,0:T(8,128)S(1)} %pad_maximum_fusion.1.refs_3_), channel_id=1, source_target_pairs={{0,1},{1,0},{2,3},{3,2},{4,5},{5,4},{6,7},{7,6},{8,9},{9,8},{10,11... | collective-permute-start | bytes 1179656 | tf_op jit(solution)/shard_map/ppermute | solution.py:578
  38.6 21.7 %collective-permute-start.15 = (f32[4,3,16,512]{3,2,1,0:T(8,128)S(1)}, f32[4,3,16,512]{3,2,1,0:T(8,128)S(1)}, u32[]{:S(2)}, u32[]{:S(2)}) collective-permute-start(f32[4,3,16,512]{3,2,1,0:T(8,128)S(1)} %collective-permute-done.14.refs_5_), channel_id=1, source_target_pairs={{0,1},{1,0},{2,3},{3,2},{4,5},{5,4},{6,7},{7,6},{8,9},{9,8},{10,11... | collective-permute-start | bytes 1179656 | tf_op jit(solution)/shard_map/ppermute | solution.py:578
  44.2 16.8 %collective-permute-start.17 = (f32[4,3,16,512]{3,2,1,0:T(8,128)S(1)}, f32[4,3,16,512]{3,2,1,0:T(8,128)S(1)}, u32[]{:S(2)}, u32[]{:S(2)}) collective-permute-start(f32[4,3,16,512]{3,2,1,0:T(8,128)S(1)} %collective-permute-done.16.refs_7_), channel_id=1, source_target_pairs={{0,1},{1,0},{2,3},{3,2},{4,5},{5,4},{6,7},{7,6},{8,9},{9,8},{10,11... | collective-permute-start | bytes 1179656 | tf_op jit(solution)/shard_map/ppermute | solution.py:578
  59.7 20.5 %collective-permute-start.3 = (f32[4,3,16,512]{3,2,1,0:T(8,128)S(1)}, f32[4,3,16,512]{3,2,1,0:T(8,128)S(1)}, u32[]{:S(2)}, u32[]{:S(2)}) collective-permute-start(f32[4,3,16,512]{3,2,1,0:T(8,128)S(1)} %pad_maximum_fusion.refs_11_.refs_3_), channel_id=1, source_target_pairs={{0,1},{1,0},{2,3},{3,2},{4,5},{5,4},{6,7},{7,6},{8,9},{9,8},{10,11... | collective-permute-start | bytes 1179656 | tf_op jit(solution)/shard_map/ppermute | solution.py:578
  60.2 20.0 %collective-permute-start.5 = (f32[4,3,16,512]{3,2,1,0:T(8,128)S(1)}, f32[4,3,16,512]{3,2,1,0:T(8,128)S(1)}, u32[]{:S(2)}, u32[]{:S(2)}) collective-permute-start(f32[4,3,16,512]{3,2,1,0:T(8,128)S(1)} %collective-permute-done.4.refs_13_.refs_5_), channel_id=1, source_target_pairs={{0,1},{1,0},{2,3},{3,2},{4,5},{5,4},{6,7},{7,6},{8,9},{9,8},{10,11... | collective-permute-start | bytes 1179656 | tf_op jit(solution)/shard_map/ppermute | solution.py:578
  60.3 20.0 %collective-permute-start.7 = (f32[4,3,16,512]{3,2,1,0:T(8,128)S(1)}, f32[4,3,16,512]{3,2,1,0:T(8,128)S(1)}, u32[]{:S(2)}, u32[]{:S(2)}) collective-permute-start(f32[4,3,16,512]{3,2,1,0:T(8,128)S(1)} %collective-permute-done.6.refs_15_.refs_7_), channel_id=1, source_target_pairs={{0,1},{1,0},{2,3},{3,2},{4,5},{5,4},{6,7},{7,6},{8,9},{9,8},{10,11... | collective-permute-start | bytes 1179656 | tf_op jit(solution)/shard_map/ppermute | solution.py:578
  61.0 19.3 %collective-permute-start.9 = (f32[4,3,16,512]{3,2,1,0:T(8,128)S(1)}, f32[4,3,16,512]{3,2,1,0:T(8,128)S(1)}, u32[]{:S(2)}, u32[]{:S(2)}) collective-permute-start(f32[4,3,16,512]{3,2,1,0:T(8,128)S(1)} %collective-permute-done.8.refs_17_.refs_9_), channel_id=1, source_target_pairs={{0,1},{1,0},{2,3},{3,2},{4,5},{5,4},{6,7},{7,6},{8,9},{9,8},{10,11... | collective-permute-start | bytes 1179656 | tf_op jit(solution)/shard_map/ppermute | solution.py:578
  173.1 40.9 %collective-permute-start.34 = (f32[4,4,64,512]{3,2,1,0:T(8,128)}, f32[4,4,64,512]{3,2,1,0:T(8,128)S(1)}, u32[]{:S(2)}, u32[]{:S(2)}) collective-permute-start(f32[4,4,64,512]{3,2,1,0:T(8,128)} %get-tuple-element.103), channel_id=1, source_target_pairs={{0,1},{1,0},{2,3},{3,2},{4,5},{5,4},{6,7},{7,6},{8,9},{9,8},{10,11... | collective-permute-start | bytes 6291464 | tf_op jit(solution)/shard_map/ppermute | solution.py:578
  182.1 27.4 %collective-permute-start.20 = (f32[4,4,48,512]{3,2,1,0:T(8,128)}, f32[4,4,48,512]{3,2,1,0:T(8,128)S(1)}, u32[]{:S(2)}, u32[]{:S(2)}) collective-permute-start(f32[4,4,48,512]{3,2,1,0:T(8,128)} %get-tuple-element.97), channel_id=1, source_target_pairs={{0,1},{1,0},{2,3},{3,2},{4,5},{5,4},{6,7},{7,6},{8,9},{9,8},{10,11... | collective-permute-start | bytes 4718600 | tf_op jit(solution)/shard_map/ppermute | solution.py:578
  213.9 15.8 %collective-permute-start.23 = (f32[4,48,512]{2,1,0:T(8,128)S(1)}, f32[4,48,512]{2,1,0:T(8,128)S(1)}, u32[]{:S(2)}, u32[]{:S(2)}) collective-permute-start(f32[4,48,512]{2,1,0:T(8,128)S(1)} %get-tuple-element.114), channel_id=1, source_target_pairs={{0,6},{1,7},{2,4},{3,5},{4,2},{5,3},{6,0},{7,1},{8,14},{9,15},{10,... | collective-permute-start | bytes 1179656 | tf_op jit(solution)/shard_map/ppermute | solution.py:578
  215.9 23.3 %collective-permute-start.35 = (f32[4,64,512]{2,1,0:T(8,128)S(1)}, f32[4,64,512]{2,1,0:T(8,128)S(1)}, u32[]{:S(2)}, u32[]{:S(2)}) collective-permute-start(f32[4,64,512]{2,1,0:T(8,128)S(1)} %get-tuple-element.110), channel_id=1, source_target_pairs={{0,2},{1,3},{2,0},{3,1},{4,6},{5,7},{6,4},{7,5},{8,10},{9,11},{10,... | collective-permute-start | bytes 1572872 | tf_op jit(solution)/shard_map/ppermute | solution.py:578
  216.5 26.2 %collective-permute-start.36 = (f32[4,64,512]{2,1,0:T(8,128)S(1)}, f32[4,64,512]{2,1,0:T(8,128)S(1)}, u32[]{:S(2)}, u32[]{:S(2)}) collective-permute-start(f32[4,64,512]{2,1,0:T(8,128)S(1)} %get-tuple-element.112), channel_id=1, source_target_pairs={{0,4},{1,5},{2,6},{3,7},{4,0},{5,1},{6,2},{7,3},{8,12},{9,13},{10,... | collective-permute-start | bytes 1572872 | tf_op jit(solution)/shard_map/ppermute | solution.py:578
  219.5 37.9 %collective-permute-start.37 = (f32[4,64,512]{2,1,0:T(8,128)S(1)}, f32[4,64,512]{2,1,0:T(8,128)S(1)}, u32[]{:S(2)}, u32[]{:S(2)}) collective-permute-start(f32[4,64,512]{2,1,0:T(8,128)S(1)} %get-tuple-element.111), channel_id=1, source_target_pairs={{0,6},{1,7},{2,4},{3,5},{4,2},{5,3},{6,0},{7,1},{8,14},{9,15},{10,... | collective-permute-start | bytes 1572872 | tf_op jit(solution)/shard_map/ppermute | solution.py:578
  223.0 35.6 %collective-permute-start.56 = (f32[24,512]{1,0:T(8,128)S(1)}, f32[24,512]{1,0:T(8,128)S(1)}, u32[]{:S(2)}, u32[]{:S(2)}) collective-permute-start(f32[24,512]{1,0:T(8,128)S(1)} %fusion.29.refs_16_), channel_id=1, source_target_pairs={{0,2},{1,3},{2,0},{3,1},{4,6},{5,7},{6,4},{7,5},{8,10},{9,11},{10,... | collective-permute-start | bytes 147464 | tf_op jit(solution)/shard_map/ppermute | solution.py:578
  229.8 30.7 %collective-permute-start.58 = (f32[24,512]{1,0:T(8,128)S(1)}, f32[24,512]{1,0:T(8,128)S(1)}, u32[]{:S(2)}, u32[]{:S(2)}) collective-permute-start(f32[24,512]{1,0:T(8,128)S(1)} %fusion.29.refs_16_), channel_id=1, source_target_pairs={{0,4},{1,5},{2,6},{3,7},{4,0},{5,1},{6,2},{7,3},{8,12},{9,13},{10,... | collective-permute-start | bytes 147464 | tf_op jit(solution)/shard_map/ppermute | solution.py:578
  239.2 21.3 %collective-permute-start.60 = (f32[24,512]{1,0:T(8,128)S(1)}, f32[24,512]{1,0:T(8,128)S(1)}, u32[]{:S(2)}, u32[]{:S(2)}) collective-permute-start(f32[24,512]{1,0:T(8,128)S(1)} %fusion.29.refs_16_), channel_id=1, source_target_pairs={{0,6},{1,7},{2,4},{3,5},{4,2},{5,3},{6,0},{7,1},{8,14},{9,15},{10,... | collective-permute-start | bytes 147464 | tf_op jit(solution)/shard_map/ppermute | solution.py:578
  242.7 18.7 %collective-permute-start.55 = (f32[24,512]{1,0:T(8,128)S(1)}, f32[24,512]{1,0:T(8,128)S(1)}, u32[]{:S(2)}, u32[]{:S(2)}) collective-permute-start(f32[24,512]{1,0:T(8,128)S(1)} %fusion.29.refs_16_), channel_id=1, source_target_pairs={{0,1},{1,0},{2,3},{3,2},{4,5},{5,4},{6,7},{7,6},{8,9},{9,8},{10,11... | collective-permute-start | bytes 147464 | tf_op jit(solution)/shard_map/ppermute | solution.py:578
  261.4 16.9 %collective-permute-start.59 = (f32[24,512]{1,0:T(8,128)S(1)}, f32[24,512]{1,0:T(8,128)S(1)}, u32[]{:S(2)}, u32[]{:S(2)}) collective-permute-start(f32[24,512]{1,0:T(8,128)S(1)} %collective-permute-done.58.refs_20_), channel_id=1, source_target_pairs={{0,1},{1,0},{2,3},{3,2},{4,5},{5,4},{6,7},{7,6},{8,9},{9,8},{10,11... | collective-permute-start | bytes 147464 | tf_op jit(solution)/shard_map/ppermute | solution.py:578
  261.8 17.4 %collective-permute-start.38 = (f32[64,512]{1,0:T(8,128)S(1)}, f32[64,512]{1,0:T(8,128)S(1)}, u32[]{:S(2)}, u32[]{:S(2)}) collective-permute-start(f32[64,512]{1,0:T(8,128)S(1)} %get-tuple-element.121), channel_id=1, source_target_pairs={{0,8},{8,0},{16,24},{24,16},{1,9},{9,1},{17,25},{25,17},{2,10},{10... | collective-permute-start | bytes 393224 | tf_op jit(solution)/shard_map/ppermute | solution.py:578
  (81 other events, 886.9 us)

commit v2 on v1

--- a/solution.py
+++ b/solution.py
@@ -18,6 +18,9 @@
 GELU_C = math.sqrt(2.0 / math.pi)
 
 GAIN, BIAS, SKIP, BIAS_V, BIAS_G, GAMMA, LAM, LAM1, LAM2, LAM4, LAM8, RATES = range(12)
+
+
+CHUNKS = (((0, 0),), ((0, 1), (0, 2), (0, 3), (1, 0)), ((1, 1), (1, 2), (1, 3)))
 
 
 class Dims:
@@ -318,13 +321,27 @@
 
 
 class Share:
-    def __init__(self, dim, nm, extra=0):
-        self.nm = nm
+    def __init__(self, dim, nm):
+        self.dim, self.nm = dim, nm
         self.q = -(-nm * dim.Hd // (8 * dim.S)) * 8
-        self.extra = extra
-        self.rows = self.q + extra
         self.step = math.gcd(self.q, dim.Hd)
-        self.shape = (dim.S // 2, dim.D, self.rows, dim.H)
+        self.shape = (dim.S // 2, dim.D, self.q, dim.H)
+
+    def place(self, m, d, r, me, my):
+        p = m * self.dim.Hd + r
+        s = p // self.q
+        return s & 1, ((s ^ me) >> 1, d ^ my), p % self.q
+
+
+class Halves:
+    def __init__(self, dim):
+        self.dim = dim
+        self.q = dim.Hd // 2
+        self.step = math.gcd(self.q, WIDE)
+        self.shape = (dim.D, self.q + SMALL, dim.H)
+
+    def place(self, m, d, r, me, my):
+        return r // self.q, (d ^ my,), r % self.q
 
 
 def weight_grad(dim, share, m, ah, al, bh, bl, tile, keep, send):
@@ -333,30 +350,46 @@
     for h0 in range(0, dim.H, WIDE):
         tile[...] = dot3(ah[:, h0 : h0 + WIDE], al[:, h0 : h0 + WIDE], bh[...], bl[...], ((0,), (0,)))
 
-        def put(odd):
+        def put(mine):
             for r0 in range(0, WIDE, share.step):
                 h = h0 + r0
-                d, p = h // dim.Hd, m * dim.Hd + h % dim.Hd
-                s, off = p // share.q, p % share.q
-                dst = keep if (s & 1) == odd else send
-                dst[(s ^ me) >> 1, d ^ my, off : off + share.step, :] = tile[r0 : r0 + share.step, :]
-
-        for odd in range(2):
-            pl.when(me & 1 == odd)(functools.partial(put, odd))
-
-
-def call(fn, outs, scratch, *args, flops=0, anywhere=0):
-    nbytes = sum(4 * math.prod(x.shape) for x in (*args, *outs))
-    spaces = [pl.ANY] * anywhere + [pltpu.VMEM] * (len(args) - anywhere)
-    return pl.pallas_call(
+                odd, index, off = share.place(m, h // dim.Hd, h % dim.Hd, me, my)
+                dst = keep if odd == mine else send
+                dst[(*index, slice(off, off + share.step), slice(None))] = tile[r0 : r0 + share.step, :]
+
+        for mine in range(2):
+            pl.when(me & 1 == mine)(functools.partial(put, mine))
+
+
+class Kept:
+    def __init__(self, value):
+        self.value = value
+        self.shape = value.shape
+
+
+def call(fn, outs, scratch, *args, us=1.0, anywhere=0):
+    spaces = [pltpu.HBM] * anywhere + [pltpu.VMEM] * (len(args) - anywhere)
+
+    def placed(x, space):
+        if isinstance(x, Kept):
+            return pltpu.with_memory_space_constraint(x.value, pltpu.VMEM)
+        return pltpu.with_memory_space_constraint(x, pltpu.HBM) if space is pltpu.HBM else x
+
+    values = [placed(x, space) for x, space in zip(args, spaces)]
+    room = 10 << 20
+    for x in scratch:
+        if len(x.shape) > 1:
+            room += math.prod(x.shape) * (2 if x.dtype == BF16 else 4)
+    results = pl.pallas_call(
         fn,
-        out_shape=[jax.ShapeDtypeStruct(s.shape, F32) for s in outs],
+        out_shape=outs,
         in_specs=[pl.BlockSpec(memory_space=space) for space in spaces],
         out_specs=[pl.BlockSpec(memory_space=pltpu.VMEM)] * len(outs),
         scratch_shapes=scratch,
-        compiler_params=pltpu.CompilerParams(vmem_limit_bytes=56 * 1024 * 1024),
-        cost_estimate=pl.CostEstimate(flops=flops, bytes_accessed=nbytes, transcendentals=0),
-    )(*args)
+        compiler_params=pltpu.CompilerParams(vmem_limit_bytes=max(20 << 20, room)),
+        cost_estimate=pl.CostEstimate(flops=1, bytes_accessed=int(us * 3.6e6), transcendentals=0),
+    )(*values)
+    return [x if isinstance(o, jax.ShapeDtypeStruct) else Kept(x) for x, o in zip(results, outs)]
 
 
 def f32(*shape):
@@ -368,45 +401,85 @@
 
 
 def prep_kernel(dim, small, table):
+    s = small[...]
+    nu, theta, gam = s[5:6, : dim.N], s[5:6, dim.N :], s[6:7, : dim.N]
+    rate, angle = jnp.exp(nu), jnp.exp(theta)
+    mod = jnp.exp(-rate)
+    re, im = mod * jnp.cos(angle), mod * jnp.sin(angle)
+    gamma = jnp.exp(gam)
+
+    def put(index, a, b):
+        table[index : index + 1, : dim.N] = a
+        table[index : index + 1, dim.N :] = b
+
+    table[...] = jnp.zeros((TABLE, dim.H), F32)
+    table[:5, :] = s[:5]
+    put(GAMMA, gamma, gamma)
+    put(LAM, re, im)
+    put(RATES, rate, angle)
+    power = 1
+    while power < dim.L:
+        re, im = cmul(re, im, re, im)
+        power *= 2
+    for index in (LAM1, LAM2, LAM4, LAM8):
+        put(index, re, im)
+        re, im = cmul(re, im, re, im)
+
+
+def shard_of(sources, name, rows, H):
+    layer, m = name
+    return sources[(0, 1, 2, 2)[m]].at[layer, rows, pl.ds(H if m == 3 else 0, H)]
+
+
+def pack_kernel(dim, in_map, out_map, glu, gain, bias, skip, nu, theta, gamma, glu_bias, *refs):
+    outs, held, sem = refs[:3], refs[3:-1], refs[-1]
+    vectors = (gain, bias, skip, nu, theta, gamma, glu_bias)
+    me, my = lax.axis_index("seq"), lax.axis_index("dp")
+    start = pl.multiple_of(jnp.minimum(me, dim.used - 1) * dim.q, 16)
+    moves = []
+    for src, dst in zip(vectors, held):
+        moves.append(pltpu.make_async_copy(src, dst, sem.at[len(moves)]))
+    gain, bias, skip, nu, theta, gamma, glu_bias = held
+    for out, chunk in zip(outs, CHUNKS):
+        head = out.shape[0] - len(chunk) * dim.q
+        for i, name in enumerate(chunk):
+            src = shard_of((in_map, out_map, glu), name, pl.ds(start, dim.q), dim.H)
+            dst = out.at[head + i * dim.q : head + (i + 1) * dim.q, :]
+            moves.append(pltpu.make_async_copy(src, dst, sem.at[len(moves)]))
+    for move in moves:
+        move.start()
+    for move in moves[: len(held)]:
+        move.wait()
+
+    def spread(ref, layer, width):
+        vec = ref[layer : layer + 1, :]
+        full = jnp.concatenate([vec] * (width // vec.shape[1]), 1)
+        lane = lax.broadcasted_iota(jnp.int32, full.shape, 1)
+        return jnp.where(lane // vec.shape[1] == my, full, 0.0)
+
     for layer in range(dim.layers):
-        s = small[layer]
-        nu, theta, gam = s[5:6, : dim.N], s[5:6, dim.N :], s[6:7, : dim.N]
-        rate, angle = jnp.exp(nu), jnp.exp(theta)
-        mod = jnp.exp(-rate)
-        re, im = mod * jnp.cos(angle), mod * jnp.sin(angle)
-        gamma = jnp.exp(gam)
-
-        def put(index, a, b):
-            table[layer, index : index + 1, : dim.N] = a
-            table[layer, index : index + 1, dim.N :] = b
-
-        table[layer] = jnp.zeros((TABLE, dim.H), F32)
-        table[layer, :5, :] = s[:5]
-        put(GAMMA, gamma, gamma)
-        put(LAM, re, im)
-        put(RATES, rate, angle)
-        power = 1
-        while power < dim.L:
-            re, im = cmul(re, im, re, im)
-            power *= 2
-        for index in (LAM1, LAM2, LAM4, LAM8):
-            put(index, re, im)
-            re, im = cmul(re, im, re, im)
+        both = spread(glu_bias, layer, 2 * dim.H)
+        rows = [spread(ref, layer, dim.H) for ref in (gain, bias, skip)] + [both[:, : dim.H], both[:, dim.H :]]
+        rows.append(jnp.concatenate([spread(nu, layer, dim.N), spread(theta, layer, dim.N)], 1))
+        rows.append(jnp.concatenate([spread(gamma, layer, dim.N), jnp.zeros((1, dim.N), F32)], 1))
+        for i, value in enumerate(rows):
+            outs[layer][i : i + 1, :] = value
+        outs[layer][7:8, :] = jnp.zeros((1, dim.H), F32)
+    for move in moves[len(held) :]:
+        move.wait()
 
 
 class Weight:
-    def __init__(self, dim, layer, m, sources, own, buf, sem):
-        self.dim, self.layer, self.m = dim, layer, m
+    def __init__(self, dim, name, place, sources, own, buf, sem):
+        self.dim, self.name, self.place = dim, name, place
         self.sources, self.own, self.buf, self.sem = sources, own, buf, sem
         self.here = False
 
     def moves(self):
-        in_map, out_map, glu = self.sources[:3]
-        lo = max(self.m - 2, 0) * self.dim.H
-        shard = (in_map, out_map, glu, glu)[self.m].at[self.layer, :, pl.ds(lo, self.dim.H)]
+        shard = shard_of(self.sources, self.name, slice(None), self.dim.H)
         yield pltpu.make_async_copy(shard, self.own, self.sem.at[self.dim.S])
         for k, piece in enumerate(self.sources[3:]):
-            yield pltpu.make_async_copy(piece.at[self.m], self.buf.at[k], self.sem.at[k])
+            yield pltpu.make_async_copy(piece.at[self.place], self.buf.at[k], self.sem.at[k])
 
     def start(self):
         for move in self.moves():
@@ -446,15 +519,14 @@
         lax.fori_loop(0, dim.S, one, 0)
 
 
-def weights_in(dim, names, fn):
-    layers = sorted({layer for layer, _ in names})
-    first = 3 + len(layers) * dim.S
+def weights_in(dim, chunk, names, fn):
+    first = 3 + dim.S
 
     def kernel(*refs):
-        sources = {layer: refs[:3] + refs[3 + i * dim.S : 3 + (i + 1) * dim.S] for i, layer in enumerate(layers)}
         spare = refs[len(refs) - 3 * len(names) :]
         weights = [
-            Weight(dim, layer, m, sources[layer], *spare[3 * i : 3 * i + 3]) for i, (layer, m) in enumerate(names)
+            Weight(dim, name, CHUNKS[chunk].index(name), refs[:first], *spare[3 * i : 3 * i + 3])
+            for i, name in enumerate(names)
         ]
         for w in weights:
             w.start()
@@ -477,12 +549,11 @@
 
 
 def k_a0(dim, weights, x, table, xhat, rstd, drive, cf, fin, ah, al, wh, wl):
-    front(dim, strided(dim, x), table.at[0], weights[0], xhat, rstd, drive, cf, fin, ah, al, wh, wl)
-
-
-def k_b0(dim, weights, x, table, drive, cf, g, xhat,
+    front(dim, strided(dim, x), table, weights[0], xhat, rstd, drive, cf, fin, ah, al, wh, wl)
+
+
+def k_b0(dim, weights, x, t, t1, drive, cf, g, xhat,
          en, states, mixed, active, v, s, act1, xhat1, rstd1, drive1, cf1, fin1, ah, al, wh, wl):
-    t = table.at[0]
     w_out, w_gv, w_gg, w_in1 = weights
     back(dim, t, drive, cf, g, xhat, w_out, w_gv, w_gg, en, states, mixed, active, v, s, ah, al, wh, wl)
     load = strided(dim, x)
@@ -492,12 +563,11 @@
         act1[rows, :] = act
         return act
 
-    front(dim, residual, table.at[1], w_in1, xhat1, rstd1, drive1, cf1, fin1, ah, al, wh, wl)
-
-
-def k_b1(dim, weights, act1, out_grad, table, drive, cf, g, xhat,
+    front(dim, residual, t1, w_in1, xhat1, rstd1, drive1, cf1, fin1, ah, al, wh, wl)
+
+
+def k_b1(dim, weights, act1, out_grad, t, drive, cf, g, xhat,
          out, en, states, active, dv, dg, dmixed, ds, rcf, rfin, sums, ah, al, bh, bl, wh, wl, mixed, v, s):
-    t = table.at[1]
     w_out, w_gv, w_gg = weights
     back(dim, t, drive, cf, g, xhat, w_out, w_gv, w_gg, en, states, mixed, active, v, s, ah, al, wh, wl)
 
@@ -521,7 +591,7 @@
     weight_grad(dim, share, 2, ah, al, bh, bl, tile, keep, send)
 
 
-def k_c1(dim, weights, out_grad, table, ds, rcf, gr, states, en, drive, xhat, rstd, dmixed,
+def k_c1(dim, weights, out_grad, t, t0, ds, rcf, gr, states, en, drive, xhat, rstd, dmixed,
          xhat0, mixed0, v0, s0,
          dproj, dmid, dv0, dg0, dmixed0, ds0, rcf0, rfin0, sums1, sums0, ah, al, bh, bl, wh, wl, adj_en):
     w_in, w_gv, w_gg, w_out = weights
@@ -529,25 +599,22 @@
     def store(j, rows, value):
         dmid[rows, :] = value
 
-    bottom(dim, table.at[1], ds, rcf, gr, states, en, drive, xhat, rstd, dmixed, w_in, strided(dim, out_grad), store,
+    bottom(dim, t, ds, rcf, gr, states, en, drive, xhat, rstd, dmixed, w_in, strided(dim, out_grad), store,
            dproj, ds0, adj_en, sums1, ah, al, wh, wl)
     sums0[...] = jnp.zeros((SMALL, dim.H), F32)
-    top(dim, table.at[0], plain(dmid), v0, s0, mixed0, xhat0, w_gv, w_gg, w_out, dv0, dg0, dmixed0, ds0, rcf0, rfin0,
+    top(dim, t0, plain(dmid), v0, s0, mixed0, xhat0, w_gv, w_gg, w_out, dv0, dg0, dmixed0, ds0, rcf0, rfin0,
         sums0, ah, al, bh, bl, wh, wl)
 
 
-def k_w2(dim, share, active, dv, dg, states, dmixed, xhat1, dproj1, table, keep, send, ah, al, bh, bl, tile):
+def k_w2(dim, share, active, dv, dg, states, dmixed, xhat1, dproj1, t, keep, send, ah, al, bh, bl, tile):
     k_w1(dim, share, active, dv, dg, states, dmixed, keep, send, ah, al, bh, bl, tile)
-    t = table.at[1]
     split_rows(dim, lambda rows: xhat1[rows, :] * row(t, GAIN) + row(t, BIAS), ah, al)
     split_rows(dim, lambda rows: dproj1[rows, :], bh, bl)
     weight_grad(dim, share, 3, ah, al, bh, bl, tile, keep, send)
 
 
-def k_c0(share, dim, weights, table, ds, rcf, gr, states, en, drive, xhat, rstd, dmixed, dmid, sums1a, sums1b, sums0a,
+def k_c0(share, dim, weights, t, ds, rcf, gr, states, en, drive, xhat, rstd, dmixed, dmid, sums1a, sums1b, sums0a,
          input_grad, keep, send, ah, al, bh, bl, wh, wl, adj_en, dproj, buf, sums0, tile):
-    t = table.at[0]
-
     def store(j, rows, value):
         input_grad[:, j, :] = value
 
@@ -560,17 +627,20 @@
     tile[0:SMALL, :] = jnp.where(upper, sums0a[...], sums0[...])
     tile[SMALL : 2 * SMALL, :] = jnp.where(upper, sums1a[...], sums1b[...])
     me = lax.axis_index("seq")
-    n = -(-2 * SMALL // dim.S)
-
-    def put(odd):
-        for s in range(dim.S):
-            dst = keep if (s & 1) == odd else send
-            lo = min(s * n, 2 * SMALL - n)
+
+    def put(mine):
+        for layer in range(dim.layers):
+            dst = keep if layer == mine else send
             for d in range(dim.D):
-                dst[(s ^ me) >> 1, d, share.q : share.q + n, :] = tile[lo : lo + n, :]
-
-    for odd in range(2):
-        pl.when(me & 1 == odd)(functools.partial(put, odd))
+                dst[d, share.q :, :] = tile[layer * SMALL : (layer + 1) * SMALL, :]
+
+    for mine in range(2):
+        pl.when(me & 1 == mine)(functools.partial(put, mine))
+
+
+def tie(x, others):
+    x, *others = lax.optimization_barrier((x, *others))
+    return x, others
 
 
 def swap(x, axis, mask):
@@ -578,33 +648,42 @@
     return lax.ppermute(x, axis, [(i, i ^ mask) for i in range(count)])
 
 
+def chips_gather(dim, x):
+    return [x] + [swap(x, "seq", k) for k in range(2, dim.S, 2)]
+
+
+def cores_gather(pieces):
+    return [p for x in pieces for p in (x, swap(x, "seq", 1))]
+
+
 def plane_gather(dim, x):
-    pieces = [None] * dim.S
-    pieces[0] = x
-    for k in range(2, dim.S, 2):
-        pieces[k] = swap(x, "seq", k)
-    for k in range(0, dim.S, 2):
-        pieces[k + 1] = swap(pieces[k], "seq", 1)
-    return pieces
-
-
-def reduce_share(dim, keep, send):
+    return cores_gather(chips_gather(dim, x))
+
+
+def tree_sum(parts):
+    while len(parts) > 1:
+        parts = [a + b for a, b in zip(parts[::2], parts[1::2])]
+    return parts[0]
+
+
+def half_sums(dim, keep, send):
     got = swap(send, "seq", 1)
-    half = [keep[k] + got[k] for k in range(dim.S // 2)]
-    total = half[0]
-    for k in range(1, dim.S // 2):
-        total = total + swap(half[k], "seq", 2 * k)
-    out = total[0]
-    for k in range(1, dim.D):
-        out = out + swap(total[k], "dp", k)
-    return out
-
-
-def unpack_kernel(dim, shares, *refs):
-    count = len(shares) * dim.S
-    pieces, (g_in, g_out, g_glu, vectors) = refs[:count], refs[count:]
-    me = lax.axis_index("seq")
-    n = -(-2 * SMALL // dim.S)
+    return [keep[k] + got[k] for k in range(dim.S // 2)]
+
+
+def plane_sums(dim, half):
+    others = [swap(half[k], "seq", 2 * k) for k in range(1, dim.S // 2)]
+    return [sum((o[k] for o in others), half[0][k]) for k in range(dim.D)]
+
+
+def dp_sum(dim, parts):
+    return sum((swap(parts[k], "dp", k) for k in range(1, dim.D)), parts[0])
+
+
+def unpack_kernel(dim, shares, kinds, last, *refs):
+    pieces, (mine, other), outs = refs[: dim.S], refs[dim.S : dim.S + 2], refs[dim.S + 2 :]
+    g_gain, g_bias, g_nu, g_theta, g_gamma, g_in, g_out, g_skip, g_glu, g_glu_bias = outs
+    me, my = lax.axis_index("seq"), lax.axis_index("dp")
 
     def place(layer, kind, rows, value):
         if kind == "in":
@@ -616,38 +695,59 @@
         else:
             g_glu[layer, rows, dim.H : 2 * dim.H] = value
 
-    for i, (share, kinds) in enumerate(shares):
-        for k in range(dim.S):
-            src = pieces[i * dim.S + k]
-            s = k ^ me
-
-            def one(known):
-                for off in range(0, share.q, share.step):
-                    p = known * share.q + off
-                    m = p // dim.Hd
-                    if m < share.nm:
-                        layer, kind = kinds[m]
-                        r = p % dim.Hd
-                        place(layer, kind, slice(r, r + share.step), src[off : off + share.step, :])
-                if share.extra:
-                    lo = min(known * n, 2 * SMALL - n)
-                    vectors[lo : lo + n, :] = src[share.q : share.q + n, :]
-
-            for known in range(dim.S):
-                pl.when(s == known)(functools.partial(one, known))
-
-
-def unpack(dim, shares, pieces):
-    args = [p for group in pieces for p in group]
-    outs = [f32(dim.layers, dim.Hd, dim.H), f32(dim.layers, dim.Hd, dim.H), f32(dim.layers, dim.Hd, 2 * dim.H),
-            f32(2 * SMALL, dim.H)]
-    return call(functools.partial(unpack_kernel, dim, shares), outs, [], *args)
-
-
-def spread(vec, width, my):
-    count = width // vec.shape[1]
-    lane = lax.broadcasted_iota(jnp.int32, (vec.shape[0], width), 1)
-    return jnp.where(lane // vec.shape[1] == my, jnp.tile(vec, (1, count)), 0.0)
+    def put(k, s):
+        base = 0
+        for share, names in zip(shares, kinds):
+            for off in range(0, share.q, share.step):
+                p = s * share.q + off
+                if p // dim.Hd < share.nm:
+                    layer, kind = names[p // dim.Hd]
+                    r = p % dim.Hd
+                    place(layer, kind, slice(r, r + share.step), pieces[k][base + off : base + off + share.step, :])
+            base += share.q
+
+    def vectors(d):
+        def own(layer, index, lo, width, out, at=0):
+            src = (mine, other)
+
+            def copy(ref):
+                start = lo + d * width
+                out[layer : layer + 1, :] = ref[last.q + index : last.q + index + 1, start : start + width]
+
+            pl.when(me & 1 == layer)(functools.partial(copy, src[0]))
+            pl.when(me & 1 != layer)(functools.partial(copy, src[1]))
+
+        for layer in range(dim.layers):
+            for index, out in ((GAIN, g_gain), (BIAS, g_bias), (SKIP, g_skip)):
+                own(layer, index, 0, dim.Hd, out)
+            n = dim.N // dim.D
+            own(layer, 5, 0, n, g_nu)
+            own(layer, 5, dim.N, n, g_theta)
+            own(layer, 6, 0, n, g_gamma)
+            width = 2 * dim.H // dim.D
+            index = BIAS_V if d * width < dim.H else BIAS_G
+            own(layer, index, 0 if index == BIAS_V else -dim.H, width, g_glu_bias)
+
+    for who in range(dim.S):
+
+        def all_of(who=who):
+            for k in range(dim.S):
+                put(k, k ^ who)
+            half = who & 1
+            for ref, part in ((mine, half), (other, 1 - half)):
+                place(0, "in", slice(part * last.q, (part + 1) * last.q), ref[: last.q, :])
+
+        pl.when(me == who)(all_of)
+    for d in range(dim.D):
+        pl.when(my == d)(functools.partial(vectors, d))
+
+
+def unpack(dim, shares, kinds, last, pieces, mine, other):
+    n, l = dim.N // dim.D, dim.layers
+    vec, small = f32(l, dim.Hd), f32(l, n)
+    mat, wide = f32(l, dim.Hd, dim.H), f32(l, dim.Hd, 2 * dim.H)
+    outs = [vec, vec, small, small, small, mat, mat, vec, wide, f32(l, 2 * dim.H // dim.D)]
+    return call(functools.partial(unpack_kernel, dim, shares, kinds, last), outs, [], *pieces, mine, other)
 
 
 def body(inputs, out_grad, ln_gain, ln_bias, nu_log, theta_log, gamma_log, in_map, out_map, skip_gain, glu_weight, glu_bias):
@@ -657,140 +757,129 @@
     x = inputs.reshape(R, dim.L, H)
     og = out_grad.reshape(R, dim.L, H)
 
-    both = spread(glu_bias, 2 * H, my)
-    small = jnp.stack(
-        [
-            spread(ln_gain, H, my),
-            spread(ln_bias, H, my),
-            spread(skip_gain, H, my),
-            both[:, :H],
-            both[:, H:],
-            jnp.concatenate([spread(nu_log, N, my), spread(theta_log, N, my)], 1),
-            spread(gamma_log, H, my),
-            jnp.zeros_like(ln_gain, shape=(dim.layers, H)),
-        ],
-        1,
+    heads = [SMALL, SMALL, 0]
+    vectors = (ln_gain, ln_bias, skip_gain, nu_log, theta_log, gamma_log, glu_bias)
+    messages = call(
+        functools.partial(pack_kernel, dim),
+        [f32(head + len(chunk) * dim.q, H) for head, chunk in zip(heads, CHUNKS)],
+        [pltpu.VMEM(v.shape, F32) for v in vectors] + [pltpu.SemaphoreType.DMA((len(vectors) + sum(map(len, CHUNKS)),))],
+        in_map, out_map, glu_weight, *vectors,
+        anywhere=3 + len(vectors),
     )
-    pieces = []
-    table = None
-    start = jnp.minimum(me, dim.used - 1) * dim.q
-    for layer in range(dim.layers):
-
-        def cut(w, lo):
-            return lax.dynamic_slice(w, (layer, start, lo), (1, dim.q, H))[0]
-
-        mine = jnp.concatenate([cut(in_map, 0), cut(out_map, 0), cut(glu_weight, 0), cut(glu_weight, H)], 0)
-        if layer == 0:
-            mine = jnp.concatenate([small.reshape(-1, H), mine], 0)
-        others = [swap(mine, "dp", k) for k in range(1, D)]
-        if layer == 0:
-            first = dim.layers * SMALL
-            total = mine[:first]
-            for other in others:
-                total = total + other[:first]
-            table = call(
-                functools.partial(prep_kernel, dim), [f32(dim.layers, TABLE, H)], [], total.reshape(small.shape)
-            )[0]
-            others = [other[first:] for other in others]
-        joined = jnp.stack([other.reshape(4, dim.q, H) for other in others], 1)
-        pieces.append(plane_gather(dim, joined))
-
-    unit = 2 * T * H * H
-    big, ent, fins = f32(T, H), f32(R, H), f32(B, H)
-    stat = f32(T, 128)
-    vec = f32(SMALL, H)
-
-    def k(fn, names, outs, scratch, *args, n):
-        kernel, count, own = weights_in(dim, names, fn)
-        layers = sorted({layer for layer, _ in names})
-        sources = [in_map, out_map, glu_weight] + [p for layer in layers for p in pieces[layer]]
-        return call(kernel, outs, scratch + own, *sources, *args, flops=3 * n * unit, anywhere=count)
+    def stacked(others, head):
+        return jnp.stack([other[head:].reshape(-1, dim.q, H) for other in others], 1)
+
+    def along_dp(mine):
+        return [swap(mine, "dp", k) for k in range(1, D)]
+
+    def table_of(mine, others, head=SMALL):
+        total = mine[:head]
+        for other in others:
+            total = total + other[:head]
+        return call(functools.partial(prep_kernel, dim), [f32(TABLE, H)], [], total)[0]
+
+    mine0, mine1, mine2 = messages
+    others0 = along_dp(mine0)
+    table0 = table_of(mine0, others0)
+    mine1, others0 = tie(mine1, others0)
+    others1 = along_dp(mine1)
+    table1 = table_of(mine1, others1)
+    chips0 = chips_gather(dim, stacked(others0, SMALL))
+    joined1, chips0 = tie(stacked(others1, SMALL), chips0)
+    pieces0 = cores_gather(chips0)
+    chips1 = chips_gather(dim, joined1)
+    mine2, (chips1[1],) = tie(mine2, [chips1[1]])
+    joined2 = stacked(along_dp(mine2), 0)
+    pieces = [pieces0, cores_gather(chips1), None]
+
+    big, ent, fins = pltpu.VMEM((T, H), F32), pltpu.VMEM((R, H), F32), f32(B, H)
+    stat = pltpu.VMEM((T, 128), F32)
+    vec = pltpu.VMEM((SMALL, H), F32)
+
+    def k(fn, chunk, names, outs, scratch, *args, us):
+        kernel, count, own = weights_in(dim, chunk, names, fn)
+        sources = [in_map, out_map, glu_weight] + pieces[chunk]
+        return call(kernel, outs, scratch + own, *sources, *args, us=us, anywhere=count)
 
     def carried(fin):
         return lax.all_gather(fin, "seq")
 
     xhat0, rstd0, drive0, cf0, fin0 = k(
-        k_a0, [(0, 0)], [big, stat, big, ent, fins], halves(dim, 1), x, table, n=1
+        k_a0, 0, [(0, 0)], [big, stat, big, ent, fins], halves(dim, 1), x, table0, us=3.4
     )
     g0 = carried(fin0)
+    joined2, (g0,) = tie(joined2, [g0])
+    chips2 = chips_gather(dim, joined2)
     en0, states0, mixed0, active0, v0, s0, act1, xhat1, rstd1, drive1, cf1, fin1 = k(
         k_b0,
+        1,
         [(0, 1), (0, 2), (0, 3), (1, 0)],
         [ent, big, big, big, big, big, big, big, stat, big, ent, fins],
         halves(dim, 1),
-        x, table, drive0, cf0, g0, xhat0,
-        n=4,
+        x, table0, table1, drive0, cf0, g0, xhat0,
+        us=10.0,
     )
+    fin1, chips2 = tie(fin1, chips2)
     g1 = carried(fin1)
+    pieces[2] = cores_gather(chips2)
     spare = [pltpu.VMEM((T, H), F32)]
     out, en1, states1, active1, dv1, dg1, dmixed1, ds1, rcf1, rfin1, sums1a = k(
         k_b1,
+        2,
         [(1, 1), (1, 2), (1, 3)],
         [f32(R, dim.L, H), ent, big, big, big, big, big, big, ent, fins, vec],
         halves(dim, 2) + spare * 3,
-        act1, og, table, drive1, cf1, g1, xhat1,
-        n=6,
+        act1, og, table1, drive1, cf1, g1, xhat1,
+        us=13.0,
     )
-    gr1 = carried(rfin1)
-    share1, share2, share3 = Share(dim, 3), Share(dim, 4), Share(dim, 1, 8)
+    share1, share2, share3 = Share(dim, 3), Share(dim, 4), Halves(dim)
     tile = [pltpu.VMEM((WIDE, H), F32)]
     pair = [pltpu.VMEM((T, H), BF16)] * 4
     keep1, send1 = call(
         functools.partial(k_w1, dim, share1), [f32(*share1.shape)] * 2, pair + tile,
-        active1, dv1, dg1, states1, dmixed1, flops=9 * unit,
+        active1, dv1, dg1, states1, dmixed1, us=5.0,
     )
+    rfin1, (send1,) = tie(rfin1, [send1])
+    gr1 = carried(rfin1)
+    gr1, half1 = tie(gr1, half_sums(dim, keep1, send1))
     dproj1, dmid, dv0, dg0, dmixed0, ds0, rcf0, rfin0, sums1b, sums0a = k(
         k_c1,
+        1,
         [(1, 0), (0, 2), (0, 3), (0, 1)],
         [big, big, big, big, big, big, ent, fins, vec, vec],
         halves(dim, 2) + [pltpu.VMEM((R, H), F32)],
-        og, table, ds1, rcf1, gr1, states1, en1, drive1, xhat1, rstd1, dmixed1,
+        og, table1, table0, ds1, rcf1, gr1, states1, en1, drive1, xhat1, rstd1, dmixed1,
         xhat0, mixed0, v0, s0,
-        n=4,
+        us=11.0,
     )
-    gr0 = carried(rfin0)
     keep2, send2 = call(
         functools.partial(k_w2, dim, share2), [f32(*share2.shape)] * 2, pair + tile,
-        active0, dv0, dg0, states0, dmixed0, xhat1, dproj1, table, flops=12 * unit,
+        active0, dv0, dg0, states0, dmixed0, xhat1, dproj1, table1, us=6.4,
     )
+    rfin0, (send2, *sums1) = tie(rfin0, [send2, *plane_sums(dim, half1)])
+    gr0 = carried(rfin0)
+    upper1 = dp_sum(dim, sums1)
+    gr0, (upper1, *half2) = tie(gr0, [upper1, *half_sums(dim, keep2, send2)])
     input_grad, keep3, send3 = k(
         functools.partial(k_c0, share3),
+        0,
         [(0, 0)],
         [f32(R, dim.L, H)] + [f32(*share3.shape)] * 2,
         halves(dim, 2) + [pltpu.VMEM((R, H), F32)] + spare * 2 + [pltpu.VMEM((SMALL, H), F32)] + tile,
-        table, ds0, rcf0, gr0, states0, en0, drive0, xhat0, rstd0, dmixed0, dmid, sums1a, sums1b, sums0a,
-        n=2,
+        table0, ds0, rcf0, gr0, states0, en0, drive0, xhat0, rstd0, dmixed0, dmid, sums1a, sums1b, sums0a,
+        us=7.4,
     )
-    shared = [plane_gather(dim, reduce_share(dim, a, b)) for a, b in ((keep1, send1), (keep2, send2), (keep3, send3))]
-    kinds1 = [(1, "gv"), (1, "gg"), (1, "out")]
-    kinds2 = [(0, "gv"), (0, "gg"), (0, "out"), (1, "in")]
-    kinds3 = [(0, "in")]
-    g_in, g_out, g_glu, vectors = unpack(
-        dim, [(share1, kinds1), (share2, kinds2), (share3, kinds3)], shared
-    )
-    vectors = vectors.reshape(2, SMALL, H)
-
-    def own(index, lo, width, total):
-        rows = vectors[:, index, lo : lo + width]
-        part = width // D if total is None else total
-        return lax.dynamic_slice_in_dim(rows, my * part, part, 1)
-
-    glu_rows = jnp.concatenate([vectors[:, BIAS_V], vectors[:, BIAS_G]], 1)
-    part = 2 * H // D
-    return (
-        out.reshape(inputs.shape),
-        input_grad.reshape(inputs.shape),
-        own(GAIN, 0, H, None),
-        own(BIAS, 0, H, None),
-        own(5, 0, N, None),
-        own(5, N, N, None),
-        own(6, 0, N, None),
-        g_in,
-        g_out,
-        own(SKIP, 0, H, None),
-        g_glu,
-        lax.dynamic_slice_in_dim(glu_rows, my * part, part, 1),
-    )
+    sums2 = plane_sums(dim, half2)
+    got3 = swap(send3, "seq", 1)
+    half3 = [keep3[d] + got3[d] for d in range(D)]
+    half3[0], sums2 = tie(half3[0], sums2)
+    total3 = tree_sum([half3[0]] + [swap(half3[k], "dp", k) for k in range(1, D)])
+    mine3 = tree_sum(chips_gather(dim, total3))
+    other3 = swap(mine3, "seq", 1)
+    upper = plane_gather(dim, jnp.concatenate([upper1, dp_sum(dim, sums2)], 0))
+    kinds = [[(1, "gv"), (1, "gg"), (1, "out")], [(0, "gv"), (0, "gg"), (0, "out"), (1, "in")]]
+    grads = unpack(dim, (share1, share2), kinds, share3, upper, mine3, other3)
+    return (out.reshape(inputs.shape), input_grad.reshape(inputs.shape), *grads)
 
 
 def solution(mesh):

time: 307 us -> 227 us (0.74)
  Pallas kernels: 93.2 us -> 59.6 us
  starting transfers between devices: 100 us -> 70.2 us
  local copies, waits for them, and re-layouts: 17.6 us -> 1.89 us
  waiting for transfers between devices: 48.6 us -> 53 us
  other arithmetic: 4.78 us -> 1.57 us
    pallas_call x9 -> x11, Pallas kernels: 93.2 us -> 59.6 us  [call(): pl.pallas_call(fn, out_shape=outs, in_specs=[pl.BlockSpec(memory_space=sp...]
    ppermute x62 -> x59, starting transfers between devices: 100 us -> 70.2 us  [swap(): return lax.ppermute(x, axis, [(i, i ^ mask) for i in range(count)])]
    another operation x13 -> x2, local copies, waits for them, and re-layouts: 4.41 us -> 0.01 us  [stacked(): jnp.stack([other[head:].reshape(-1, dim.q, H) for other in others], 1)]
    ppermute x62 -> x59, waiting for transfers between devices: 48.6 us -> 53 us  [swap(): return lax.ppermute(x, axis, [(i, i ^ mask) for i in range(count)])]
    dynamic_slice x6 -> x0, local copies, waits for them, and re-layouts: 3.6 us -> none  [own(): return lax.dynamic_slice_in_dim(rows, my * part, part, 1)]
    unnamed x94 -> x52, local copies, waits for them, and re-layouts: 5.43 us -> 1.86 us
  transfers between devices with their start and end apart: 62 -> 59, of which waited for: 19 -> 20; matrix products, arithmetic and copies ran while one was open for 4% -> 0% of each run, Pallas kernels for 9% -> 17%
where the time goes in v2:
time: 227 us
  starting transfers between devices  70.2 us (31%)
  Pallas kernels  59.6 us (26%)
  waiting for transfers between devices  53 us (23%)
  blocking collectives  39.3 us (17%)
    ppermute x59, starting transfers between devices, swap(): return lax.ppermute(x, axis, [(i, i ^ mask) for i in range(count)])  70.2 us
    pallas_call x11, Pallas kernels, call(): pl.pallas_call(fn, out_shape=outs, in_specs=[pl.BlockSpec(memory_space=sp...  59.6 us
    ppermute x59, waiting for transfers between devices, swap(): return lax.ppermute(x, axis, [(i, i ^ mask) for i in range(count)])  53 us
    all_gather x4, blocking collectives, carried(): return lax.all_gather(fin, 'seq')  39.3 us
  transfers between devices with their start and end apart: 59, of which 20 were waited for; matrix products, arithmetic and copies ran while one was open for 0% of the time, Pallas kernels for 17%

profile of v2, /device:TPU:9, one launch (start us, length us, event | category | flops | bytes accessed | tf_op | source)
XLA Modules:
  0.0 226.9 jit_solution(11434729434822374448)
XLA Ops:
  1.9 2.5 %collective-permute-start.1 = (f32[24,512]{1,0:T(8,128)S(1)}, f32[24,512]{1,0:T(8,128)S(1)}, u32[]{:S(2)}, u32[]{:S(2)}) collective-permute-start(f32[24,512]{1,0:T(8,128)S(1)} %get-tuple-element.113), channel_id=1, source_target_pairs={{0,16},{8,24},{16,0},{24,8},{1,17},{9,25},{17,1},{25,9},{2,18},{10... | collective-permute-start | bytes 147464 | tf_op jit(solution)/shard_map/ppermute | solution.py:648
  16.7 6.8 %collective-permute-done.5 = f32[72,512]{1,0:T(8,128)S(1)} collective-permute-done((f32[72,512]{1,0:T(8,128)S(1)}, f32[72,512]{1,0:T(8,128)S(1)}, u32[]{:S(2)}, u32[]{:S(2)}) %collective-permute-start.5) | collective-permute-done | bytes 147488 | tf_op jit(solution)/shard_map/ppermute | solution.py:648
  26.3 3.4 %collective-permute-start.16 = (f32[1,3,16,512]{3,2,1,0:T(8,128)S(1)}, f32[1,3,16,512]{3,2,1,0:T(8,128)S(1)}, u32[]{:S(2)}, u32[]{:S(2)}) collective-permute-start(f32[1,3,16,512]{3,2,1,0:T(8,128)S(1)} %pad_maximum_fusion.3.refs_3_), channel_id=1, source_target_pairs={{0,1},{1,0},{2,3},{3,2},{4,5},{5,4},{6,7},{7,6},{8,9},{9,8},{10,11... | collective-permute-start | bytes 294920 | tf_op jit(solution)/shard_map/ppermute | solution.py:648
  31.7 6.6 %collective-permute-start.19 = (f32[1,3,16,512]{3,2,1,0:T(8,128)S(1)}, f32[1,3,16,512]{3,2,1,0:T(8,128)S(1)}, u32[]{:S(2)}, u32[]{:S(2)}) collective-permute-start(f32[1,3,16,512]{3,2,1,0:T(8,128)S(1)} %collective-permute-done.8.refs_9_), channel_id=1, source_target_pairs={{0,1},{1,0},{2,3},{3,2},{4,5},{5,4},{6,7},{7,6},{8,9},{9,8},{10,11... | collective-permute-start | bytes 294920 | tf_op jit(solution)/shard_map/ppermute | solution.py:648
  42.1 3.4 %shard_map.214 = (f32[512,512]{1,0:T(8,128)S(1)}, f32[512,128]{1,0:T(8,128)S(1)}, f32[512,512]{1,0:T(8,128)S(1)}, f32[16,512]{1,0:T(8,128)S(1)}, f32[2,512]{1,0:T(2,128)S(1)}) custom-call(f32[2,128,512]{2,1,0:T(8,128)} %refs_0_.9, f32[2,128,512]{2,1,0:T(8,128)} %refs_1_.9, f32[2,128,1024]{2,1,0:T(8,128)} %refs_2_.9, f32[1,3,16,512]{3,2,1,0:T(8,128)} %copy-done.11, ...), custom_call_target="tpu_custom_call" | custom-call | flops 1 | bytes 12240000 | tf_op jit(solution)/shard_map/pallas_call | solution.py:383
  45.5 12.6 %all-gather.4.refs_16_ = f32[8,2,512]{2,1,0:T(2,128)S(1)} all-gather(f32[1,2,512]{2,1,0:T(2,128)S(1)} %bitcast.67), channel_id=2, replica_groups=mesh['dp'=4,'seq'=8] {'seq'}, dimensions={0}, use_global_device_ids=true | all-gather | bytes 36864 | tf_op jit(solution)/shard_map/all_gather | solution.py:805
  62.4 10.2 %shard_map.215 = (f32[16,512]{1,0:T(8,128)S(1)}, f32[512,512]{1,0:T(8,128)S(1)}, f32[512,512]{1,0:T(8,128)S(1)}, f32[512,512]{1,0:T(8,128)S(1)}, f32[512,512]{1,...) custom-call(f32[2,128,512]{2,1,0:T(8,128)} %refs_0_.9, ...), custom_call_target="tpu_custom_call" | custom-call | flops 1 | bytes 36000000 | tf_op jit(solution)/shard_map/pallas_call | solution.py:383
  75.4 9.3 %all-gather.5.refs_16_ = f32[8,2,512]{2,1,0:T(2,128)S(1)} all-gather(f32[1,2,512]{2,1,0:T(2,128)S(1)} %bitcast.65), channel_id=3, replica_groups=mesh['dp'=4,'seq'=8] {'seq'}, dimensions={0}, use_global_device_ids=true | all-gather | bytes 36864 | tf_op jit(solution)/shard_map/all_gather | solution.py:805
  85.7 13.4 %shard_map.216 = (f32[16,32,512]{2,1,0:T(8,128)}, f32[16,512]{1,0:T(8,128)S(1)}, f32[512,512]{1,0:T(8,128)S(1)}, f32[512,512]{1,0:T(8,128)S(1)}, f32[512,512]{1,...) custom-call(f32[2,128,512]{2,1,0:T(8,128)} %refs_0_.9, ...), custom_call_target="tpu_custom_call" | custom-call | flops 1 | bytes 46800000 | tf_op jit(solution)/shard_map/pallas_call | solution.py:383
  99.1 4.9 %shard_map.217 = (f32[4,4,48,512]{3,2,1,0:T(8,128)S(1)}, f32[4,4,48,512]{3,2,1,0:T(8,128)S(1)}) custom-call(f32[512,512]{1,0:T(8,128)S(1)} %get-tuple-element.146.active, f32[512,512]{1,0:T(8,128)S(1)} %get-tuple-element.147.dv, f32[512,512]{1,0:T(8,128)S(1)} %get-tuple-element.148.dg, f32[512,512]{1,0:T(8,128)S(1)} %get-tuple-element.149.states.refs_17_, ...), custom_call_target="tpu_custom_call" | custom-call | flops 1 | bytes 18000000 | tf_op jit(solution)/shard_map/pallas_call | solution.py:383
  104.2 8.2 %all-gather.6.refs_16_ = f32[8,2,512]{2,1,0:T(2,128)S(1)} all-gather(f32[1,2,512]{2,1,0:T(2,128)S(1)} %bitcast.66), channel_id=4, replica_groups=mesh['dp'=4,'seq'=8] {'seq'}, dimensions={0}, use_global_device_ids=true | all-gather | bytes 36864 | tf_op jit(solution)/shard_map/all_gather | solution.py:805
  115.6 10.7 %shard_map.218 = (f32[512,512]{1,0:T(8,128)S(1)}, f32[512,512]{1,0:T(8,128)S(1)}, f32[512,512]{1,0:T(8,128)S(1)}, f32[512,512]{1,0:T(8,128)S(1)}, f32[512,512]{1...) custom-call(f32[2,128,512]{2,1,0:T(8,128)} %refs_0_.9, ...), custom_call_target="tpu_custom_call" | custom-call | flops 1 | bytes 39600000 | tf_op jit(solution)/shard_map/pallas_call | solution.py:383
  126.3 6.3 %shard_map.219 = (f32[4,4,64,512]{3,2,1,0:T(8,128)S(1)}, f32[4,4,64,512]{3,2,1,0:T(8,128)S(1)}) custom-call(f32[512,512]{1,0:T(8,128)S(1)} %get-tuple-element.164.active, f32[512,512]{1,0:T(8,128)S(1)} %get-tuple-element.165.dv, f32[512,512]{1,0:T(8,128)S(1)} %get-tuple-element.166.dg, f32[512,512]{1,0:T(8,128)S(1)} %get-tuple-element.167.states.refs_15_, ...), custom_call_target="tpu_custom_call" | custom-call | flops 1 | bytes 23040000 | tf_op jit(solution)/shard_map/pallas_call | solution.py:383
  134.3 3.4 %collective-permute-start.34 = (f32[48,512]{1,0:T(8,128)S(1)}, f32[48,512]{1,0:T(8,128)S(1)}, u32[]{:S(2)}, u32[]{:S(2)}) collective-permute-start(f32[48,512]{1,0:T(8,128)S(1)} %get-tuple-element.177), channel_id=1, source_target_pairs={{0,8},{8,0},{16,24},{24,16},{1,9},{9,1},{17,25},{25,17},{2,10},{10... | collective-permute-start | bytes 294920 | tf_op jit(solution)/shard_map/ppermute | solution.py:648
  138.8 9.2 %all-gather.7.refs_14_ = f32[8,2,512]{2,1,0:T(2,128)S(1)} all-gather(f32[1,2,512]{2,1,0:T(2,128)S(1)} %bitcast.64), channel_id=5, replica_groups=mesh['dp'=4,'seq'=8] {'seq'}, dimensions={0}, use_global_device_ids=true | all-gather | bytes 36864 | tf_op jit(solution)/shard_map/all_gather | solution.py:805
  151.3 7.4 %shard_map.220 = (f32[16,32,512]{2,1,0:T(8,128)}, f32[4,72,512]{2,1,0:T(8,128)S(1)}, f32[4,72,512]{2,1,0:T(8,128)S(1)}) custom-call(f32[2,128,512]{2,1,0:T(8,128)} %refs_0_.9, f32[2,128,512]{2,1,0:T(8,128)} %refs_1_.9, f32[2,128,1024]{2,1,0:T(8,128)} %refs_2_.9, f32[1,3,16,512]{3,2,1,0:T(8,128)} %copy-done.11, f32[1,3,16,512]{3,2,1,0:T(8,128)} %copy-done.15, ...), custom_call_target="tpu_custom_call" | custom-call | flops 1 | bytes 26640000 | tf_op jit(solution)/shard_map/pallas_call | solution.py:383
  161.6 11.3 %collective-permute-done.41 = f32[4,64,512]{2,1,0:T(8,128)S(1)} collective-permute-done((f32[4,64,512]{2,1,0:T(8,128)S(1)}, f32[4,64,512]{2,1,0:T(8,128)S(1)}, u32[]{:S(2)}, u32[]{:S(2)}) %collective-permute-start.41) | collective-permute-done | bytes 524320 | tf_op jit(solution)/shard_map/ppermute | solution.py:648
  173.3 3.3 %collective-permute-start.42 = (f32[64,512]{1,0:T(8,128)S(1)}, f32[64,512]{1,0:T(8,128)S(1)}, u32[]{:S(2)}, u32[]{:S(2)}) collective-permute-start(f32[64,512]{1,0:T(8,128)S(1)} %get-tuple-element.198), channel_id=1, source_target_pairs={{0,8},{8,0},{16,24},{24,16},{1,9},{9,1},{17,25},{25,17},{2,10},{10... | collective-permute-start | bytes 393224 | tf_op jit(solution)/shard_map/ppermute | solution.py:648
  177.9 2.3 %collective-permute-start.52 = (f32[72,512]{1,0:T(8,128)S(1)}, f32[72,512]{1,0:T(8,128)S(1)}, u32[]{:S(2)}, u32[]{:S(2)}) collective-permute-start(f32[72,512]{1,0:T(8,128)S(1)} %get-tuple-element.228), channel_id=1, source_target_pairs={{0,8},{8,0},{16,24},{24,16},{1,9},{9,1},{17,25},{25,17},{2,10},{10... | collective-permute-start | bytes 442376 | tf_op jit(solution)/shard_map/ppermute | solution.py:648
  181.9 8.0 %collective-permute-done.44 = f32[64,512]{1,0:T(8,128)S(1)} collective-permute-done((f32[64,512]{1,0:T(8,128)S(1)}, f32[64,512]{1,0:T(8,128)S(1)}, u32[]{:S(2)}, u32[]{:S(2)}) %collective-permute-start.44) | collective-permute-done | bytes 131104 | tf_op jit(solution)/shard_map/ppermute | solution.py:648
  189.9 6.7 %collective-permute-done.53 = f32[72,512]{1,0:T(8,128)S(1)} collective-permute-done((f32[72,512]{1,0:T(8,128)S(1)}, f32[72,512]{1,0:T(8,128)S(1)}, u32[]{:S(2)}, u32[]{:S(2)}) %collective-permute-start.53) | collective-permute-done | bytes 147488 | tf_op jit(solution)/shard_map/ppermute | solution.py:648
  196.7 5.0 %collective-permute-done.54 = f32[72,512]{1,0:T(8,128)S(1)} collective-permute-done((f32[72,512]{1,0:T(8,128)S(1)}, f32[72,512]{1,0:T(8,128)S(1)}, u32[]{:S(2)}, u32[]{:S(2)}) %collective-permute-start.54) | collective-permute-done | bytes 147488 | tf_op jit(solution)/shard_map/ppermute | solution.py:648
  207.1 4.5 %collective-permute-done.56 = f32[72,512]{1,0:T(8,128)S(1)} collective-permute-done((f32[72,512]{1,0:T(8,128)S(1)}, f32[72,512]{1,0:T(8,128)S(1)}, u32[]{:S(2)}, u32[]{:S(2)}) %collective-permute-start.56) | collective-permute-done | bytes 147488 | tf_op jit(solution)/shard_map/ppermute | solution.py:648
  211.6 11.0 %collective-permute-start.45 = (f32[112,512]{1,0:T(8,128)S(1)}, f32[112,512]{1,0:T(8,128)S(1)}, u32[]{:S(2)}, u32[]{:S(2)}) collective-permute-start(f32[112,512]{1,0:T(8,128)S(1)} %pad_maximum_fusion.2.refs_0_), channel_id=1, source_target_pairs={{0,1},{1,0},{2,3},{3,2},{4,5},{5,4},{6,7},{7,6},{8,9},{9,8},{10,11... | collective-permute-start | bytes 688136 | tf_op jit(solution)/shard_map/ppermute | solution.py:648
  (181 shorter events, 55.4 us)
Async XLA Ops:
  24.9 14.4 %collective-permute-start.12 = (f32[4,3,16,512]{3,2,1,0:T(8,128)S(1)}, f32[4,3,16,512]{3,2,1,0:T(8,128)S(1)}, u32[]{:S(2)}, u32[]{:S(2)}) collective-permute-start(f32[4,3,16,512]{3,2,1,0:T(8,128)S(1)} %pad_maximum_fusion.refs_3_), channel_id=1, source_target_pairs={{0,4},{1,5},{2,6},{3,7},{4,0},{5,1},{6,2},{7,3},{8,12},{9,13},{10,... | collective-permute-start | bytes 1179656 | tf_op jit(solution)/shard_map/ppermute | solution.py:648
  26.1 15.0 %collective-permute-start.14 = (f32[4,3,16,512]{3,2,1,0:T(8,128)S(1)}, f32[4,3,16,512]{3,2,1,0:T(8,128)S(1)}, u32[]{:S(2)}, u32[]{:S(2)}) collective-permute-start(f32[4,3,16,512]{3,2,1,0:T(8,128)S(1)} %pad_maximum_fusion.refs_3_), channel_id=1, source_target_pairs={{0,6},{1,7},{2,4},{3,5},{4,2},{5,3},{6,0},{7,1},{8,14},{9,15},{10,... | collective-permute-start | bytes 1179656 | tf_op jit(solution)/shard_map/ppermute | solution.py:648
  38.3 20.7 %collective-permute-start.9 = (f32[4,3,16,512]{3,2,1,0:T(8,128)S(1)}, f32[4,3,16,512]{3,2,1,0:T(8,128)S(1)}, u32[]{:S(2)}, u32[]{:S(2)}) collective-permute-start(f32[4,3,16,512]{3,2,1,0:T(8,128)S(1)} %pad_maximum_fusion.refs_3_), channel_id=1, source_target_pairs={{0,1},{1,0},{2,3},{3,2},{4,5},{5,4},{6,7},{7,6},{8,9},{9,8},{10,11... | collective-permute-start | bytes 1179656 | tf_op jit(solution)/shard_map/ppermute | solution.py:648
  38.4 21.8 %collective-permute-start.11 = (f32[4,3,16,512]{3,2,1,0:T(8,128)S(1)}, f32[4,3,16,512]{3,2,1,0:T(8,128)S(1)}, u32[]{:S(2)}, u32[]{:S(2)}) collective-permute-start(f32[4,3,16,512]{3,2,1,0:T(8,128)S(1)} %collective-permute-done.10.refs_5_), channel_id=1, source_target_pairs={{0,1},{1,0},{2,3},{3,2},{4,5},{5,4},{6,7},{7,6},{8,9},{9,8},{10,11... | collective-permute-start | bytes 1179656 | tf_op jit(solution)/shard_map/ppermute | solution.py:648
  39.3 18.8 %collective-permute-start.20 = (f32[48,512]{1,0:T(8,128)S(1)}, f32[48,512]{1,0:T(8,128)S(1)}, u32[]{:S(2)}, u32[]{:S(2)}) collective-permute-start(f32[48,512]{1,0:T(8,128)S(1)} %get-tuple-element.127), channel_id=1, source_target_pairs={{0,8},{8,0},{16,24},{24,16},{1,9},{9,1},{17,25},{25,17},{2,10},{10... | collective-permute-start | bytes 294920 | tf_op jit(solution)/shard_map/ppermute | solution.py:648
  39.3 19.0 %collective-permute-start.21 = (f32[48,512]{1,0:T(8,128)S(1)}, f32[48,512]{1,0:T(8,128)S(1)}, u32[]{:S(2)}, u32[]{:S(2)}) collective-permute-start(f32[48,512]{1,0:T(8,128)S(1)} %get-tuple-element.127), channel_id=1, source_target_pairs={{0,16},{8,24},{16,0},{24,8},{1,17},{9,25},{17,1},{25,9},{2,18},{10... | collective-permute-start | bytes 294920 | tf_op jit(solution)/shard_map/ppermute | solution.py:648
  41.1 17.5 %collective-permute-start.22 = (f32[48,512]{1,0:T(8,128)S(1)}, f32[48,512]{1,0:T(8,128)S(1)}, u32[]{:S(2)}, u32[]{:S(2)}) collective-permute-start(f32[48,512]{1,0:T(8,128)S(1)} %get-tuple-element.127), channel_id=1, source_target_pairs={{0,24},{8,16},{16,8},{24,0},{1,25},{9,17},{17,9},{25,1},{2,26},{10... | collective-permute-start | bytes 294920 | tf_op jit(solution)/shard_map/ppermute | solution.py:648
  58.7 13.9 %collective-permute-start.23 = (f32[3,3,16,512]{3,2,1,0:T(8,128)S(1)}, f32[3,3,16,512]{3,2,1,0:T(8,128)S(1)}, u32[]{:S(2)}, u32[]{:S(2)}) collective-permute-start(f32[3,3,16,512]{3,2,1,0:T(8,128)S(1)} %pad_maximum_fusion.1.refs_3_), channel_id=1, source_target_pairs={{0,2},{1,3},{2,0},{3,1},{4,6},{5,7},{6,4},{7,5},{8,10},{9,11},{10,... | collective-permute-start | bytes 884744 | tf_op jit(solution)/shard_map/ppermute | solution.py:648
  59.0 13.6 %collective-permute-start.24 = (f32[3,3,16,512]{3,2,1,0:T(8,128)S(1)}, f32[3,3,16,512]{3,2,1,0:T(8,128)S(1)}, u32[]{:S(2)}, u32[]{:S(2)}) collective-permute-start(f32[3,3,16,512]{3,2,1,0:T(8,128)S(1)} %pad_maximum_fusion.1.refs_3_), channel_id=1, source_target_pairs={{0,4},{1,5},{2,6},{3,7},{4,0},{5,1},{6,2},{7,3},{8,12},{9,13},{10,... | collective-permute-start | bytes 884744 | tf_op jit(solution)/shard_map/ppermute | solution.py:648
  60.2 13.3 %collective-permute-start.25 = (f32[3,3,16,512]{3,2,1,0:T(8,128)S(1)}, f32[3,3,16,512]{3,2,1,0:T(8,128)S(1)}, u32[]{:S(2)}, u32[]{:S(2)}) collective-permute-start(f32[3,3,16,512]{3,2,1,0:T(8,128)S(1)} %pad_maximum_fusion.1.refs_3_), channel_id=1, source_target_pairs={{0,6},{1,7},{2,4},{3,5},{4,2},{5,3},{6,0},{7,1},{8,14},{9,15},{10,... | collective-permute-start | bytes 884744 | tf_op jit(solution)/shard_map/ppermute | solution.py:648
  112.8 19.8 %collective-permute-start.31 = (f32[4,48,512]{2,1,0:T(8,128)S(1)}, f32[4,48,512]{2,1,0:T(8,128)S(1)}, u32[]{:S(2)}, u32[]{:S(2)}) collective-permute-start(f32[4,48,512]{2,1,0:T(8,128)S(1)} %get-tuple-element.172), channel_id=1, source_target_pairs={{0,2},{1,3},{2,0},{3,1},{4,6},{5,7},{6,4},{7,5},{8,10},{9,11},{10,... | collective-permute-start | bytes 1179656 | tf_op jit(solution)/shard_map/ppermute | solution.py:648
  114.1 18.6 %collective-permute-start.32 = (f32[4,48,512]{2,1,0:T(8,128)S(1)}, f32[4,48,512]{2,1,0:T(8,128)S(1)}, u32[]{:S(2)}, u32[]{:S(2)}) collective-permute-start(f32[4,48,512]{2,1,0:T(8,128)S(1)} %get-tuple-element.173), channel_id=1, source_target_pairs={{0,4},{1,5},{2,6},{3,7},{4,0},{5,1},{6,2},{7,3},{8,12},{9,13},{10,... | collective-permute-start | bytes 1179656 | tf_op jit(solution)/shard_map/ppermute | solution.py:648
  114.4 18.5 %collective-permute-start.33 = (f32[4,48,512]{2,1,0:T(8,128)S(1)}, f32[4,48,512]{2,1,0:T(8,128)S(1)}, u32[]{:S(2)}, u32[]{:S(2)}) collective-permute-start(f32[4,48,512]{2,1,0:T(8,128)S(1)} %get-tuple-element.174), channel_id=1, source_target_pairs={{0,6},{1,7},{2,4},{3,5},{4,2},{5,3},{6,0},{7,1},{8,14},{9,15},{10,... | collective-permute-start | bytes 1179656 | tf_op jit(solution)/shard_map/ppermute | solution.py:648
  133.0 15.1 %collective-permute-start.37 = (f32[4,4,64,512]{3,2,1,0:T(8,128)S(1)}, f32[4,4,64,512]{3,2,1,0:T(8,128)S(1)}, u32[]{:S(2)}, u32[]{:S(2)}) collective-permute-start(f32[4,4,64,512]{3,2,1,0:T(8,128)S(1)} %get-tuple-element.181), channel_id=1, source_target_pairs={{0,1},{1,0},{2,3},{3,2},{4,5},{5,4},{6,7},{7,6},{8,9},{9,8},{10,11... | collective-permute-start | bytes 6291464 | tf_op jit(solution)/shard_map/ppermute | solution.py:648
  134.3 13.8 %collective-permute-start.34 = (f32[48,512]{1,0:T(8,128)S(1)}, f32[48,512]{1,0:T(8,128)S(1)}, u32[]{:S(2)}, u32[]{:S(2)}) collective-permute-start(f32[48,512]{1,0:T(8,128)S(1)} %get-tuple-element.177), channel_id=1, source_target_pairs={{0,8},{8,0},{16,24},{24,16},{1,9},{9,1},{17,25},{25,17},{2,10},{10... | collective-permute-start | bytes 294920 | tf_op jit(solution)/shard_map/ppermute | solution.py:648
  150.1 22.8 %collective-permute-start.41 = (f32[4,64,512]{2,1,0:T(8,128)S(1)}, f32[4,64,512]{2,1,0:T(8,128)S(1)}, u32[]{:S(2)}, u32[]{:S(2)}) collective-permute-start(f32[4,64,512]{2,1,0:T(8,128)S(1)} %get-tuple-element.196), channel_id=1, source_target_pairs={{0,6},{1,7},{2,4},{3,5},{4,2},{5,3},{6,0},{7,1},{8,14},{9,15},{10,... | collective-permute-start | bytes 1572872 | tf_op jit(solution)/shard_map/ppermute | solution.py:648
  158.7 14.4 %collective-permute-start.38 = (f32[4,72,512]{2,1,0:T(8,128)S(1)}, f32[4,72,512]{2,1,0:T(8,128)S(1)}, u32[]{:S(2)}, u32[]{:S(2)}) collective-permute-start(f32[4,72,512]{2,1,0:T(8,128)S(1)} %get-tuple-element.192), channel_id=1, source_target_pairs={{0,1},{1,0},{2,3},{3,2},{4,5},{5,4},{6,7},{7,6},{8,9},{9,8},{10,11... | collective-permute-start | bytes 1769480 | tf_op jit(solution)/shard_map/ppermute | solution.py:648
  176.8 13.1 %collective-permute-start.44 = (f32[64,512]{1,0:T(8,128)S(1)}, f32[64,512]{1,0:T(8,128)S(1)}, u32[]{:S(2)}, u32[]{:S(2)}) collective-permute-start(f32[64,512]{1,0:T(8,128)S(1)} %get-tuple-element.200), channel_id=1, source_target_pairs={{0,24},{8,16},{16,8},{24,0},{1,25},{9,17},{17,9},{25,1},{2,26},{10... | collective-permute-start | bytes 393224 | tf_op jit(solution)/shard_map/ppermute | solution.py:648
  180.2 16.5 %collective-permute-start.53 = (f32[72,512]{1,0:T(8,128)S(1)}, f32[72,512]{1,0:T(8,128)S(1)}, u32[]{:S(2)}, u32[]{:S(2)}) collective-permute-start(f32[72,512]{1,0:T(8,128)S(1)} %get-tuple-element.230), channel_id=1, source_target_pairs={{0,16},{8,24},{16,0},{24,8},{1,17},{9,25},{17,1},{25,9},{2,18},{10... | collective-permute-start | bytes 442376 | tf_op jit(solution)/shard_map/ppermute | solution.py:648
  180.3 21.3 %collective-permute-start.54 = (f32[72,512]{1,0:T(8,128)S(1)}, f32[72,512]{1,0:T(8,128)S(1)}, u32[]{:S(2)}, u32[]{:S(2)}) collective-permute-start(f32[72,512]{1,0:T(8,128)S(1)} %get-tuple-element.229), channel_id=1, source_target_pairs={{0,24},{8,16},{16,8},{24,0},{1,25},{9,17},{17,9},{25,1},{2,26},{10... | collective-permute-start | bytes 442376 | tf_op jit(solution)/shard_map/ppermute | solution.py:648
  202.6 19.9 %collective-permute-start.46 = (f32[112,512]{1,0:T(8,128)S(1)}, f32[112,512]{1,0:T(8,128)S(1)}, u32[]{:S(2)}, u32[]{:S(2)}) collective-permute-start(f32[112,512]{1,0:T(8,128)S(1)} %pad_maximum_fusion.2.refs_0_), channel_id=1, source_target_pairs={{0,2},{1,3},{2,0},{3,1},{4,6},{5,7},{6,4},{7,5},{8,10},{9,11},{10,... | collective-permute-start | bytes 688136 | tf_op jit(solution)/shard_map/ppermute | solution.py:648
  203.3 19.3 %collective-permute-start.48 = (f32[112,512]{1,0:T(8,128)S(1)}, f32[112,512]{1,0:T(8,128)S(1)}, u32[]{:S(2)}, u32[]{:S(2)}) collective-permute-start(f32[112,512]{1,0:T(8,128)S(1)} %pad_maximum_fusion.2.refs_0_), channel_id=1, source_target_pairs={{0,4},{1,5},{2,6},{3,7},{4,0},{5,1},{6,2},{7,3},{8,12},{9,13},{10,... | collective-permute-start | bytes 688136 | tf_op jit(solution)/shard_map/ppermute | solution.py:648
  204.1 18.9 %collective-permute-start.50 = (f32[112,512]{1,0:T(8,128)S(1)}, f32[112,512]{1,0:T(8,128)S(1)}, u32[]{:S(2)}, u32[]{:S(2)}) collective-permute-start(f32[112,512]{1,0:T(8,128)S(1)} %pad_maximum_fusion.2.refs_0_), channel_id=1, source_target_pairs={{0,6},{1,7},{2,4},{3,5},{4,2},{5,3},{6,0},{7,1},{8,14},{9,15},{10,... | collective-permute-start | bytes 688136 | tf_op jit(solution)/shard_map/ppermute | solution.py:648
  205.9 17.2 %collective-permute-start.57 = (f32[72,512]{1,0:T(8,128)S(1)}, f32[72,512]{1,0:T(8,128)S(1)}, u32[]{:S(2)}, u32[]{:S(2)}) collective-permute-start(f32[72,512]{1,0:T(8,128)S(1)} %add_add_fusion.1), channel_id=1, source_target_pairs={{0,6},{1,7},{2,4},{3,5},{4,2},{5,3},{6,0},{7,1},{8,14},{9,15},{10,... | collective-permute-start | bytes 442376 | tf_op jit(solution)/shard_map/ppermute | solution.py:648
  (61 other events, 601.9 us)

commit v3 on v2

--- a/solution.py
+++ b/solution.py
@@ -20,7 +20,7 @@
 GAIN, BIAS, SKIP, BIAS_V, BIAS_G, GAMMA, LAM, LAM1, LAM2, LAM4, LAM8, RATES = range(12)
 
 
-CHUNKS = (((0, 0),), ((0, 1), (0, 2), (0, 3), (1, 0)), ((1, 1), (1, 2), (1, 3)))
+CHUNKS = (((0, 0), (1, 0)), ((0, 1), (0, 2), (0, 3)), ((1, 1), (1, 2), (1, 3)))
 
 
 class Dims:
@@ -69,6 +69,18 @@
         return fn(j, rows, carry)
 
     return lax.fori_loop(0, dim.L, one, init, unroll=unroll)
+
+
+def each_span(dim, fn, init=0, steps=8):
+    def one(i, carry):
+        rows = pl.ds(pl.multiple_of(i * steps * dim.R, steps * dim.R), steps * dim.R)
+        return fn([i * steps + u for u in range(steps)], rows, carry)
+
+    return lax.fori_loop(0, dim.L // steps, one, init)
+
+
+def fold(x):
+    return jnp.sum(x.reshape(x.shape[0] // 8, 8, x.shape[1]), 0)
 
 
 def row(table, index, n=1):
@@ -154,14 +166,14 @@
 
 
 def front(dim, load_act, table, w_in, xhat, rstd, drive, cf, fin, ah, al, wh, wl):
-    def norm(j, rows, _):
-        xh, rs, normed = norm_step(dim, load_act(j, rows), table)
+    def norm(steps, rows, _):
+        xh, rs, normed = norm_step(dim, load_act(steps, rows), table)
         xhat[rows, :] = xh
-        rstd[rows, :] = jnp.broadcast_to(rs, (dim.R, 128))
+        rstd[rows, :] = jnp.broadcast_to(rs, (rs.shape[0], 128))
         ah[rows, :], al[rows, :] = split(normed)
         return 0
 
-    each_step(dim, norm, 4)
+    each_span(dim, norm)
     w_in.fill(wh, wl)
     product(ah, al, wh, wl, drive)
 
@@ -206,7 +218,7 @@
         ah[rows, :], al[rows, :] = split(a)
         return 0
 
-    each_step(dim, gelu, 2)
+    each_step(dim, gelu, 4)
     w_gv.fill(wh, wl)
     product(ah, al, wh, wl, v)
     w_gg.fill(wh, wl)
@@ -296,18 +308,18 @@
 
     w_in.fill(wh, wl)
     product(ah, al, wh, wl, buf, True)
-    wide = jnp.zeros((dim.R, dim.H), F32)
-
-    def dnorm(j, rows, carry):
+    wide = jnp.zeros((8, dim.H), F32)
+
+    def dnorm(steps, rows, carry):
         dn = buf[rows, :] + dmixed[rows, :] * row(table, SKIP)
         xh = xhat[rows, :]
         dx = dn * row(table, GAIN)
         m1 = jnp.mean(dx, -1, keepdims=True)
         m2 = jnp.mean(dx * xh, -1, keepdims=True)
-        store(j, rows, load_dact(j, rows) + rstd[rows, 0:1] * (dx - m1 - xh * m2))
-        return carry[0] + dn * xh, carry[1] + dn
-
-    sgain, sbias = each_step(dim, dnorm, 2, False, (wide, wide))
+        store(steps, rows, load_dact(steps, rows) + rstd[rows, 0:1] * (dx - m1 - xh * m2))
+        return carry[0] + fold(dn * xh), carry[1] + fold(dn)
+
+    sgain, sbias = each_span(dim, dnorm, (wide, wide))
     sums[GAIN : GAIN + 1, :] = jnp.sum(sgain, 0, keepdims=True)
     sums[BIAS : BIAS + 1, :] = jnp.sum(sbias, 0, keepdims=True)
 
@@ -432,7 +444,7 @@
 
 
 def pack_kernel(dim, in_map, out_map, glu, gain, bias, skip, nu, theta, gamma, glu_bias, *refs):
-    outs, held, sem = refs[:3], refs[3:-1], refs[-1]
+    outs, held, sem = refs[:2], refs[2:-1], refs[-1]
     vectors = (gain, bias, skip, nu, theta, gamma, glu_bias)
     me, my = lax.axis_index("seq"), lax.axis_index("dp")
     start = pl.multiple_of(jnp.minimum(me, dim.used - 1) * dim.q, 16)
@@ -440,7 +452,7 @@
     for src, dst in zip(vectors, held):
         moves.append(pltpu.make_async_copy(src, dst, sem.at[len(moves)]))
     gain, bias, skip, nu, theta, gamma, glu_bias = held
-    for out, chunk in zip(outs, CHUNKS):
+    for out, chunk in zip(outs, (CHUNKS[0], CHUNKS[1] + CHUNKS[2])):
         head = out.shape[0] - len(chunk) * dim.q
         for i, name in enumerate(chunk):
             src = shard_of((in_map, out_map, glu), name, pl.ds(start, dim.q), dim.H)
@@ -519,15 +531,17 @@
         lax.fori_loop(0, dim.S, one, 0)
 
 
-def weights_in(dim, chunk, names, fn):
-    first = 3 + dim.S
+def weights_in(dim, chunks, names, fn):
+    first = 3 + len(chunks) * dim.S
 
     def kernel(*refs):
         spare = refs[len(refs) - 3 * len(names) :]
-        weights = [
-            Weight(dim, name, CHUNKS[chunk].index(name), refs[:first], *spare[3 * i : 3 * i + 3])
-            for i, name in enumerate(names)
-        ]
+        weights = []
+        for i, name in enumerate(names):
+            (n,) = [n for n, c in enumerate(chunks) if name in CHUNKS[c]]
+            sources = refs[:3] + refs[3 + n * dim.S : 3 + (n + 1) * dim.S]
+            place = CHUNKS[chunks[n]].index(name)
+            weights.append(Weight(dim, name, place, sources, *spare[3 * i : 3 * i + 3]))
         for w in weights:
             w.start()
         fn(dim, weights, *refs[first : len(refs) - 3 * len(names)])
@@ -541,7 +555,12 @@
 
 
 def strided(dim, ref):
-    return lambda j, rows: ref[:, j, :]
+    def load(steps, rows):
+        if isinstance(steps, list):
+            return jnp.concatenate([ref[:, j, :] for j in steps], 0)
+        return ref[:, steps, :]
+
+    return load
 
 
 def plain(ref):
@@ -558,8 +577,8 @@
     back(dim, t, drive, cf, g, xhat, w_out, w_gv, w_gg, en, states, mixed, active, v, s, ah, al, wh, wl)
     load = strided(dim, x)
 
-    def residual(j, rows):
-        act = load(j, rows) + gate(dim, t, v, s, rows)
+    def residual(steps, rows):
+        act = load(steps, rows) + gate(dim, t, v, s, rows)
         act1[rows, :] = act
         return act
 
@@ -615,8 +634,9 @@
 
 def k_c0(share, dim, weights, t, ds, rcf, gr, states, en, drive, xhat, rstd, dmixed, dmid, sums1a, sums1b, sums0a,
          input_grad, keep, send, ah, al, bh, bl, wh, wl, adj_en, dproj, buf, sums0, tile):
-    def store(j, rows, value):
-        input_grad[:, j, :] = value
+    def store(steps, rows, value):
+        for u, j in enumerate(steps):
+            input_grad[:, j, :] = value[u * dim.R : (u + 1) * dim.R, :]
 
     bottom(dim, t, ds, rcf, gr, states, en, drive, xhat, rstd, dmixed, weights[0], plain(dmid), store, dproj, buf, adj_en,
            sums0, ah, al, wh, wl)
@@ -757,11 +777,12 @@
     x = inputs.reshape(R, dim.L, H)
     og = out_grad.reshape(R, dim.L, H)
 
-    heads = [SMALL, SMALL, 0]
+    heads = [SMALL, SMALL]
+    sends = [CHUNKS[0], CHUNKS[1] + CHUNKS[2]]
     vectors = (ln_gain, ln_bias, skip_gain, nu_log, theta_log, gamma_log, glu_bias)
     messages = call(
         functools.partial(pack_kernel, dim),
-        [f32(head + len(chunk) * dim.q, H) for head, chunk in zip(heads, CHUNKS)],
+        [f32(head + len(chunk) * dim.q, H) for head, chunk in zip(heads, sends)],
         [pltpu.VMEM(v.shape, F32) for v in vectors] + [pltpu.SemaphoreType.DMA((len(vectors) + sum(map(len, CHUNKS)),))],
         in_map, out_map, glu_weight, *vectors,
         anywhere=3 + len(vectors),
@@ -778,41 +799,41 @@
             total = total + other[:head]
         return call(functools.partial(prep_kernel, dim), [f32(TABLE, H)], [], total)[0]
 
-    mine0, mine1, mine2 = messages
+    mine0, mine1 = messages
     others0 = along_dp(mine0)
     table0 = table_of(mine0, others0)
     mine1, others0 = tie(mine1, others0)
     others1 = along_dp(mine1)
     table1 = table_of(mine1, others1)
     chips0 = chips_gather(dim, stacked(others0, SMALL))
-    joined1, chips0 = tie(stacked(others1, SMALL), chips0)
+    cut = SMALL + len(CHUNKS[1]) * dim.q
+    joined1, chips0 = tie(stacked([o[:cut] for o in others1], SMALL), chips0)
+    joined2 = stacked(others1, cut)
     pieces0 = cores_gather(chips0)
     chips1 = chips_gather(dim, joined1)
-    mine2, (chips1[1],) = tie(mine2, [chips1[1]])
-    joined2 = stacked(along_dp(mine2), 0)
     pieces = [pieces0, cores_gather(chips1), None]
 
     big, ent, fins = pltpu.VMEM((T, H), F32), pltpu.VMEM((R, H), F32), f32(B, H)
     stat = pltpu.VMEM((T, 128), F32)
     vec = pltpu.VMEM((SMALL, H), F32)
 
-    def k(fn, chunk, names, outs, scratch, *args, us):
-        kernel, count, own = weights_in(dim, chunk, names, fn)
-        sources = [in_map, out_map, glu_weight] + pieces[chunk]
+    def k(fn, names, outs, scratch, *args, us):
+        chunks = [c for c, chunk in enumerate(CHUNKS) if set(chunk) & set(names)]
+        kernel, count, own = weights_in(dim, chunks, names, fn)
+        sources = [in_map, out_map, glu_weight] + [p for c in chunks for p in pieces[c]]
         return call(kernel, outs, scratch + own, *sources, *args, us=us, anywhere=count)
 
     def carried(fin):
         return lax.all_gather(fin, "seq")
 
     xhat0, rstd0, drive0, cf0, fin0 = k(
-        k_a0, 0, [(0, 0)], [big, stat, big, ent, fins], halves(dim, 1), x, table0, us=3.4
+        k_a0, [(0, 0)], [big, stat, big, ent, fins], halves(dim, 1), x, table0, us=3.4
     )
     g0 = carried(fin0)
     joined2, (g0,) = tie(joined2, [g0])
     chips2 = chips_gather(dim, joined2)
     en0, states0, mixed0, active0, v0, s0, act1, xhat1, rstd1, drive1, cf1, fin1 = k(
         k_b0,
-        1,
         [(0, 1), (0, 2), (0, 3), (1, 0)],
         [ent, big, big, big, big, big, big, big, stat, big, ent, fins],
         halves(dim, 1),
@@ -825,7 +846,6 @@
     spare = [pltpu.VMEM((T, H), F32)]
     out, en1, states1, active1, dv1, dg1, dmixed1, ds1, rcf1, rfin1, sums1a = k(
         k_b1,
-        2,
         [(1, 1), (1, 2), (1, 3)],
         [f32(R, dim.L, H), ent, big, big, big, big, big, big, ent, fins, vec],
         halves(dim, 2) + spare * 3,
@@ -844,7 +864,6 @@
     gr1, half1 = tie(gr1, half_sums(dim, keep1, send1))
     dproj1, dmid, dv0, dg0, dmixed0, ds0, rcf0, rfin0, sums1b, sums0a = k(
         k_c1,
-        1,
         [(1, 0), (0, 2), (0, 3), (0, 1)],
         [big, big, big, big, big, big, ent, fins, vec, vec],
         halves(dim, 2) + [pltpu.VMEM((R, H), F32)],
@@ -862,7 +881,6 @@
     gr0, (upper1, *half2) = tie(gr0, [upper1, *half_sums(dim, keep2, send2)])
     input_grad, keep3, send3 = k(
         functools.partial(k_c0, share3),
-        0,
         [(0, 0)],
         [f32(R, dim.L, H)] + [f32(*share3.shape)] * 2,
         halves(dim, 2) + [pltpu.VMEM((R, H), F32)] + spare * 2 + [pltpu.VMEM((SMALL, H), F32)] + tile,
@@ -872,11 +890,11 @@
     sums2 = plane_sums(dim, half2)
     got3 = swap(send3, "seq", 1)
     half3 = [keep3[d] + got3[d] for d in range(D)]
-    half3[0], sums2 = tie(half3[0], sums2)
     total3 = tree_sum([half3[0]] + [swap(half3[k], "dp", k) for k in range(1, D)])
     mine3 = tree_sum(chips_gather(dim, total3))
+    joint, (mine3,) = tie(jnp.concatenate([upper1, dp_sum(dim, sums2)], 0), [mine3])
+    upper = plane_gather(dim, joint)
     other3 = swap(mine3, "seq", 1)
-    upper = plane_gather(dim, jnp.concatenate([upper1, dp_sum(dim, sums2)], 0))
     kinds = [[(1, "gv"), (1, "gg"), (1, "out")], [(0, "gv"), (0, "gg"), (0, "out"), (1, "in")]]
     grads = unpack(dim, (share1, share2), kinds, share3, upper, mine3, other3)
     return (out.reshape(inputs.shape), input_grad.reshape(inputs.shape), *grads)

time: 227 us -> 209 us (0.921)
  starting transfers between devices: 70.2 us -> 59.3 us
  Pallas kernels: 59.6 us -> 56.2 us
  blocking collectives: 39.3 us -> 36.5 us
    ppermute x59 -> x56, starting transfers between devices: 70.2 us -> 59.3 us  [swap(): return lax.ppermute(x, axis, [(i, i ^ mask) for i in range(count)])]
    pallas_call x11, Pallas kernels: 59.6 us -> 56.2 us  [call(): pl.pallas_call(fn, out_shape=outs, in_specs=[pl.BlockSpec(memory_space=sp...]
    all_gather x4, blocking collectives: 39.3 us -> 36.5 us  [carried(): return lax.all_gather(fin, 'seq')]
    ppermute x59 -> x56, waiting for transfers between devices: 53 us -> 51.5 us  [swap(): return lax.ppermute(x, axis, [(i, i ^ mask) for i in range(count)])]
  transfers between devices with their start and end apart: 59 -> 56, of which waited for: 20 -> 12; matrix products, arithmetic and copies ran while one was open for 0% -> 0% of each run, Pallas kernels for 17% -> 14%
where the time goes in v3:
time: 209 us
  starting transfers between devices  59.3 us (28%)
  Pallas kernels  56.2 us (27%)
  waiting for transfers between devices  51.5 us (25%)
  blocking collectives  36.5 us (17%)
  local copies, waits for them, and re-layouts  2.48 us (1%)
    ppermute x56, starting transfers between devices, swap(): return lax.ppermute(x, axis, [(i, i ^ mask) for i in range(count)])  59.3 us
    pallas_call x11, Pallas kernels, call(): pl.pallas_call(fn, out_shape=outs, in_specs=[pl.BlockSpec(memory_space=sp...  56.2 us
    ppermute x56, waiting for transfers between devices, swap(): return lax.ppermute(x, axis, [(i, i ^ mask) for i in range(count)])  51.5 us
    all_gather x4, blocking collectives, carried(): return lax.all_gather(fin, 'seq')  36.5 us
  transfers between devices with their start and end apart: 56, of which 12 were waited for; matrix products, arithmetic and copies ran while one was open for 0% of the time, Pallas kernels for 14%

profile of v3, /device:TPU:9, one launch (start us, length us, event | category | flops | bytes accessed | tf_op | source)
XLA Modules:
  0.0 208.8 jit_solution(6585356036621003333)
XLA Ops:
  7.6 3.9 %collective-permute-done.2 = f32[40,512]{1,0:T(8,128)S(1)} collective-permute-done((f32[40,512]{1,0:T(8,128)S(1)}, f32[40,512]{1,0:T(8,128)S(1)}, u32[]{:S(2)}, u32[]{:S(2)}) %collective-permute-start.2) | collective-permute-done | bytes 81952 | tf_op jit(solution)/shard_map/ppermute | solution.py:668
  18.7 2.7 %collective-permute-done.4 = f32[104,512]{1,0:T(8,128)S(1)} collective-permute-done((f32[104,512]{1,0:T(8,128)S(1)}, f32[104,512]{1,0:T(8,128)S(1)}, u32[]{:S(2)}, u32[]{:S(2)}) %collective-permute-start.4) | collective-permute-done | bytes 213024 | tf_op jit(solution)/shard_map/ppermute | solution.py:668
  21.5 10.0 %collective-permute-done.5 = f32[104,512]{1,0:T(8,128)S(1)} collective-permute-done((f32[104,512]{1,0:T(8,128)S(1)}, f32[104,512]{1,0:T(8,128)S(1)}, u32[]{:S(2)}, u32[]{:S(2)}) %collective-permute-start.5) | collective-permute-done | bytes 213024 | tf_op jit(solution)/shard_map/ppermute | solution.py:668
  32.9 2.8 %collective-permute-start.10 = (f32[2,3,16,512]{3,2,1,0:T(8,128)S(1)}, f32[2,3,16,512]{3,2,1,0:T(8,128)S(1)}, u32[]{:S(2)}, u32[]{:S(2)}) collective-permute-start(f32[2,3,16,512]{3,2,1,0:T(8,128)S(1)} %collective-permute-done.6.refs_5_), channel_id=1, source_target_pairs={{0,1},{1,0},{2,3},{3,2},{4,5},{5,4},{6,7},{7,6},{8,9},{9,8},{10,11... | collective-permute-start | bytes 589832 | tf_op jit(solution)/shard_map/ppermute | solution.py:668
  38.8 2.5 %collective-permute-start.15 = (f32[3,3,16,512]{3,2,1,0:T(8,128)S(1)}, f32[3,3,16,512]{3,2,1,0:T(8,128)S(1)}, u32[]{:S(2)}, u32[]{:S(2)}) collective-permute-start(f32[3,3,16,512]{3,2,1,0:T(8,128)S(1)} %collective-permute-done.14.refs_13_), channel_id=1, source_target_pairs={{0,1},{1,0},{2,3},{3,2},{4,5},{5,4},{6,7},{7,6},{8,9},{9,8},{10,11... | collective-permute-start | bytes 884744 | tf_op jit(solution)/shard_map/ppermute | solution.py:668
  42.2 2.8 %shard_map.214 = (f32[512,512]{1,0:T(8,128)S(1)}, f32[512,128]{1,0:T(8,128)S(1)}, f32[512,512]{1,0:T(8,128)S(1)}, f32[16,512]{1,0:T(8,128)S(1)}, f32[2,512]{1,0:T(2,128)S(1)}) custom-call(f32[2,128,512]{2,1,0:T(8,128)} %refs_0_.9, f32[2,128,512]{2,1,0:T(8,128)} %refs_1_.9, f32[2,128,1024]{2,1,0:T(8,128)} %refs_2_.9, f32[2,3,16,512]{3,2,1,0:T(8,128)} %copy-done.2, ...), custom_call_target="tpu_custom_call" | custom-call | flops 1 | bytes 12240000 | tf_op jit(solution)/shard_map/pallas_call | solution.py:395
  45.0 10.1 %all-gather.4.refs_24_ = f32[8,2,512]{2,1,0:T(2,128)S(1)} all-gather(f32[1,2,512]{2,1,0:T(2,128)S(1)} %bitcast.74), channel_id=2, replica_groups=mesh['dp'=4,'seq'=8] {'seq'}, dimensions={0}, use_global_device_ids=true | all-gather | bytes 36864 | tf_op jit(solution)/shard_map/all_gather | solution.py:827
  59.3 9.3 %shard_map.215 = (f32[16,512]{1,0:T(8,128)S(1)}, f32[512,512]{1,0:T(8,128)S(1)}, f32[512,512]{1,0:T(8,128)S(1)}, f32[512,512]{1,0:T(8,128)S(1)}, f32[512,512]{1,...) custom-call(f32[2,128,512]{2,1,0:T(8,128)} %refs_0_.9, ...), custom_call_target="tpu_custom_call" | custom-call | flops 1 | bytes 36000000 | tf_op jit(solution)/shard_map/pallas_call | solution.py:395
  68.6 2.9 %collective-permute-done.22.refs_9_ = f32[3,3,16,512]{3,2,1,0:T(8,128)S(1)} collective-permute-done((f32[3,3,16,512]{3,2,1,0:T(8,128)S(1)}, f32[3,3,16,512]{3,2,1,0:T(8,128)S(1)}, u32[]{:S(2)}, u32[]{:S(2)}) %collective-permute-start.22) | collective-permute-done | bytes 294944 | tf_op jit(solution)/shard_map/ppermute | solution.py:668
  73.4 9.2 %all-gather.5.refs_16_ = f32[8,2,512]{2,1,0:T(2,128)S(1)} all-gather(f32[1,2,512]{2,1,0:T(2,128)S(1)} %bitcast.72), channel_id=3, replica_groups=mesh['dp'=4,'seq'=8] {'seq'}, dimensions={0}, use_global_device_ids=true | all-gather | bytes 36864 | tf_op jit(solution)/shard_map/all_gather | solution.py:827
  83.6 13.4 %shard_map.216 = (f32[16,32,512]{2,1,0:T(8,128)}, f32[16,512]{1,0:T(8,128)S(1)}, f32[512,512]{1,0:T(8,128)S(1)}, f32[512,512]{1,0:T(8,128)S(1)}, f32[512,512]{1,...) custom-call(f32[2,128,512]{2,1,0:T(8,128)} %refs_0_.9, ...), custom_call_target="tpu_custom_call" | custom-call | flops 1 | bytes 46800000 | tf_op jit(solution)/shard_map/pallas_call | solution.py:395
  97.0 4.9 %shard_map.217 = (f32[4,4,48,512]{3,2,1,0:T(8,128)S(1)}, f32[4,4,48,512]{3,2,1,0:T(8,128)S(1)}) custom-call(f32[512,512]{1,0:T(8,128)S(1)} %get-tuple-element.137.active, f32[512,512]{1,0:T(8,128)S(1)} %get-tuple-element.138.dv, f32[512,512]{1,0:T(8,128)S(1)} %get-tuple-element.139.dg, f32[512,512]{1,0:T(8,128)S(1)} %get-tuple-element.140.states.refs_25_, ...), custom_call_target="tpu_custom_call" | custom-call | flops 1 | bytes 18000000 | tf_op jit(solution)/shard_map/pallas_call | solution.py:395
  102.1 8.3 %all-gather.6.refs_24_ = f32[8,2,512]{2,1,0:T(2,128)S(1)} all-gather(f32[1,2,512]{2,1,0:T(2,128)S(1)} %bitcast.73), channel_id=4, replica_groups=mesh['dp'=4,'seq'=8] {'seq'}, dimensions={0}, use_global_device_ids=true | all-gather | bytes 36864 | tf_op jit(solution)/shard_map/all_gather | solution.py:827
  113.5 9.9 %shard_map.218 = (f32[512,512]{1,0:T(8,128)S(1)}, f32[512,512]{1,0:T(8,128)S(1)}, f32[512,512]{1,0:T(8,128)S(1)}, f32[512,512]{1,0:T(8,128)S(1)}, f32[512,512]{1...) custom-call(f32[2,128,512]{2,1,0:T(8,128)} %refs_0_.9, ...), custom_call_target="tpu_custom_call" | custom-call | flops 1 | bytes 39600000 | tf_op jit(solution)/shard_map/pallas_call | solution.py:395
  123.4 6.4 %shard_map.219 = (f32[4,4,64,512]{3,2,1,0:T(8,128)S(1)}, f32[4,4,64,512]{3,2,1,0:T(8,128)S(1)}) custom-call(f32[512,512]{1,0:T(8,128)S(1)} %get-tuple-element.155.active, f32[512,512]{1,0:T(8,128)S(1)} %get-tuple-element.156.dv, f32[512,512]{1,0:T(8,128)S(1)} %get-tuple-element.157.dg, f32[512,512]{1,0:T(8,128)S(1)} %get-tuple-element.158.states.refs_15_, ...), custom_call_target="tpu_custom_call" | custom-call | flops 1 | bytes 23040000 | tf_op jit(solution)/shard_map/pallas_call | solution.py:395
  134.8 8.9 %all-gather.7.refs_14_ = f32[8,2,512]{2,1,0:T(2,128)S(1)} all-gather(f32[1,2,512]{2,1,0:T(2,128)S(1)} %bitcast.71), channel_id=5, replica_groups=mesh['dp'=4,'seq'=8] {'seq'}, dimensions={0}, use_global_device_ids=true | all-gather | bytes 36864 | tf_op jit(solution)/shard_map/all_gather | solution.py:827
  144.2 6.4 %shard_map.220 = (f32[16,32,512]{2,1,0:T(8,128)}, f32[4,72,512]{2,1,0:T(8,128)S(1)}, f32[4,72,512]{2,1,0:T(8,128)S(1)}) custom-call(f32[2,128,512]{2,1,0:T(8,128)} %refs_0_.9, f32[2,128,512]{2,1,0:T(8,128)} %refs_1_.9, f32[2,128,1024]{2,1,0:T(8,128)} %refs_2_.9, f32[2,3,16,512]{3,2,1,0:T(8,128)} %copy-done.2, f32[2,3,16,512]{3,2,1,0:T(8,128)} %copy-done.9, ...), custom_call_target="tpu_custom_call" | custom-call | flops 1 | bytes 26640000 | tf_op jit(solution)/shard_map/pallas_call | solution.py:395
  156.9 8.4 %collective-permute-done.35 = f32[4,64,512]{2,1,0:T(8,128)S(1)} collective-permute-done((f32[4,64,512]{2,1,0:T(8,128)S(1)}, f32[4,64,512]{2,1,0:T(8,128)S(1)}, u32[]{:S(2)}, u32[]{:S(2)}) %collective-permute-start.35) | collective-permute-done | bytes 524320 | tf_op jit(solution)/shard_map/ppermute | solution.py:668
  166.4 10.2 %collective-permute-done.37 = f32[4,64,512]{2,1,0:T(8,128)S(1)} collective-permute-done((f32[4,64,512]{2,1,0:T(8,128)S(1)}, f32[4,64,512]{2,1,0:T(8,128)S(1)}, u32[]{:S(2)}, u32[]{:S(2)}) %collective-permute-start.37) | collective-permute-done | bytes 524320 | tf_op jit(solution)/shard_map/ppermute | solution.py:668
  182.3 5.0 %collective-permute-done.39 = f32[64,512]{1,0:T(8,128)S(1)} collective-permute-done((f32[64,512]{1,0:T(8,128)S(1)}, f32[64,512]{1,0:T(8,128)S(1)}, u32[]{:S(2)}, u32[]{:S(2)}) %collective-permute-start.39) | collective-permute-done | bytes 131104 | tf_op jit(solution)/shard_map/ppermute | solution.py:668
  187.3 3.0 %collective-permute-done.40 = f32[64,512]{1,0:T(8,128)S(1)} collective-permute-done((f32[64,512]{1,0:T(8,128)S(1)}, f32[64,512]{1,0:T(8,128)S(1)}, u32[]{:S(2)}, u32[]{:S(2)}) %collective-permute-start.40) | collective-permute-done | bytes 131104 | tf_op jit(solution)/shard_map/ppermute | solution.py:668
  193.4 2.7 %collective-permute-start.48 = (f32[112,512]{1,0:T(8,128)S(1)}, f32[112,512]{1,0:T(8,128)S(1)}, u32[]{:S(2)}, u32[]{:S(2)}) collective-permute-start(f32[112,512]{1,0:T(8,128)S(1)} %pad_maximum_fusion.2.refs_0_), channel_id=1, source_target_pairs={{0,1},{1,0},{2,3},{3,2},{4,5},{5,4},{6,7},{7,6},{8,9},{9,8},{10,11... | collective-permute-start | bytes 688136 | tf_op jit(solution)/shard_map/ppermute | solution.py:668
  196.1 4.8 %collective-permute-start.50 = (f32[112,512]{1,0:T(8,128)S(1)}, f32[112,512]{1,0:T(8,128)S(1)}, u32[]{:S(2)}, u32[]{:S(2)}) collective-permute-start(f32[112,512]{1,0:T(8,128)S(1)} %collective-permute-done.49.refs_2_), channel_id=1, source_target_pairs={{0,1},{1,0},{2,3},{3,2},{4,5},{5,4},{6,7},{7,6},{8,9},{9,8},{10,11... | collective-permute-start | bytes 688136 | tf_op jit(solution)/shard_map/ppermute | solution.py:668
  200.9 4.1 %collective-permute-start.52 = (f32[112,512]{1,0:T(8,128)S(1)}, f32[112,512]{1,0:T(8,128)S(1)}, u32[]{:S(2)}, u32[]{:S(2)}) collective-permute-start(f32[112,512]{1,0:T(8,128)S(1)} %collective-permute-done.51.refs_4_), channel_id=1, source_target_pairs={{0,1},{1,0},{2,3},{3,2},{4,5},{5,4},{6,7},{7,6},{8,9},{9,8},{10,11... | collective-permute-start | bytes 688136 | tf_op jit(solution)/shard_map/ppermute | solution.py:668
  (176 shorter events, 54.9 us)
Async XLA Ops:
  13.8 17.8 %collective-permute-start.5 = (f32[104,512]{1,0:T(8,128)S(1)}, f32[104,512]{1,0:T(8,128)S(1)}, u32[]{:S(2)}, u32[]{:S(2)}) collective-permute-start(f32[104,512]{1,0:T(8,128)S(1)} %get-tuple-element.108), channel_id=1, source_target_pairs={{0,24},{8,16},{16,8},{24,0},{1,25},{9,17},{17,9},{25,1},{2,26},{10... | collective-permute-start | bytes 638984 | tf_op jit(solution)/shard_map/ppermute | solution.py:668
  14.2 17.4 %collective-permute-start.6 = (f32[2,3,16,512]{3,2,1,0:T(8,128)S(1)}, f32[2,3,16,512]{3,2,1,0:T(8,128)S(1)}, u32[]{:S(2)}, u32[]{:S(2)}) collective-permute-start(f32[2,3,16,512]{3,2,1,0:T(8,128)S(1)} %pad_maximum_fusion.3.refs_3_), channel_id=1, source_target_pairs={{0,2},{1,3},{2,0},{3,1},{4,6},{5,7},{6,4},{7,5},{8,10},{9,11},{10,... | collective-permute-start | bytes 589832 | tf_op jit(solution)/shard_map/ppermute | solution.py:668
  15.5 16.1 %collective-permute-start.7 = (f32[2,3,16,512]{3,2,1,0:T(8,128)S(1)}, f32[2,3,16,512]{3,2,1,0:T(8,128)S(1)}, u32[]{:S(2)}, u32[]{:S(2)}) collective-permute-start(f32[2,3,16,512]{3,2,1,0:T(8,128)S(1)} %pad_maximum_fusion.3.refs_3_), channel_id=1, source_target_pairs={{0,4},{1,5},{2,6},{3,7},{4,0},{5,1},{6,2},{7,3},{8,12},{9,13},{10,... | collective-permute-start | bytes 589832 | tf_op jit(solution)/shard_map/ppermute | solution.py:668
  16.7 14.9 %collective-permute-start.8 = (f32[2,3,16,512]{3,2,1,0:T(8,128)S(1)}, f32[2,3,16,512]{3,2,1,0:T(8,128)S(1)}, u32[]{:S(2)}, u32[]{:S(2)}) collective-permute-start(f32[2,3,16,512]{3,2,1,0:T(8,128)S(1)} %pad_maximum_fusion.3.refs_3_), channel_id=1, source_target_pairs={{0,6},{1,7},{2,4},{3,5},{4,2},{5,3},{6,0},{7,1},{8,14},{9,15},{10,... | collective-permute-start | bytes 589832 | tf_op jit(solution)/shard_map/ppermute | solution.py:668
  36.3 18.9 %collective-permute-start.16 = (f32[3,3,16,512]{3,2,1,0:T(8,128)S(1)}, f32[3,3,16,512]{3,2,1,0:T(8,128)S(1)}, u32[]{:S(2)}, u32[]{:S(2)}) collective-permute-start(f32[3,3,16,512]{3,2,1,0:T(8,128)S(1)} %pad_maximum_fusion.refs_11_), channel_id=1, source_target_pairs={{0,4},{1,5},{2,6},{3,7},{4,0},{5,1},{6,2},{7,3},{8,12},{9,13},{10,... | collective-permute-start | bytes 884744 | tf_op jit(solution)/shard_map/ppermute | solution.py:668
  37.5 17.8 %collective-permute-start.18 = (f32[3,3,16,512]{3,2,1,0:T(8,128)S(1)}, f32[3,3,16,512]{3,2,1,0:T(8,128)S(1)}, u32[]{:S(2)}, u32[]{:S(2)}) collective-permute-start(f32[3,3,16,512]{3,2,1,0:T(8,128)S(1)} %pad_maximum_fusion.refs_11_), channel_id=1, source_target_pairs={{0,6},{1,7},{2,4},{3,5},{4,2},{5,3},{6,0},{7,1},{8,14},{9,15},{10,... | collective-permute-start | bytes 884744 | tf_op jit(solution)/shard_map/ppermute | solution.py:668
  38.0 18.9 %collective-permute-start.13 = (f32[3,3,16,512]{3,2,1,0:T(8,128)S(1)}, f32[3,3,16,512]{3,2,1,0:T(8,128)S(1)}, u32[]{:S(2)}, u32[]{:S(2)}) collective-permute-start(f32[3,3,16,512]{3,2,1,0:T(8,128)S(1)} %pad_maximum_fusion.refs_11_), channel_id=1, source_target_pairs={{0,1},{1,0},{2,3},{3,2},{4,5},{5,4},{6,7},{7,6},{8,9},{9,8},{10,11... | collective-permute-start | bytes 884744 | tf_op jit(solution)/shard_map/ppermute | solution.py:668
  38.8 19.3 %collective-permute-start.15 = (f32[3,3,16,512]{3,2,1,0:T(8,128)S(1)}, f32[3,3,16,512]{3,2,1,0:T(8,128)S(1)}, u32[]{:S(2)}, u32[]{:S(2)}) collective-permute-start(f32[3,3,16,512]{3,2,1,0:T(8,128)S(1)} %collective-permute-done.14.refs_13_), channel_id=1, source_target_pairs={{0,1},{1,0},{2,3},{3,2},{4,5},{5,4},{6,7},{7,6},{8,9},{9,8},{10,11... | collective-permute-start | bytes 884744 | tf_op jit(solution)/shard_map/ppermute | solution.py:668
  55.7 12.9 %collective-permute-start.20 = (f32[3,3,16,512]{3,2,1,0:T(8,128)S(1)}, f32[3,3,16,512]{3,2,1,0:T(8,128)S(1)}, u32[]{:S(2)}, u32[]{:S(2)}) collective-permute-start(f32[3,3,16,512]{3,2,1,0:T(8,128)S(1)} %pad_maximum_fusion.1.refs_3_), channel_id=1, source_target_pairs={{0,2},{1,3},{2,0},{3,1},{4,6},{5,7},{6,4},{7,5},{8,10},{9,11},{10,... | collective-permute-start | bytes 884744 | tf_op jit(solution)/shard_map/ppermute | solution.py:668
  57.0 11.6 %collective-permute-start.21 = (f32[3,3,16,512]{3,2,1,0:T(8,128)S(1)}, f32[3,3,16,512]{3,2,1,0:T(8,128)S(1)}, u32[]{:S(2)}, u32[]{:S(2)}) collective-permute-start(f32[3,3,16,512]{3,2,1,0:T(8,128)S(1)} %pad_maximum_fusion.1.refs_3_), channel_id=1, source_target_pairs={{0,4},{1,5},{2,6},{3,7},{4,0},{5,1},{6,2},{7,3},{8,12},{9,13},{10,... | collective-permute-start | bytes 884744 | tf_op jit(solution)/shard_map/ppermute | solution.py:668
  58.1 13.4 %collective-permute-start.22 = (f32[3,3,16,512]{3,2,1,0:T(8,128)S(1)}, f32[3,3,16,512]{3,2,1,0:T(8,128)S(1)}, u32[]{:S(2)}, u32[]{:S(2)}) collective-permute-start(f32[3,3,16,512]{3,2,1,0:T(8,128)S(1)} %pad_maximum_fusion.1.refs_3_), channel_id=1, source_target_pairs={{0,6},{1,7},{2,4},{3,5},{4,2},{5,3},{6,0},{7,1},{8,14},{9,15},{10,... | collective-permute-start | bytes 884744 | tf_op jit(solution)/shard_map/ppermute | solution.py:668
  110.8 19.0 %collective-permute-start.28 = (f32[4,48,512]{2,1,0:T(8,128)S(1)}, f32[4,48,512]{2,1,0:T(8,128)S(1)}, u32[]{:S(2)}, u32[]{:S(2)}) collective-permute-start(f32[4,48,512]{2,1,0:T(8,128)S(1)} %get-tuple-element.163), channel_id=1, source_target_pairs={{0,2},{1,3},{2,0},{3,1},{4,6},{5,7},{6,4},{7,5},{8,10},{9,11},{10,... | collective-permute-start | bytes 1179656 | tf_op jit(solution)/shard_map/ppermute | solution.py:668
  111.9 17.8 %collective-permute-start.29 = (f32[4,48,512]{2,1,0:T(8,128)S(1)}, f32[4,48,512]{2,1,0:T(8,128)S(1)}, u32[]{:S(2)}, u32[]{:S(2)}) collective-permute-start(f32[4,48,512]{2,1,0:T(8,128)S(1)} %get-tuple-element.164), channel_id=1, source_target_pairs={{0,4},{1,5},{2,6},{3,7},{4,0},{5,1},{6,2},{7,3},{8,12},{9,13},{10,... | collective-permute-start | bytes 1179656 | tf_op jit(solution)/shard_map/ppermute | solution.py:668
  112.3 18.4 %collective-permute-start.30 = (f32[4,48,512]{2,1,0:T(8,128)S(1)}, f32[4,48,512]{2,1,0:T(8,128)S(1)}, u32[]{:S(2)}, u32[]{:S(2)}) collective-permute-start(f32[4,48,512]{2,1,0:T(8,128)S(1)} %get-tuple-element.165), channel_id=1, source_target_pairs={{0,6},{1,7},{2,4},{3,5},{4,2},{5,3},{6,0},{7,1},{8,14},{9,15},{10,... | collective-permute-start | bytes 1179656 | tf_op jit(solution)/shard_map/ppermute | solution.py:668
  130.8 12.9 %collective-permute-start.34 = (f32[4,4,64,512]{3,2,1,0:T(8,128)S(1)}, f32[4,4,64,512]{3,2,1,0:T(8,128)S(1)}, u32[]{:S(2)}, u32[]{:S(2)}) collective-permute-start(f32[4,4,64,512]{3,2,1,0:T(8,128)S(1)} %get-tuple-element.172), channel_id=1, source_target_pairs={{0,1},{1,0},{2,3},{3,2},{4,5},{5,4},{6,7},{7,6},{8,9},{9,8},{10,11... | collective-permute-start | bytes 6291464 | tf_op jit(solution)/shard_map/ppermute | solution.py:668
  132.1 11.6 %collective-permute-start.31 = (f32[48,512]{1,0:T(8,128)S(1)}, f32[48,512]{1,0:T(8,128)S(1)}, u32[]{:S(2)}, u32[]{:S(2)}) collective-permute-start(f32[48,512]{1,0:T(8,128)S(1)} %get-tuple-element.168), channel_id=1, source_target_pairs={{0,8},{8,0},{16,24},{24,16},{1,9},{9,1},{17,25},{25,17},{2,10},{10... | collective-permute-start | bytes 294920 | tf_op jit(solution)/shard_map/ppermute | solution.py:668
  151.9 13.5 %collective-permute-start.35 = (f32[4,64,512]{2,1,0:T(8,128)S(1)}, f32[4,64,512]{2,1,0:T(8,128)S(1)}, u32[]{:S(2)}, u32[]{:S(2)}) collective-permute-start(f32[4,64,512]{2,1,0:T(8,128)S(1)} %get-tuple-element.183), channel_id=1, source_target_pairs={{0,2},{1,3},{2,0},{3,1},{4,6},{5,7},{6,4},{7,5},{8,10},{9,11},{10,... | collective-permute-start | bytes 1572872 | tf_op jit(solution)/shard_map/ppermute | solution.py:668
  152.2 14.2 %collective-permute-start.36 = (f32[4,64,512]{2,1,0:T(8,128)S(1)}, f32[4,64,512]{2,1,0:T(8,128)S(1)}, u32[]{:S(2)}, u32[]{:S(2)}) collective-permute-start(f32[4,64,512]{2,1,0:T(8,128)S(1)} %get-tuple-element.184), channel_id=1, source_target_pairs={{0,4},{1,5},{2,6},{3,7},{4,0},{5,1},{6,2},{7,3},{8,12},{9,13},{10,... | collective-permute-start | bytes 1572872 | tf_op jit(solution)/shard_map/ppermute | solution.py:668
  153.3 23.3 %collective-permute-start.37 = (f32[4,64,512]{2,1,0:T(8,128)S(1)}, f32[4,64,512]{2,1,0:T(8,128)S(1)}, u32[]{:S(2)}, u32[]{:S(2)}) collective-permute-start(f32[4,64,512]{2,1,0:T(8,128)S(1)} %get-tuple-element.185), channel_id=1, source_target_pairs={{0,6},{1,7},{2,4},{3,5},{4,2},{5,3},{6,0},{7,1},{8,14},{9,15},{10,... | collective-permute-start | bytes 1572872 | tf_op jit(solution)/shard_map/ppermute | solution.py:668
  154.6 24.9 %collective-permute-start.42 = (f32[72,512]{1,0:T(8,128)S(1)}, f32[72,512]{1,0:T(8,128)S(1)}, u32[]{:S(2)}, u32[]{:S(2)}) collective-permute-start(f32[72,512]{1,0:T(8,128)S(1)} %get-tuple-element.217), channel_id=1, source_target_pairs={{0,8},{8,0},{16,24},{24,16},{1,9},{9,1},{17,25},{25,17},{2,10},{10... | collective-permute-start | bytes 442376 | tf_op jit(solution)/shard_map/ppermute | solution.py:668
  154.7 24.8 %collective-permute-start.43 = (f32[72,512]{1,0:T(8,128)S(1)}, f32[72,512]{1,0:T(8,128)S(1)}, u32[]{:S(2)}, u32[]{:S(2)}) collective-permute-start(f32[72,512]{1,0:T(8,128)S(1)} %get-tuple-element.216), channel_id=1, source_target_pairs={{0,16},{8,24},{16,0},{24,8},{1,17},{9,25},{17,1},{25,9},{2,18},{10... | collective-permute-start | bytes 442376 | tf_op jit(solution)/shard_map/ppermute | solution.py:668
  165.4 14.1 %collective-permute-start.44 = (f32[72,512]{1,0:T(8,128)S(1)}, f32[72,512]{1,0:T(8,128)S(1)}, u32[]{:S(2)}, u32[]{:S(2)}) collective-permute-start(f32[72,512]{1,0:T(8,128)S(1)} %get-tuple-element.215), channel_id=1, source_target_pairs={{0,24},{8,16},{16,8},{24,0},{1,25},{9,17},{17,9},{25,1},{2,26},{10... | collective-permute-start | bytes 442376 | tf_op jit(solution)/shard_map/ppermute | solution.py:668
  192.2 12.9 %collective-permute-start.53 = (f32[112,512]{1,0:T(8,128)S(1)}, f32[112,512]{1,0:T(8,128)S(1)}, u32[]{:S(2)}, u32[]{:S(2)}) collective-permute-start(f32[112,512]{1,0:T(8,128)S(1)} %pad_maximum_fusion.2.refs_0_), channel_id=1, source_target_pairs={{0,6},{1,7},{2,4},{3,5},{4,2},{5,3},{6,0},{7,1},{8,14},{9,15},{10,... | collective-permute-start | bytes 688136 | tf_op jit(solution)/shard_map/ppermute | solution.py:668
  193.4 13.4 %collective-permute-start.48 = (f32[112,512]{1,0:T(8,128)S(1)}, f32[112,512]{1,0:T(8,128)S(1)}, u32[]{:S(2)}, u32[]{:S(2)}) collective-permute-start(f32[112,512]{1,0:T(8,128)S(1)} %pad_maximum_fusion.2.refs_0_), channel_id=1, source_target_pairs={{0,1},{1,0},{2,3},{3,2},{4,5},{5,4},{6,7},{7,6},{8,9},{9,8},{10,11... | collective-permute-start | bytes 688136 | tf_op jit(solution)/shard_map/ppermute | solution.py:668
  (58 other events, 482.9 us)

commit v4 on v3

--- a/solution.py
+++ b/solution.py
@@ -444,7 +444,7 @@
 
 
 def pack_kernel(dim, in_map, out_map, glu, gain, bias, skip, nu, theta, gamma, glu_bias, *refs):
-    outs, held, sem = refs[:2], refs[2:-1], refs[-1]
+    outs, held, sem = refs[:3], refs[3:-1], refs[-1]
     vectors = (gain, bias, skip, nu, theta, gamma, glu_bias)
     me, my = lax.axis_index("seq"), lax.axis_index("dp")
     start = pl.multiple_of(jnp.minimum(me, dim.used - 1) * dim.q, 16)
@@ -452,7 +452,7 @@
     for src, dst in zip(vectors, held):
         moves.append(pltpu.make_async_copy(src, dst, sem.at[len(moves)]))
     gain, bias, skip, nu, theta, gamma, glu_bias = held
-    for out, chunk in zip(outs, (CHUNKS[0], CHUNKS[1] + CHUNKS[2])):
+    for out, chunk in zip(outs, CHUNKS):
         head = out.shape[0] - len(chunk) * dim.q
         for i, name in enumerate(chunk):
             src = shard_of((in_map, out_map, glu), name, pl.ds(start, dim.q), dim.H)
@@ -701,7 +701,10 @@
 
 
 def unpack_kernel(dim, shares, kinds, last, *refs):
-    pieces, (mine, other), outs = refs[: dim.S], refs[dim.S : dim.S + 2], refs[dim.S + 2 :]
+    lower, upper, outs, (mine, other) = refs[: dim.S], refs[dim.S : 2 * dim.S], refs[2 * dim.S : -2], refs[-2:]
+    head = last.q + SMALL
+    for dst, first in ((mine, 0), (other, 1)):
+        dst[...] = tree_sum([lower[k][:head, :] for k in range(first, dim.S, 2)])
     g_gain, g_bias, g_nu, g_theta, g_gamma, g_in, g_out, g_skip, g_glu, g_glu_bias = outs
     me, my = lax.axis_index("seq"), lax.axis_index("dp")
 
@@ -716,15 +719,13 @@
             g_glu[layer, rows, dim.H : 2 * dim.H] = value
 
     def put(k, s):
-        base = 0
-        for share, names in zip(shares, kinds):
+        for share, names, src, base in zip(shares, kinds, (lower[k], upper[k]), (head, 0)):
             for off in range(0, share.q, share.step):
                 p = s * share.q + off
                 if p // dim.Hd < share.nm:
                     layer, kind = names[p // dim.Hd]
                     r = p % dim.Hd
-                    place(layer, kind, slice(r, r + share.step), pieces[k][base + off : base + off + share.step, :])
-            base += share.q
+                    place(layer, kind, slice(r, r + share.step), src[base + off : base + off + share.step, :])
 
     def vectors(d):
         def own(layer, index, lo, width, out, at=0):
@@ -762,12 +763,12 @@
         pl.when(my == d)(functools.partial(vectors, d))
 
 
-def unpack(dim, shares, kinds, last, pieces, mine, other):
+def unpack(dim, shares, kinds, last, lower, upper):
     n, l = dim.N // dim.D, dim.layers
     vec, small = f32(l, dim.Hd), f32(l, n)
     mat, wide = f32(l, dim.Hd, dim.H), f32(l, dim.Hd, 2 * dim.H)
     outs = [vec, vec, small, small, small, mat, mat, vec, wide, f32(l, 2 * dim.H // dim.D)]
-    return call(functools.partial(unpack_kernel, dim, shares, kinds, last), outs, [], *pieces, mine, other)
+    return call(functools.partial(unpack_kernel, dim, shares, kinds, last), outs, [pltpu.VMEM((last.q + SMALL, dim.H), F32)] * 2, *lower, *upper)
 
 
 def body(inputs, out_grad, ln_gain, ln_bias, nu_log, theta_log, gamma_log, in_map, out_map, skip_gain, glu_weight, glu_bias):
@@ -777,12 +778,11 @@
     x = inputs.reshape(R, dim.L, H)
     og = out_grad.reshape(R, dim.L, H)
 
-    heads = [SMALL, SMALL]
-    sends = [CHUNKS[0], CHUNKS[1] + CHUNKS[2]]
+    heads = [SMALL, SMALL, 0]
     vectors = (ln_gain, ln_bias, skip_gain, nu_log, theta_log, gamma_log, glu_bias)
     messages = call(
         functools.partial(pack_kernel, dim),
-        [f32(head + len(chunk) * dim.q, H) for head, chunk in zip(heads, sends)],
+        [f32(head + len(chunk) * dim.q, H) for head, chunk in zip(heads, CHUNKS)],
         [pltpu.VMEM(v.shape, F32) for v in vectors] + [pltpu.SemaphoreType.DMA((len(vectors) + sum(map(len, CHUNKS)),))],
         in_map, out_map, glu_weight, *vectors,
         anywhere=3 + len(vectors),
@@ -799,18 +799,21 @@
             total = total + other[:head]
         return call(functools.partial(prep_kernel, dim), [f32(TABLE, H)], [], total)[0]
 
-    mine0, mine1 = messages
+    mine0, mine1, mine2 = messages
     others0 = along_dp(mine0)
     table0 = table_of(mine0, others0)
     mine1, others0 = tie(mine1, others0)
     others1 = along_dp(mine1)
     table1 = table_of(mine1, others1)
     chips0 = chips_gather(dim, stacked(others0, SMALL))
-    cut = SMALL + len(CHUNKS[1]) * dim.q
-    joined1, chips0 = tie(stacked([o[:cut] for o in others1], SMALL), chips0)
-    joined2 = stacked(others1, cut)
+    joined1, chips0 = tie(stacked(others1, SMALL), chips0)
     pieces0 = cores_gather(chips0)
+    mine2, (joined1,) = tie(mine2, [joined1])
     chips1 = chips_gather(dim, joined1)
+    blocks = mine2[None]
+    while blocks.shape[0] < D:
+        blocks = jnp.concatenate([blocks, swap(blocks, "dp", blocks.shape[0])], 0)
+    joined2 = stacked([blocks[k] for k in range(1, D)], 0)
     pieces = [pieces0, cores_gather(chips1), None]
 
     big, ent, fins = pltpu.VMEM((T, H), F32), pltpu.VMEM((R, H), F32), f32(B, H)
@@ -877,8 +880,7 @@
     )
     rfin0, (send2, *sums1) = tie(rfin0, [send2, *plane_sums(dim, half1)])
     gr0 = carried(rfin0)
-    upper1 = dp_sum(dim, sums1)
-    gr0, (upper1, *half2) = tie(gr0, [upper1, *half_sums(dim, keep2, send2)])
+    gr0, half2 = tie(gr0, half_sums(dim, keep2, send2))
     input_grad, keep3, send3 = k(
         functools.partial(k_c0, share3),
         [(0, 0)],
@@ -889,14 +891,14 @@
     )
     sums2 = plane_sums(dim, half2)
     got3 = swap(send3, "seq", 1)
-    half3 = [keep3[d] + got3[d] for d in range(D)]
+    half3 = [jnp.concatenate([keep3[d] + got3[d], sums1[d]], 0) for d in range(D)]
     total3 = tree_sum([half3[0]] + [swap(half3[k], "dp", k) for k in range(1, D)])
-    mine3 = tree_sum(chips_gather(dim, total3))
-    joint, (mine3,) = tie(jnp.concatenate([upper1, dp_sum(dim, sums2)], 0), [mine3])
+    chips3 = chips_gather(dim, total3)
+    joint, chips3 = tie(dp_sum(dim, sums2), chips3)
+    last = cores_gather(chips3)
     upper = plane_gather(dim, joint)
-    other3 = swap(mine3, "seq", 1)
     kinds = [[(1, "gv"), (1, "gg"), (1, "out")], [(0, "gv"), (0, "gg"), (0, "out"), (1, "in")]]
-    grads = unpack(dim, (share1, share2), kinds, share3, upper, mine3, other3)
+    grads = unpack(dim, (share1, share2), kinds, share3, last, upper)
     return (out.reshape(inputs.shape), input_grad.reshape(inputs.shape), *grads)
 
 

time: 209 us -> 197 us (0.943)
  waiting for transfers between devices: 51.5 us -> 44.6 us
  starting transfers between devices: 59.3 us -> 53.2 us
    ppermute x56 -> x58, waiting for transfers between devices: 51.5 us -> 44.6 us  [swap(): return lax.ppermute(x, axis, [(i, i ^ mask) for i in range(count)])]
    ppermute x56 -> x58, starting transfers between devices: 59.3 us -> 53.2 us  [swap(): return lax.ppermute(x, axis, [(i, i ^ mask) for i in range(count)])]
  transfers between devices with their start and end apart: 56 -> 58, of which waited for: 12 -> 15; matrix products, arithmetic and copies ran while one was open for 0% -> 0% of each run, Pallas kernels for 14% -> 15%
where the time goes in v4:
time: 197 us; the launch traced here: 195 us
  Pallas kernels  56.3 us (29%)
  starting transfers between devices  53.2 us (27%)
  waiting for transfers between devices  44.6 us (23%)
  blocking collectives  36.2 us (18%)
    pallas_call x11, Pallas kernels, call(): pl.pallas_call(fn, out_shape=outs, in_specs=[pl.BlockSpec(memory_space=sp...  56.3 us
    ppermute x58, starting transfers between devices, swap(): return lax.ppermute(x, axis, [(i, i ^ mask) for i in range(count)])  53.2 us
    ppermute x58, waiting for transfers between devices, swap(): return lax.ppermute(x, axis, [(i, i ^ mask) for i in range(count)])  44.6 us
    all_gather x4, blocking collectives, carried(): return lax.all_gather(fin, 'seq')  36.2 us
  transfers between devices with their start and end apart: 58, of which 15 were waited for; matrix products, arithmetic and copies ran while one was open for 0% of the time, Pallas kernels for 15%

profile of v4, /device:TPU:9, one launch (start us, length us, event | category | flops | bytes accessed | tf_op | source)
XLA Modules:
  0.0 194.9 jit_solution(16976738980684790229)
XLA Ops:
  1.9 2.5 %collective-permute-start.1 = (f32[40,512]{1,0:T(8,128)S(1)}, f32[40,512]{1,0:T(8,128)S(1)}, u32[]{:S(2)}, u32[]{:S(2)}) collective-permute-start(f32[40,512]{1,0:T(8,128)S(1)} %get-tuple-element.112), channel_id=1, source_target_pairs={{0,16},{8,24},{16,0},{24,8},{1,17},{9,25},{17,1},{25,9},{2,18},{10... | collective-permute-start | bytes 245768 | tf_op jit(solution)/shard_map/ppermute | solution.py:668
  5.2 2.5 %collective-permute-done.1 = f32[40,512]{1,0:T(8,128)S(1)} collective-permute-done((f32[40,512]{1,0:T(8,128)S(1)}, f32[40,512]{1,0:T(8,128)S(1)}, u32[]{:S(2)}, u32[]{:S(2)}) %collective-permute-start.1) | collective-permute-done | bytes 81952 | tf_op jit(solution)/shard_map/ppermute | solution.py:668
  7.7 3.9 %collective-permute-done.2 = f32[40,512]{1,0:T(8,128)S(1)} collective-permute-done((f32[40,512]{1,0:T(8,128)S(1)}, f32[40,512]{1,0:T(8,128)S(1)}, u32[]{:S(2)}, u32[]{:S(2)}) %collective-permute-start.2) | collective-permute-done | bytes 81952 | tf_op jit(solution)/shard_map/ppermute | solution.py:668
  11.6 2.3 %collective-permute-start.4 = (f32[56,512]{1,0:T(8,128)S(1)}, f32[56,512]{1,0:T(8,128)S(1)}, u32[]{:S(2)}, u32[]{:S(2)}) collective-permute-start(f32[56,512]{1,0:T(8,128)S(1)} %get-tuple-element.113), channel_id=1, source_target_pairs={{0,16},{8,24},{16,0},{24,8},{1,17},{9,25},{17,1},{25,9},{2,18},{10... | collective-permute-start | bytes 344072 | tf_op jit(solution)/shard_map/ppermute | solution.py:668
  17.7 6.4 %collective-permute-done.5 = f32[56,512]{1,0:T(8,128)S(1)} collective-permute-done((f32[56,512]{1,0:T(8,128)S(1)}, f32[56,512]{1,0:T(8,128)S(1)}, u32[]{:S(2)}, u32[]{:S(2)}) %collective-permute-start.5) | collective-permute-done | bytes 114720 | tf_op jit(solution)/shard_map/ppermute | solution.py:668
  24.7 4.0 %collective-permute-start.10 = (f32[2,3,16,512]{3,2,1,0:T(8,128)S(1)}, f32[2,3,16,512]{3,2,1,0:T(8,128)S(1)}, u32[]{:S(2)}, u32[]{:S(2)}) collective-permute-start(f32[2,3,16,512]{3,2,1,0:T(8,128)S(1)} %collective-permute-done.6.refs_5_), channel_id=1, source_target_pairs={{0,1},{1,0},{2,3},{3,2},{4,5},{5,4},{6,7},{7,6},{8,9},{9,8},{10,11... | collective-permute-start | bytes 589832 | tf_op jit(solution)/shard_map/ppermute | solution.py:668
  29.8 2.3 %collective-permute-start.12 = (f32[2,3,16,512]{3,2,1,0:T(8,128)S(1)}, f32[2,3,16,512]{3,2,1,0:T(8,128)S(1)}, u32[]{:S(2)}, u32[]{:S(2)}) collective-permute-start(f32[2,3,16,512]{3,2,1,0:T(8,128)S(1)} %collective-permute-done.8.refs_9_), channel_id=1, source_target_pairs={{0,1},{1,0},{2,3},{3,2},{4,5},{5,4},{6,7},{7,6},{8,9},{9,8},{10,11... | collective-permute-start | bytes 589832 | tf_op jit(solution)/shard_map/ppermute | solution.py:668
  36.1 2.8 %shard_map.214 = (f32[512,512]{1,0:T(8,128)S(1)}, f32[512,128]{1,0:T(8,128)S(1)}, f32[512,512]{1,0:T(8,128)S(1)}, f32[16,512]{1,0:T(8,128)S(1)}, f32[2,512]{1,0:T(2,128)S(1)}) custom-call(f32[2,128,512]{2,1,0:T(8,128)} %refs_0_.9, f32[2,128,512]{2,1,0:T(8,128)} %refs_1_.9, f32[2,128,1024]{2,1,0:T(8,128)} %refs_2_.9, f32[2,3,16,512]{3,2,1,0:T(8,128)} %copy-done.2, ...), custom_call_target="tpu_custom_call" | custom-call | flops 1 | bytes 12240000 | tf_op jit(solution)/shard_map/pallas_call | solution.py:395
  38.9 9.7 %all-gather.4.refs_24_ = f32[8,2,512]{2,1,0:T(2,128)S(1)} all-gather(f32[1,2,512]{2,1,0:T(2,128)S(1)} %bitcast.73), channel_id=2, replica_groups=mesh['dp'=4,'seq'=8] {'seq'}, dimensions={0}, use_global_device_ids=true | all-gather | bytes 36864 | tf_op jit(solution)/shard_map/all_gather | solution.py:830
  53.1 9.3 %shard_map.215 = (f32[16,512]{1,0:T(8,128)S(1)}, f32[512,512]{1,0:T(8,128)S(1)}, f32[512,512]{1,0:T(8,128)S(1)}, f32[512,512]{1,0:T(8,128)S(1)}, f32[512,512]{1,...) custom-call(f32[2,128,512]{2,1,0:T(8,128)} %refs_0_.9, ...), custom_call_target="tpu_custom_call" | custom-call | flops 1 | bytes 36000000 | tf_op jit(solution)/shard_map/pallas_call | solution.py:395
  62.4 2.3 %collective-permute-done.24.refs_9_ = f32[3,3,16,512]{3,2,1,0:T(8,128)S(1)} collective-permute-done((f32[3,3,16,512]{3,2,1,0:T(8,128)S(1)}, f32[3,3,16,512]{3,2,1,0:T(8,128)S(1)}, u32[]{:S(2)}, u32[]{:S(2)}) %collective-permute-start.24) | collective-permute-done | bytes 294944 | tf_op jit(solution)/shard_map/ppermute | solution.py:668
  66.5 9.0 %all-gather.5.refs_16_ = f32[8,2,512]{2,1,0:T(2,128)S(1)} all-gather(f32[1,2,512]{2,1,0:T(2,128)S(1)} %bitcast.71), channel_id=3, replica_groups=mesh['dp'=4,'seq'=8] {'seq'}, dimensions={0}, use_global_device_ids=true | all-gather | bytes 36864 | tf_op jit(solution)/shard_map/all_gather | solution.py:830
  76.5 13.4 %shard_map.216 = (f32[16,32,512]{2,1,0:T(8,128)}, f32[16,512]{1,0:T(8,128)S(1)}, f32[512,512]{1,0:T(8,128)S(1)}, f32[512,512]{1,0:T(8,128)S(1)}, f32[512,512]{1,...) custom-call(f32[2,128,512]{2,1,0:T(8,128)} %refs_0_.9, ...), custom_call_target="tpu_custom_call" | custom-call | flops 1 | bytes 46800000 | tf_op jit(solution)/shard_map/pallas_call | solution.py:395
  89.9 4.9 %shard_map.217 = (f32[4,4,48,512]{3,2,1,0:T(8,128)S(1)}, f32[4,4,48,512]{3,2,1,0:T(8,128)S(1)}) custom-call(f32[512,512]{1,0:T(8,128)S(1)} %get-tuple-element.145.active, f32[512,512]{1,0:T(8,128)S(1)} %get-tuple-element.146.dv, f32[512,512]{1,0:T(8,128)S(1)} %get-tuple-element.147.dg, f32[512,512]{1,0:T(8,128)S(1)} %get-tuple-element.148.states.refs_25_, ...), custom_call_target="tpu_custom_call" | custom-call | flops 1 | bytes 18000000 | tf_op jit(solution)/shard_map/pallas_call | solution.py:395
  95.0 8.9 %all-gather.6.refs_24_ = f32[8,2,512]{2,1,0:T(2,128)S(1)} all-gather(f32[1,2,512]{2,1,0:T(2,128)S(1)} %bitcast.72), channel_id=4, replica_groups=mesh['dp'=4,'seq'=8] {'seq'}, dimensions={0}, use_global_device_ids=true | all-gather | bytes 36864 | tf_op jit(solution)/shard_map/all_gather | solution.py:830
  107.0 9.9 %shard_map.218 = (f32[512,512]{1,0:T(8,128)S(1)}, f32[512,512]{1,0:T(8,128)S(1)}, f32[512,512]{1,0:T(8,128)S(1)}, f32[512,512]{1,0:T(8,128)S(1)}, f32[512,512]{1...) custom-call(f32[2,128,512]{2,1,0:T(8,128)} %refs_0_.9, ...), custom_call_target="tpu_custom_call" | custom-call | flops 1 | bytes 39600000 | tf_op jit(solution)/shard_map/pallas_call | solution.py:395
  116.8 6.4 %shard_map.219 = (f32[4,4,64,512]{3,2,1,0:T(8,128)S(1)}, f32[4,4,64,512]{3,2,1,0:T(8,128)S(1)}) custom-call(f32[512,512]{1,0:T(8,128)S(1)} %get-tuple-element.163.active, f32[512,512]{1,0:T(8,128)S(1)} %get-tuple-element.164.dv, f32[512,512]{1,0:T(8,128)S(1)} %get-tuple-element.165.dg, f32[512,512]{1,0:T(8,128)S(1)} %get-tuple-element.166.states.refs_15_, ...), custom_call_target="tpu_custom_call" | custom-call | flops 1 | bytes 23040000 | tf_op jit(solution)/shard_map/pallas_call | solution.py:395
  125.0 8.6 %all-gather.7.refs_14_ = f32[8,2,512]{2,1,0:T(2,128)S(1)} all-gather(f32[1,2,512]{2,1,0:T(2,128)S(1)} %bitcast.70), channel_id=5, replica_groups=mesh['dp'=4,'seq'=8] {'seq'}, dimensions={0}, use_global_device_ids=true | all-gather | bytes 36864 | tf_op jit(solution)/shard_map/all_gather | solution.py:830
  134.1 6.4 %shard_map.220 = (f32[16,32,512]{2,1,0:T(8,128)}, f32[4,72,512]{2,1,0:T(8,128)S(1)}, f32[4,72,512]{2,1,0:T(8,128)S(1)}) custom-call(f32[2,128,512]{2,1,0:T(8,128)} %refs_0_.9, f32[2,128,512]{2,1,0:T(8,128)} %refs_1_.9, f32[2,128,1024]{2,1,0:T(8,128)} %refs_2_.9, f32[2,3,16,512]{3,2,1,0:T(8,128)} %copy-done.2, f32[2,3,16,512]{3,2,1,0:T(8,128)} %copy-done.9, ...), custom_call_target="tpu_custom_call" | custom-call | flops 1 | bytes 26640000 | tf_op jit(solution)/shard_map/pallas_call | solution.py:395
  146.4 7.6 %collective-permute-done.34 = f32[4,64,512]{2,1,0:T(8,128)S(1)} collective-permute-done((f32[4,64,512]{2,1,0:T(8,128)S(1)}, f32[4,64,512]{2,1,0:T(8,128)S(1)}, u32[]{:S(2)}, u32[]{:S(2)}) %collective-permute-start.34) | collective-permute-done | bytes 524320 | tf_op jit(solution)/shard_map/ppermute | solution.py:668
  154.6 11.0 %collective-permute-done.36 = f32[4,64,512]{2,1,0:T(8,128)S(1)} collective-permute-done((f32[4,64,512]{2,1,0:T(8,128)S(1)}, f32[4,64,512]{2,1,0:T(8,128)S(1)}, u32[]{:S(2)}, u32[]{:S(2)}) %collective-permute-start.36) | collective-permute-done | bytes 524320 | tf_op jit(solution)/shard_map/ppermute | solution.py:668
  172.7 6.9 %collective-permute-done.39 = f32[64,512]{1,0:T(8,128)S(1)} collective-permute-done((f32[64,512]{1,0:T(8,128)S(1)}, f32[64,512]{1,0:T(8,128)S(1)}, u32[]{:S(2)}, u32[]{:S(2)}) %collective-permute-start.39) | collective-permute-done | bytes 131104 | tf_op jit(solution)/shard_map/ppermute | solution.py:668
  182.3 4.3 %collective-permute-start.47 = (f32[120,512]{1,0:T(8,128)S(1)}, f32[120,512]{1,0:T(8,128)S(1)}, u32[]{:S(2)}, u32[]{:S(2)}) collective-permute-start(f32[120,512]{1,0:T(8,128)S(1)} %fusion.8.refs_0_), channel_id=1, source_target_pairs={{0,1},{1,0},{2,3},{3,2},{4,5},{5,4},{6,7},{7,6},{8,9},{9,8},{10,11... | collective-permute-start | bytes 737288 | tf_op jit(solution)/shard_map/ppermute | solution.py:668
  188.9 2.1 %collective-permute-start.50 = (f32[120,512]{1,0:T(8,128)S(1)}, f32[120,512]{1,0:T(8,128)S(1)}, u32[]{:S(2)}, u32[]{:S(2)}) collective-permute-start(f32[120,512]{1,0:T(8,128)S(1)} %collective-permute-done.46.refs_6_), channel_id=1, source_target_pairs={{0,1},{1,0},{2,3},{3,2},{4,5},{5,4},{6,7},{7,6},{8,9},{9,8},{10,11... | collective-permute-start | bytes 737288 | tf_op jit(solution)/shard_map/ppermute | solution.py:668
  (182 shorter events, 46.7 us)
Async XLA Ops:
  13.9 10.3 %collective-permute-start.5 = (f32[56,512]{1,0:T(8,128)S(1)}, f32[56,512]{1,0:T(8,128)S(1)}, u32[]{:S(2)}, u32[]{:S(2)}) collective-permute-start(f32[56,512]{1,0:T(8,128)S(1)} %get-tuple-element.113), channel_id=1, source_target_pairs={{0,24},{8,16},{16,8},{24,0},{1,25},{9,17},{17,9},{25,1},{2,26},{10... | collective-permute-start | bytes 344072 | tf_op jit(solution)/shard_map/ppermute | solution.py:668
  14.3 9.9 %collective-permute-start.6 = (f32[2,3,16,512]{3,2,1,0:T(8,128)S(1)}, f32[2,3,16,512]{3,2,1,0:T(8,128)S(1)}, u32[]{:S(2)}, u32[]{:S(2)}) collective-permute-start(f32[2,3,16,512]{3,2,1,0:T(8,128)S(1)} %pad_maximum_fusion.5.refs_3_), channel_id=1, source_target_pairs={{0,2},{1,3},{2,0},{3,1},{4,6},{5,7},{6,4},{7,5},{8,10},{9,11},{10,... | collective-permute-start | bytes 589832 | tf_op jit(solution)/shard_map/ppermute | solution.py:668
  28.7 20.0 %collective-permute-start.14 = (f32[3,3,16,512]{3,2,1,0:T(8,128)S(1)}, f32[3,3,16,512]{3,2,1,0:T(8,128)S(1)}, u32[]{:S(2)}, u32[]{:S(2)}) collective-permute-start(f32[3,3,16,512]{3,2,1,0:T(8,128)S(1)} %pad_maximum_fusion.refs_11_), channel_id=1, source_target_pairs={{0,2},{1,3},{2,0},{3,1},{4,6},{5,7},{6,4},{7,5},{8,10},{9,11},{10,... | collective-permute-start | bytes 884744 | tf_op jit(solution)/shard_map/ppermute | solution.py:668
  29.2 19.6 %collective-permute-start.16 = (f32[3,3,16,512]{3,2,1,0:T(8,128)S(1)}, f32[3,3,16,512]{3,2,1,0:T(8,128)S(1)}, u32[]{:S(2)}, u32[]{:S(2)}) collective-permute-start(f32[3,3,16,512]{3,2,1,0:T(8,128)S(1)} %pad_maximum_fusion.refs_11_), channel_id=1, source_target_pairs={{0,4},{1,5},{2,6},{3,7},{4,0},{5,1},{6,2},{7,3},{8,12},{9,13},{10,... | collective-permute-start | bytes 884744 | tf_op jit(solution)/shard_map/ppermute | solution.py:668
  32.2 17.0 %collective-permute-start.21 = (f32[2,48,512]{2,1,0:T(8,128)S(1)}, f32[2,48,512]{2,1,0:T(8,128)S(1)}, u32[]{:S(2)}, u32[]{:S(2)}) collective-permute-start(f32[2,48,512]{2,1,0:T(8,128)S(1)} %pad_maximum_fusion.6), channel_id=1, source_target_pairs={{0,16},{8,24},{16,0},{24,8},{1,17},{9,25},{17,1},{25,9},{2,18},{10... | collective-permute-start | bytes 589832 | tf_op jit(solution)/shard_map/ppermute | solution.py:668
  34.1 15.2 %collective-permute-start.18 = (f32[3,3,16,512]{3,2,1,0:T(8,128)S(1)}, f32[3,3,16,512]{3,2,1,0:T(8,128)S(1)}, u32[]{:S(2)}, u32[]{:S(2)}) collective-permute-start(f32[3,3,16,512]{3,2,1,0:T(8,128)S(1)} %pad_maximum_fusion.refs_11_), channel_id=1, source_target_pairs={{0,6},{1,7},{2,4},{3,5},{4,2},{5,3},{6,0},{7,1},{8,14},{9,15},{10,... | collective-permute-start | bytes 884744 | tf_op jit(solution)/shard_map/ppermute | solution.py:668
  35.1 15.0 %collective-permute-start.13 = (f32[3,3,16,512]{3,2,1,0:T(8,128)S(1)}, f32[3,3,16,512]{3,2,1,0:T(8,128)S(1)}, u32[]{:S(2)}, u32[]{:S(2)}) collective-permute-start(f32[3,3,16,512]{3,2,1,0:T(8,128)S(1)} %pad_maximum_fusion.refs_11_), channel_id=1, source_target_pairs={{0,1},{1,0},{2,3},{3,2},{4,5},{5,4},{6,7},{7,6},{8,9},{9,8},{10,11... | collective-permute-start | bytes 884744 | tf_op jit(solution)/shard_map/ppermute | solution.py:668
  49.5 12.9 %collective-permute-start.22 = (f32[3,3,16,512]{3,2,1,0:T(8,128)S(1)}, f32[3,3,16,512]{3,2,1,0:T(8,128)S(1)}, u32[]{:S(2)}, u32[]{:S(2)}) collective-permute-start(f32[3,3,16,512]{3,2,1,0:T(8,128)S(1)} %pad_maximum_fusion.1.refs_3_), channel_id=1, source_target_pairs={{0,2},{1,3},{2,0},{3,1},{4,6},{5,7},{6,4},{7,5},{8,10},{9,11},{10,... | collective-permute-start | bytes 884744 | tf_op jit(solution)/shard_map/ppermute | solution.py:668
  50.1 12.3 %collective-permute-start.23 = (f32[3,3,16,512]{3,2,1,0:T(8,128)S(1)}, f32[3,3,16,512]{3,2,1,0:T(8,128)S(1)}, u32[]{:S(2)}, u32[]{:S(2)}) collective-permute-start(f32[3,3,16,512]{3,2,1,0:T(8,128)S(1)} %pad_maximum_fusion.1.refs_3_), channel_id=1, source_target_pairs={{0,4},{1,5},{2,6},{3,7},{4,0},{5,1},{6,2},{7,3},{8,12},{9,13},{10,... | collective-permute-start | bytes 884744 | tf_op jit(solution)/shard_map/ppermute | solution.py:668
  50.8 14.0 %collective-permute-start.24 = (f32[3,3,16,512]{3,2,1,0:T(8,128)S(1)}, f32[3,3,16,512]{3,2,1,0:T(8,128)S(1)}, u32[]{:S(2)}, u32[]{:S(2)}) collective-permute-start(f32[3,3,16,512]{3,2,1,0:T(8,128)S(1)} %pad_maximum_fusion.1.refs_3_), channel_id=1, source_target_pairs={{0,6},{1,7},{2,4},{3,5},{4,2},{5,3},{6,0},{7,1},{8,14},{9,15},{10,... | collective-permute-start | bytes 884744 | tf_op jit(solution)/shard_map/ppermute | solution.py:668
  64.7 10.8 %collective-permute-start.25 = (f32[3,3,16,512]{3,2,1,0:T(8,128)S(1)}, f32[3,3,16,512]{3,2,1,0:T(8,128)S(1)}, u32[]{:S(2)}, u32[]{:S(2)}) collective-permute-start(f32[3,3,16,512]{3,2,1,0:T(8,128)S(1)} %pad_maximum_fusion.1.refs_3_), channel_id=1, source_target_pairs={{0,1},{1,0},{2,3},{3,2},{4,5},{5,4},{6,7},{7,6},{8,9},{9,8},{10,11... | collective-permute-start | bytes 884744 | tf_op jit(solution)/shard_map/ppermute | solution.py:668
  104.2 19.0 %collective-permute-start.30 = (f32[4,48,512]{2,1,0:T(8,128)S(1)}, f32[4,48,512]{2,1,0:T(8,128)S(1)}, u32[]{:S(2)}, u32[]{:S(2)}) collective-permute-start(f32[4,48,512]{2,1,0:T(8,128)S(1)} %get-tuple-element.171), channel_id=1, source_target_pairs={{0,2},{1,3},{2,0},{3,1},{4,6},{5,7},{6,4},{7,5},{8,10},{9,11},{10,... | collective-permute-start | bytes 1179656 | tf_op jit(solution)/shard_map/ppermute | solution.py:668
  104.9 18.4 %collective-permute-start.31 = (f32[4,48,512]{2,1,0:T(8,128)S(1)}, f32[4,48,512]{2,1,0:T(8,128)S(1)}, u32[]{:S(2)}, u32[]{:S(2)}) collective-permute-start(f32[4,48,512]{2,1,0:T(8,128)S(1)} %get-tuple-element.172), channel_id=1, source_target_pairs={{0,4},{1,5},{2,6},{3,7},{4,0},{5,1},{6,2},{7,3},{8,12},{9,13},{10,... | collective-permute-start | bytes 1179656 | tf_op jit(solution)/shard_map/ppermute | solution.py:668
  105.8 17.8 %collective-permute-start.32 = (f32[4,48,512]{2,1,0:T(8,128)S(1)}, f32[4,48,512]{2,1,0:T(8,128)S(1)}, u32[]{:S(2)}, u32[]{:S(2)}) collective-permute-start(f32[4,48,512]{2,1,0:T(8,128)S(1)} %get-tuple-element.173), channel_id=1, source_target_pairs={{0,6},{1,7},{2,4},{3,5},{4,2},{5,3},{6,0},{7,1},{8,14},{9,15},{10,... | collective-permute-start | bytes 1179656 | tf_op jit(solution)/shard_map/ppermute | solution.py:668
  123.7 9.9 %collective-permute-start.33 = (f32[4,4,64,512]{3,2,1,0:T(8,128)S(1)}, f32[4,4,64,512]{3,2,1,0:T(8,128)S(1)}, u32[]{:S(2)}, u32[]{:S(2)}) collective-permute-start(f32[4,4,64,512]{3,2,1,0:T(8,128)S(1)} %get-tuple-element.176), channel_id=1, source_target_pairs={{0,1},{1,0},{2,3},{3,2},{4,5},{5,4},{6,7},{7,6},{8,9},{9,8},{10,11... | collective-permute-start | bytes 6291464 | tf_op jit(solution)/shard_map/ppermute | solution.py:668
  140.8 13.2 %collective-permute-start.34 = (f32[4,64,512]{2,1,0:T(8,128)S(1)}, f32[4,64,512]{2,1,0:T(8,128)S(1)}, u32[]{:S(2)}, u32[]{:S(2)}) collective-permute-start(f32[4,64,512]{2,1,0:T(8,128)S(1)} %get-tuple-element.186), channel_id=1, source_target_pairs={{0,2},{1,3},{2,0},{3,1},{4,6},{5,7},{6,4},{7,5},{8,10},{9,11},{10,... | collective-permute-start | bytes 1572872 | tf_op jit(solution)/shard_map/ppermute | solution.py:668
  141.3 13.2 %collective-permute-start.35 = (f32[4,64,512]{2,1,0:T(8,128)S(1)}, f32[4,64,512]{2,1,0:T(8,128)S(1)}, u32[]{:S(2)}, u32[]{:S(2)}) collective-permute-start(f32[4,64,512]{2,1,0:T(8,128)S(1)} %get-tuple-element.187), channel_id=1, source_target_pairs={{0,4},{1,5},{2,6},{3,7},{4,0},{5,1},{6,2},{7,3},{8,12},{9,13},{10,... | collective-permute-start | bytes 1572872 | tf_op jit(solution)/shard_map/ppermute | solution.py:668
  142.3 23.3 %collective-permute-start.36 = (f32[4,64,512]{2,1,0:T(8,128)S(1)}, f32[4,64,512]{2,1,0:T(8,128)S(1)}, u32[]{:S(2)}, u32[]{:S(2)}) collective-permute-start(f32[4,64,512]{2,1,0:T(8,128)S(1)} %get-tuple-element.188), channel_id=1, source_target_pairs={{0,6},{1,7},{2,4},{3,5},{4,2},{5,3},{6,0},{7,1},{8,14},{9,15},{10,... | collective-permute-start | bytes 1572872 | tf_op jit(solution)/shard_map/ppermute | solution.py:668
  143.6 24.4 %collective-permute-start.43 = (f32[120,512]{1,0:T(8,128)S(1)}, f32[120,512]{1,0:T(8,128)S(1)}, u32[]{:S(2)}, u32[]{:S(2)}) collective-permute-start(f32[120,512]{1,0:T(8,128)S(1)} %pad_maximum_fusion.4), channel_id=1, source_target_pairs={{0,24},{8,16},{16,8},{24,0},{1,25},{9,17},{17,9},{25,1},{2,26},{10... | collective-permute-start | bytes 737288 | tf_op jit(solution)/shard_map/ppermute | solution.py:668
  144.8 23.7 %collective-permute-start.42 = (f32[120,512]{1,0:T(8,128)S(1)}, f32[120,512]{1,0:T(8,128)S(1)}, u32[]{:S(2)}, u32[]{:S(2)}) collective-permute-start(f32[120,512]{1,0:T(8,128)S(1)} %pad_maximum_fusion.3), channel_id=1, source_target_pairs={{0,16},{8,24},{16,0},{24,8},{1,17},{9,25},{17,1},{25,9},{2,18},{10... | collective-permute-start | bytes 737288 | tf_op jit(solution)/shard_map/ppermute | solution.py:668
  154.0 14.4 %collective-permute-start.41 = (f32[120,512]{1,0:T(8,128)S(1)}, f32[120,512]{1,0:T(8,128)S(1)}, u32[]{:S(2)}, u32[]{:S(2)}) collective-permute-start(f32[120,512]{1,0:T(8,128)S(1)} %pad_maximum_fusion.2), channel_id=1, source_target_pairs={{0,8},{8,0},{16,24},{24,16},{1,9},{9,1},{17,25},{25,17},{2,10},{10... | collective-permute-start | bytes 737288 | tf_op jit(solution)/shard_map/ppermute | solution.py:668
  168.0 11.5 %collective-permute-start.39 = (f32[64,512]{1,0:T(8,128)S(1)}, f32[64,512]{1,0:T(8,128)S(1)}, u32[]{:S(2)}, u32[]{:S(2)}) collective-permute-start(f32[64,512]{1,0:T(8,128)S(1)} %get-tuple-element.219), channel_id=1, source_target_pairs={{0,24},{8,16},{16,8},{24,0},{1,25},{9,17},{17,9},{25,1},{2,26},{10... | collective-permute-start | bytes 393224 | tf_op jit(solution)/shard_map/ppermute | solution.py:668
  168.5 11.1 %collective-permute-start.44 = (f32[120,512]{1,0:T(8,128)S(1)}, f32[120,512]{1,0:T(8,128)S(1)}, u32[]{:S(2)}, u32[]{:S(2)}) collective-permute-start(f32[120,512]{1,0:T(8,128)S(1)} %fusion.8.refs_0_), channel_id=1, source_target_pairs={{0,2},{1,3},{2,0},{3,1},{4,6},{5,7},{6,4},{7,5},{8,10},{9,11},{10,... | collective-permute-start | bytes 737288 | tf_op jit(solution)/shard_map/ppermute | solution.py:668
  169.5 10.1 %collective-permute-start.45 = (f32[120,512]{1,0:T(8,128)S(1)}, f32[120,512]{1,0:T(8,128)S(1)}, u32[]{:S(2)}, u32[]{:S(2)}) collective-permute-start(f32[120,512]{1,0:T(8,128)S(1)} %fusion.8.refs_0_), channel_id=1, source_target_pairs={{0,4},{1,5},{2,6},{3,7},{4,0},{5,1},{6,2},{7,3},{8,12},{9,13},{10,... | collective-permute-start | bytes 737288 | tf_op jit(solution)/shard_map/ppermute | solution.py:668
  (60 other events, 414.6 us)

commit v5 on v4

--- a/solution.py
+++ b/solution.py
@@ -357,20 +357,24 @@
 
 
 def weight_grad(dim, share, m, ah, al, bh, bl, tile, keep, send):
+    for h0 in range(0, dim.H, WIDE):
+        tile[...] = dot3(ah[:, h0 : h0 + WIDE], al[:, h0 : h0 + WIDE], bh[...], bl[...], ((0,), (0,)))
+        put_rows(dim, share, m, h0, tile, keep, send)
+
+
+def put_rows(dim, share, m, h0, tile, keep, send):
     me = lax.axis_index("seq")
     my = lax.axis_index("dp")
-    for h0 in range(0, dim.H, WIDE):
-        tile[...] = dot3(ah[:, h0 : h0 + WIDE], al[:, h0 : h0 + WIDE], bh[...], bl[...], ((0,), (0,)))
-
-        def put(mine):
-            for r0 in range(0, WIDE, share.step):
-                h = h0 + r0
-                odd, index, off = share.place(m, h // dim.Hd, h % dim.Hd, me, my)
-                dst = keep if odd == mine else send
-                dst[(*index, slice(off, off + share.step), slice(None))] = tile[r0 : r0 + share.step, :]
-
-        for mine in range(2):
-            pl.when(me & 1 == mine)(functools.partial(put, mine))
+
+    def put(mine):
+        for r0 in range(0, WIDE, share.step):
+            h = h0 + r0
+            odd, index, off = share.place(m, h // dim.Hd, h % dim.Hd, me, my)
+            dst = keep if odd == mine else send
+            dst[(*index, slice(off, off + share.step), slice(None))] = tile[r0 : r0 + share.step, :]
+
+    for mine in range(2):
+        pl.when(me & 1 == mine)(functools.partial(put, mine))
 
 
 class Kept:
@@ -379,8 +383,48 @@
         self.shape = value.shape
 
 
-def call(fn, outs, scratch, *args, us=1.0, anywhere=0):
-    spaces = [pltpu.HBM] * anywhere + [pltpu.VMEM] * (len(args) - anywhere)
+class Moved:
+    def __init__(self, far, near, sem):
+        self.far, self.near, self.sem, self.copies = far, near, sem, []
+
+    def fetch(self):
+        self.copies.append(pltpu.make_async_copy(self.far, self.near, self.sem.at[0]))
+        self.copies[0].start()
+
+    def flush(self, *index):
+        sem = self.sem.at[len(self.copies)]
+        near, far = (self.near.at[index], self.far.at[index]) if index else (self.near, self.far)
+        self.copies.append(pltpu.make_async_copy(near, far, sem))
+        self.copies[-1].start()
+
+    def get(self):
+        for copy in self.copies:
+            copy.wait()
+        return self.near
+
+
+def call(fn, outs, scratch, *args, us=1.0, anywhere=0, late=(), sinks=()):
+    scratch = list(scratch)
+    first, total = len(args), len(args) + len(outs)
+    moved = list(late) + [first + i for i in sinks]
+    if moved:
+        inner = fn
+        for i in moved:
+            shape = args[i].shape if i < first else outs[i - first].shape
+            scratch += [pltpu.VMEM(shape, F32), pltpu.SemaphoreType.DMA((8,))]
+
+        def fn(*refs):
+            refs, spare = list(refs[: -2 * len(moved)]), refs[-2 * len(moved) :]
+            for n, i in enumerate(moved):
+                refs[i] = Moved(refs[i], *spare[2 * n : 2 * n + 2])
+                if i < first:
+                    refs[i].fetch()
+            inner(*refs)
+            for i in moved:
+                if i >= first:
+                    refs[i].get()
+
+    spaces = [pltpu.HBM if i < anywhere or i in late else pltpu.VMEM for i in range(first)]
 
     def placed(x, space):
         if isinstance(x, Kept):
@@ -396,7 +440,7 @@
         fn,
         out_shape=outs,
         in_specs=[pl.BlockSpec(memory_space=space) for space in spaces],
-        out_specs=[pl.BlockSpec(memory_space=pltpu.VMEM)] * len(outs),
+        out_specs=[pl.BlockSpec(memory_space=pl.ANY if i in sinks else pltpu.VMEM) for i in range(len(outs))],
         scratch_shapes=scratch,
         compiler_params=pltpu.CompilerParams(vmem_limit_bytes=max(20 << 20, room)),
         cost_estimate=pl.CostEstimate(flops=1, bytes_accessed=int(us * 3.6e6), transcendentals=0),
@@ -591,10 +635,11 @@
     back(dim, t, drive, cf, g, xhat, w_out, w_gv, w_gg, en, states, mixed, active, v, s, ah, al, wh, wl)
 
     def residual(j, rows, _):
-        out[:, j, :] = act1[rows, :] + gate(dim, t, v, s, rows)
+        out.near[:, j, :] = act1[rows, :] + gate(dim, t, v, s, rows)
         return 0
 
     each_step(dim, residual, 2)
+    out.flush()
     sums[...] = jnp.zeros((SMALL, dim.H), F32)
     top(dim, t, strided(dim, out_grad), v, s, mixed, xhat, w_gv, w_gg, w_out, dv, dg, dmixed, ds, rcf, rfin, sums,
         ah, al, bh, bl, wh, wl)
@@ -610,6 +655,13 @@
     weight_grad(dim, share, 2, ah, al, bh, bl, tile, keep, send)
 
 
+def k_w2(dim, share, active, dv, dg, states, dmixed, xhat1, dproj1, t, keep, send, ah, al, bh, bl, tile):
+    k_w1(dim, share, active, dv, dg, states, dmixed, keep, send, ah, al, bh, bl, tile)
+    split_rows(dim, lambda rows: xhat1[rows, :] * row(t, GAIN) + row(t, BIAS), ah, al)
+    split_rows(dim, lambda rows: dproj1[rows, :], bh, bl)
+    weight_grad(dim, share, 3, ah, al, bh, bl, tile, keep, send)
+
+
 def k_c1(dim, weights, out_grad, t, t0, ds, rcf, gr, states, en, drive, xhat, rstd, dmixed,
          xhat0, mixed0, v0, s0,
          dproj, dmid, dv0, dg0, dmixed0, ds0, rcf0, rfin0, sums1, sums0, ah, al, bh, bl, wh, wl, adj_en):
@@ -625,21 +677,15 @@
         sums0, ah, al, bh, bl, wh, wl)
 
 
-def k_w2(dim, share, active, dv, dg, states, dmixed, xhat1, dproj1, t, keep, send, ah, al, bh, bl, tile):
-    k_w1(dim, share, active, dv, dg, states, dmixed, keep, send, ah, al, bh, bl, tile)
-    split_rows(dim, lambda rows: xhat1[rows, :] * row(t, GAIN) + row(t, BIAS), ah, al)
-    split_rows(dim, lambda rows: dproj1[rows, :], bh, bl)
-    weight_grad(dim, share, 3, ah, al, bh, bl, tile, keep, send)
-
-
 def k_c0(share, dim, weights, t, ds, rcf, gr, states, en, drive, xhat, rstd, dmixed, dmid, sums1a, sums1b, sums0a,
          input_grad, keep, send, ah, al, bh, bl, wh, wl, adj_en, dproj, buf, sums0, tile):
     def store(steps, rows, value):
         for u, j in enumerate(steps):
-            input_grad[:, j, :] = value[u * dim.R : (u + 1) * dim.R, :]
+            input_grad.near[:, j, :] = value[u * dim.R : (u + 1) * dim.R, :]
 
     bottom(dim, t, ds, rcf, gr, states, en, drive, xhat, rstd, dmixed, weights[0], plain(dmid), store, dproj, buf, adj_en,
            sums0, ah, al, wh, wl)
+    input_grad.flush()
     split_rows(dim, lambda rows: xhat[rows, :] * row(t, GAIN) + row(t, BIAS), bh, bl)
     weight_grad(dim, share, 0, bh, bl, ah, al, tile, keep, send)
     place = lax.broadcasted_iota(jnp.int32, (SMALL, dim.H), 0)
@@ -694,6 +740,30 @@
 def plane_sums(dim, half):
     others = [swap(half[k], "seq", 2 * k) for k in range(1, dim.S // 2)]
     return [sum((o[k] for o in others), half[0][k]) for k in range(dim.D)]
+
+
+def split_half(dim, half):
+    cut = dim.D // 2
+    a, b = [h[:cut] for h in half], [h[cut:] for h in half]
+    return [jnp.stack([a[1], a[3]]), jnp.stack([b[2], b[3]]), a[0], a[2], b[0], b[1]]
+
+
+def two_step_sums(dim, parts):
+    send_a, send_b, a0, a2, b0, b1 = parts
+    got_a, got_b = swap(send_a, "seq", 2), swap(send_b, "seq", 4)
+    far_a, far_b = swap(a2 + got_a[1], "seq", 4), swap(b1 + got_b[1], "seq", 2)
+    a, b = a0 + got_a[0] + far_a, b0 + got_b[0] + far_b
+    cut = dim.D // 2
+    return [a[d] for d in range(cut)] + [b[d] for d in range(dim.D - cut)]
+
+
+def dp_sum_halving(dim, parts):
+    n = dim.D
+    while n > 1:
+        n //= 2
+        got = swap(jnp.stack(parts[n:]), "dp", n)
+        parts = [parts[k] + got[k] for k in range(n)]
+    return parts[0]
 
 
 def dp_sum(dim, parts):
@@ -820,11 +890,12 @@
     stat = pltpu.VMEM((T, 128), F32)
     vec = pltpu.VMEM((SMALL, H), F32)
 
-    def k(fn, names, outs, scratch, *args, us):
+    def k(fn, names, outs, scratch, *args, us, late=(), sinks=()):
         chunks = [c for c, chunk in enumerate(CHUNKS) if set(chunk) & set(names)]
         kernel, count, own = weights_in(dim, chunks, names, fn)
         sources = [in_map, out_map, glu_weight] + [p for c in chunks for p in pieces[c]]
-        return call(kernel, outs, scratch + own, *sources, *args, us=us, anywhere=count)
+        late = [count + i for i in late]
+        return call(kernel, outs, scratch + own, *sources, *args, us=us, anywhere=count, late=late, sinks=sinks)
 
     def carried(fin):
         return lax.all_gather(fin, "seq")
@@ -841,7 +912,7 @@
         [ent, big, big, big, big, big, big, big, stat, big, ent, fins],
         halves(dim, 1),
         x, table0, table1, drive0, cf0, g0, xhat0,
-        us=10.0,
+        us=9.0,
     )
     fin1, chips2 = tie(fin1, chips2)
     g1 = carried(fin1)
@@ -853,7 +924,7 @@
         [f32(R, dim.L, H), ent, big, big, big, big, big, big, ent, fins, vec],
         halves(dim, 2) + spare * 3,
         act1, og, table1, drive1, cf1, g1, xhat1,
-        us=13.0,
+        us=12.5, sinks=[0],
     )
     share1, share2, share3 = Share(dim, 3), Share(dim, 4), Halves(dim)
     tile = [pltpu.VMEM((WIDE, H), F32)]
@@ -872,7 +943,7 @@
         halves(dim, 2) + [pltpu.VMEM((R, H), F32)],
         og, table1, table0, ds1, rcf1, gr1, states1, en1, drive1, xhat1, rstd1, dmixed1,
         xhat0, mixed0, v0, s0,
-        us=11.0,
+        us=9.5,
     )
     keep2, send2 = call(
         functools.partial(k_w2, dim, share2), [f32(*share2.shape)] * 2, pair + tile,
@@ -880,23 +951,25 @@
     )
     rfin0, (send2, *sums1) = tie(rfin0, [send2, *plane_sums(dim, half1)])
     gr0 = carried(rfin0)
-    gr0, half2 = tie(gr0, half_sums(dim, keep2, send2))
+    half2 = half_sums(dim, keep2, send2)
+    two_steps = S == 8
+    gr0, half2 = tie(gr0, split_half(dim, half2) if two_steps else half2)
     input_grad, keep3, send3 = k(
         functools.partial(k_c0, share3),
         [(0, 0)],
         [f32(R, dim.L, H)] + [f32(*share3.shape)] * 2,
         halves(dim, 2) + [pltpu.VMEM((R, H), F32)] + spare * 2 + [pltpu.VMEM((SMALL, H), F32)] + tile,
         table0, ds0, rcf0, gr0, states0, en0, drive0, xhat0, rstd0, dmixed0, dmid, sums1a, sums1b, sums0a,
-        us=7.4,
+        us=6.0, sinks=[0],
     )
-    sums2 = plane_sums(dim, half2)
+    sums2 = two_step_sums(dim, half2) if two_steps else plane_sums(dim, half2)
     got3 = swap(send3, "seq", 1)
-    half3 = [jnp.concatenate([keep3[d] + got3[d], sums1[d]], 0) for d in range(D)]
+    half3 = [keep3[d] + got3[d] for d in range(D)]
     total3 = tree_sum([half3[0]] + [swap(half3[k], "dp", k) for k in range(1, D)])
-    chips3 = chips_gather(dim, total3)
-    joint, chips3 = tie(dp_sum(dim, sums2), chips3)
+    upper1 = dp_sum(dim, sums1)
+    chips3 = chips_gather(dim, jnp.concatenate([total3, upper1], 0))
     last = cores_gather(chips3)
-    upper = plane_gather(dim, joint)
+    upper = plane_gather(dim, dp_sum(dim, sums2))
     kinds = [[(1, "gv"), (1, "gg"), (1, "out")], [(0, "gv"), (0, "gg"), (0, "out"), (1, "in")]]
     grads = unpack(dim, (share1, share2), kinds, share3, last, upper)
     return (out.reshape(inputs.shape), input_grad.reshape(inputs.shape), *grads)

time: 197 us -> 195 us (0.990)
  starting transfers between devices: 53.2 us -> 63.7 us
  waiting for transfers between devices: 44.6 us -> 34.9 us
    ppermute x58 -> x62, starting transfers between devices: 53.2 us -> 63.7 us  [swap(): return lax.ppermute(x, axis, [(i, i ^ mask) for i in range(count)])]
    ppermute x58 -> x62, waiting for transfers between devices: 44.6 us -> 34.9 us  [swap(): return lax.ppermute(x, axis, [(i, i ^ mask) for i in range(count)])]
  transfers between devices with their start and end apart: 58 -> 62, of which waited for: 15 -> 15; matrix products, arithmetic and copies ran while one was open for 0% -> 0% of each run, Pallas kernels for 15% -> 17%
where the time goes in v5:
time: 195 us; the launch traced here: 194 us
  starting transfers between devices  63.7 us (33%)
  Pallas kernels  54.4 us (28%)
  blocking collectives  36.4 us (19%)
  waiting for transfers between devices  34.9 us (18%)
  local copies, waits for them, and re-layouts  1.97 us (1%)
    ppermute x62, starting transfers between devices, swap(): return lax.ppermute(x, axis, [(i, i ^ mask) for i in range(count)])  63.7 us
    pallas_call x11, Pallas kernels, call(): pl.pallas_call(fn, out_shape=outs, in_specs=[pl.BlockSpec(memory_space=sp...  54.4 us
    all_gather x4, blocking collectives, carried(): return lax.all_gather(fin, 'seq')  36.4 us
    ppermute x62, waiting for transfers between devices, swap(): return lax.ppermute(x, axis, [(i, i ^ mask) for i in range(count)])  34.9 us
  transfers between devices with their start and end apart: 62, of which 15 were waited for; matrix products, arithmetic and copies ran while one was open for 0% of the time, Pallas kernels for 17%

profile of v5, /device:TPU:9, one launch (start us, length us, event | category | flops | bytes accessed | tf_op | source)
XLA Modules:
  0.0 194.2 jit_solution(11319969368302614392)
XLA Ops:
  1.9 2.5 %collective-permute-start.1 = (f32[40,512]{1,0:T(8,128)S(1)}, f32[40,512]{1,0:T(8,128)S(1)}, u32[]{:S(2)}, u32[]{:S(2)}) collective-permute-start(f32[40,512]{1,0:T(8,128)S(1)} %get-tuple-element.109), channel_id=1, source_target_pairs={{0,16},{8,24},{16,0},{24,8},{1,17},{9,25},{17,1},{25,9},{2,18},{10... | collective-permute-start | bytes 245768 | tf_op jit(solution)/shard_map/ppermute | solution.py:714
  5.2 2.5 %collective-permute-done.1 = f32[40,512]{1,0:T(8,128)S(1)} collective-permute-done((f32[40,512]{1,0:T(8,128)S(1)}, f32[40,512]{1,0:T(8,128)S(1)}, u32[]{:S(2)}, u32[]{:S(2)}) %collective-permute-start.1) | collective-permute-done | bytes 81952 | tf_op jit(solution)/shard_map/ppermute | solution.py:714
  7.7 3.9 %collective-permute-done.2 = f32[40,512]{1,0:T(8,128)S(1)} collective-permute-done((f32[40,512]{1,0:T(8,128)S(1)}, f32[40,512]{1,0:T(8,128)S(1)}, u32[]{:S(2)}, u32[]{:S(2)}) %collective-permute-start.2) | collective-permute-done | bytes 81952 | tf_op jit(solution)/shard_map/ppermute | solution.py:714
  11.6 2.3 %collective-permute-start.4 = (f32[56,512]{1,0:T(8,128)S(1)}, f32[56,512]{1,0:T(8,128)S(1)}, u32[]{:S(2)}, u32[]{:S(2)}) collective-permute-start(f32[56,512]{1,0:T(8,128)S(1)} %get-tuple-element.110), channel_id=1, source_target_pairs={{0,16},{8,24},{16,0},{24,8},{1,17},{9,25},{17,1},{25,9},{2,18},{10... | collective-permute-start | bytes 344072 | tf_op jit(solution)/shard_map/ppermute | solution.py:714
  17.7 6.4 %collective-permute-done.5 = f32[56,512]{1,0:T(8,128)S(1)} collective-permute-done((f32[56,512]{1,0:T(8,128)S(1)}, f32[56,512]{1,0:T(8,128)S(1)}, u32[]{:S(2)}, u32[]{:S(2)}) %collective-permute-start.5) | collective-permute-done | bytes 114720 | tf_op jit(solution)/shard_map/ppermute | solution.py:714
  24.7 4.0 %collective-permute-start.10 = (f32[2,3,16,512]{3,2,1,0:T(8,128)S(1)}, f32[2,3,16,512]{3,2,1,0:T(8,128)S(1)}, u32[]{:S(2)}, u32[]{:S(2)}) collective-permute-start(f32[2,3,16,512]{3,2,1,0:T(8,128)S(1)} %collective-permute-done.6.refs_5_), channel_id=1, source_target_pairs={{0,1},{1,0},{2,3},{3,2},{4,5},{5,4},{6,7},{7,6},{8,9},{9,8},{10,11... | collective-permute-start | bytes 589832 | tf_op jit(solution)/shard_map/ppermute | solution.py:714
  29.8 2.3 %collective-permute-start.12 = (f32[2,3,16,512]{3,2,1,0:T(8,128)S(1)}, f32[2,3,16,512]{3,2,1,0:T(8,128)S(1)}, u32[]{:S(2)}, u32[]{:S(2)}) collective-permute-start(f32[2,3,16,512]{3,2,1,0:T(8,128)S(1)} %collective-permute-done.8.refs_9_), channel_id=1, source_target_pairs={{0,1},{1,0},{2,3},{3,2},{4,5},{5,4},{6,7},{7,6},{8,9},{9,8},{10,11... | collective-permute-start | bytes 589832 | tf_op jit(solution)/shard_map/ppermute | solution.py:714
  36.1 2.8 %shard_map.214 = (f32[512,512]{1,0:T(8,128)S(1)}, f32[512,128]{1,0:T(8,128)S(1)}, f32[512,512]{1,0:T(8,128)S(1)}, f32[16,512]{1,0:T(8,128)S(1)}, f32[2,512]{1,0:T(2,128)S(1)}) custom-call(f32[2,128,512]{2,1,0:T(8,128)} %refs_0_.9, f32[2,128,512]{2,1,0:T(8,128)} %refs_1_.9, f32[2,128,1024]{2,1,0:T(8,128)} %refs_2_.9, f32[2,3,16,512]{3,2,1,0:T(8,128)} %copy-done.2, ...), custom_call_target="tpu_custom_call" | custom-call | flops 1 | bytes 12240000 | tf_op jit(solution)/shard_map/pallas_call | solution.py:439
  38.9 9.7 %all-gather.4.refs_24_ = f32[8,2,512]{2,1,0:T(2,128)S(1)} all-gather(f32[1,2,512]{2,1,0:T(2,128)S(1)} %bitcast.97), channel_id=2, replica_groups=mesh['dp'=4,'seq'=8] {'seq'}, dimensions={0}, use_global_device_ids=true | all-gather | bytes 36864 | tf_op jit(solution)/shard_map/all_gather | solution.py:901
  53.1 9.3 %shard_map.215 = (f32[16,512]{1,0:T(8,128)S(1)}, f32[512,512]{1,0:T(8,128)S(1)}, f32[512,512]{1,0:T(8,128)S(1)}, f32[512,512]{1,0:T(8,128)S(1)}, f32[512,512]{1,...) custom-call(f32[2,128,512]{2,1,0:T(8,128)} %refs_0_.9, ...), custom_call_target="tpu_custom_call" | custom-call | flops 1 | bytes 32400000 | tf_op jit(solution)/shard_map/pallas_call | solution.py:439
  62.4 2.3 %collective-permute-done.24.refs_9_ = f32[3,3,16,512]{3,2,1,0:T(8,128)S(1)} collective-permute-done((f32[3,3,16,512]{3,2,1,0:T(8,128)S(1)}, f32[3,3,16,512]{3,2,1,0:T(8,128)S(1)}, u32[]{:S(2)}, u32[]{:S(2)}) %collective-permute-start.24) | collective-permute-done | bytes 294944 | tf_op jit(solution)/shard_map/ppermute | solution.py:714
  66.5 9.0 %all-gather.5.refs_16_ = f32[8,2,512]{2,1,0:T(2,128)S(1)} all-gather(f32[1,2,512]{2,1,0:T(2,128)S(1)} %bitcast.95), channel_id=3, replica_groups=mesh['dp'=4,'seq'=8] {'seq'}, dimensions={0}, use_global_device_ids=true | all-gather | bytes 36864 | tf_op jit(solution)/shard_map/all_gather | solution.py:901
  76.5 12.5 %shard_map.216 = (f32[16,32,512]{2,1,0:T(8,128)}, f32[16,512]{1,0:T(8,128)S(1)}, f32[512,512]{1,0:T(8,128)S(1)}, f32[512,512]{1,0:T(8,128)S(1)}, f32[512,512]{1,...) custom-call(f32[2,128,512]{2,1,0:T(8,128)} %refs_0_.9, ...), custom_call_target="tpu_custom_call" | custom-call | flops 1 | bytes 45000000 | tf_op jit(solution)/shard_map/pallas_call | solution.py:439
  89.0 4.9 %shard_map.217 = (f32[4,4,48,512]{3,2,1,0:T(8,128)S(1)}, f32[4,4,48,512]{3,2,1,0:T(8,128)S(1)}) custom-call(f32[512,512]{1,0:T(8,128)S(1)} %get-tuple-element.142.active, f32[512,512]{1,0:T(8,128)S(1)} %get-tuple-element.143.dv, f32[512,512]{1,0:T(8,128)S(1)} %get-tuple-element.144.dg, f32[512,512]{1,0:T(8,128)S(1)} %get-tuple-element.145.states.refs_25_, ...), custom_call_target="tpu_custom_call" | custom-call | flops 1 | bytes 18000000 | tf_op jit(solution)/shard_map/pallas_call | solution.py:439
  94.1 8.9 %all-gather.6.refs_24_ = f32[8,2,512]{2,1,0:T(2,128)S(1)} all-gather(f32[1,2,512]{2,1,0:T(2,128)S(1)} %bitcast.96), channel_id=4, replica_groups=mesh['dp'=4,'seq'=8] {'seq'}, dimensions={0}, use_global_device_ids=true | all-gather | bytes 36864 | tf_op jit(solution)/shard_map/all_gather | solution.py:901
  106.1 9.9 %shard_map.218 = (f32[512,512]{1,0:T(8,128)S(1)}, f32[512,512]{1,0:T(8,128)S(1)}, f32[512,512]{1,0:T(8,128)S(1)}, f32[512,512]{1,0:T(8,128)S(1)}, f32[512,512]{1...) custom-call(f32[2,128,512]{2,1,0:T(8,128)} %refs_0_.9, ...), custom_call_target="tpu_custom_call" | custom-call | flops 1 | bytes 34200000 | tf_op jit(solution)/shard_map/pallas_call | solution.py:439
  116.0 6.4 %shard_map.219 = (f32[4,4,64,512]{3,2,1,0:T(8,128)S(1)}, f32[4,4,64,512]{3,2,1,0:T(8,128)S(1)}) custom-call(f32[512,512]{1,0:T(8,128)S(1)} %get-tuple-element.160.active, f32[512,512]{1,0:T(8,128)S(1)} %get-tuple-element.161.dv, f32[512,512]{1,0:T(8,128)S(1)} %get-tuple-element.162.dg, f32[512,512]{1,0:T(8,128)S(1)} %get-tuple-element.163.states.refs_15_, ...), custom_call_target="tpu_custom_call" | custom-call | flops 1 | bytes 23040000 | tf_op jit(solution)/shard_map/pallas_call | solution.py:439
  124.2 8.8 %all-gather.7.refs_14_ = f32[8,2,512]{2,1,0:T(2,128)S(1)} all-gather(f32[1,2,512]{2,1,0:T(2,128)S(1)} %bitcast.94), channel_id=5, replica_groups=mesh['dp'=4,'seq'=8] {'seq'}, dimensions={0}, use_global_device_ids=true | all-gather | bytes 36864 | tf_op jit(solution)/shard_map/all_gather | solution.py:901
  137.9 5.3 %shard_map.220 = (f32[16,32,512]{2,1,0:T(8,128)}, f32[4,72,512]{2,1,0:T(8,128)S(1)}, f32[4,72,512]{2,1,0:T(8,128)S(1)}) custom-call(f32[2,128,512]{2,1,0:T(8,128)} %refs_0_.9, f32[2,128,512]{2,1,0:T(8,128)} %refs_1_.9, f32[2,128,1024]{2,1,0:T(8,128)} %refs_2_.9, f32[2,3,16,512]{3,2,1,0:T(8,128)} %copy-done.2, f32[2,3,16,512]{3,2,1,0:T(8,128)} %copy-done.9, ...), custom_call_target="tpu_custom_call" | custom-call | flops 1 | bytes 21600000 | tf_op jit(solution)/shard_map/pallas_call | solution.py:439
  153.0 2.6 %collective-permute-done.49 = f32[2,64,512]{2,1,0:T(8,128)S(1)} collective-permute-done((f32[2,64,512]{2,1,0:T(8,128)S(1)}, f32[2,64,512]{2,1,0:T(8,128)S(1)}, u32[]{:S(2)}, u32[]{:S(2)}) %collective-permute-start.49) | collective-permute-done | bytes 262176 | tf_op jit(solution)/shard_map/ppermute | solution.py:714
  158.6 3.6 %collective-permute-done.37 = f32[72,512]{1,0:T(8,128)S(1)} collective-permute-done((f32[72,512]{1,0:T(8,128)S(1)}, f32[72,512]{1,0:T(8,128)S(1)}, u32[]{:S(2)}, u32[]{:S(2)}) %collective-permute-start.37) | collective-permute-done | bytes 147488 | tf_op jit(solution)/shard_map/ppermute | solution.py:714
  165.0 7.4 %collective-permute-done.53 = f32[64,512]{1,0:T(8,128)S(1)} collective-permute-done((f32[64,512]{1,0:T(8,128)S(1)}, f32[64,512]{1,0:T(8,128)S(1)}, u32[]{:S(2)}, u32[]{:S(2)}) %collective-permute-start.53) | collective-permute-done | bytes 131104 | tf_op jit(solution)/shard_map/ppermute | solution.py:714
  172.4 6.1 %collective-permute-start.41 = (f32[120,512]{1,0:T(8,128)S(1)}, f32[120,512]{1,0:T(8,128)S(1)}, u32[]{:S(2)}, u32[]{:S(2)}) collective-permute-start(f32[120,512]{1,0:T(8,128)S(1)} %pad_maximum_fusion.4.refs_0_), channel_id=1, source_target_pairs={{0,1},{1,0},{2,3},{3,2},{4,5},{5,4},{6,7},{7,6},{8,9},{9,8},{10,11... | collective-permute-start | bytes 737288 | tf_op jit(solution)/shard_map/ppermute | solution.py:714
  181.2 5.1 %collective-permute-start.55 = (f32[64,512]{1,0:T(8,128)S(1)}, f32[64,512]{1,0:T(8,128)S(1)}, u32[]{:S(2)}, u32[]{:S(2)}) collective-permute-start(f32[64,512]{1,0:T(8,128)S(1)} %fusion.18.refs_8_), channel_id=1, source_target_pairs={{0,1},{1,0},{2,3},{3,2},{4,5},{5,4},{6,7},{7,6},{8,9},{9,8},{10,11... | collective-permute-start | bytes 393224 | tf_op jit(solution)/shard_map/ppermute | solution.py:714
  (199 shorter events, 54.5 us)
Async XLA Ops:
  13.9 10.3 %collective-permute-start.5 = (f32[56,512]{1,0:T(8,128)S(1)}, f32[56,512]{1,0:T(8,128)S(1)}, u32[]{:S(2)}, u32[]{:S(2)}) collective-permute-start(f32[56,512]{1,0:T(8,128)S(1)} %get-tuple-element.110), channel_id=1, source_target_pairs={{0,24},{8,16},{16,8},{24,0},{1,25},{9,17},{17,9},{25,1},{2,26},{10... | collective-permute-start | bytes 344072 | tf_op jit(solution)/shard_map/ppermute | solution.py:714
  28.7 20.0 %collective-permute-start.14 = (f32[3,3,16,512]{3,2,1,0:T(8,128)S(1)}, f32[3,3,16,512]{3,2,1,0:T(8,128)S(1)}, u32[]{:S(2)}, u32[]{:S(2)}) collective-permute-start(f32[3,3,16,512]{3,2,1,0:T(8,128)S(1)} %pad_maximum_fusion.2.refs_11_), channel_id=1, source_target_pairs={{0,2},{1,3},{2,0},{3,1},{4,6},{5,7},{6,4},{7,5},{8,10},{9,11},{10,... | collective-permute-start | bytes 884744 | tf_op jit(solution)/shard_map/ppermute | solution.py:714
  29.2 19.6 %collective-permute-start.16 = (f32[3,3,16,512]{3,2,1,0:T(8,128)S(1)}, f32[3,3,16,512]{3,2,1,0:T(8,128)S(1)}, u32[]{:S(2)}, u32[]{:S(2)}) collective-permute-start(f32[3,3,16,512]{3,2,1,0:T(8,128)S(1)} %pad_maximum_fusion.2.refs_11_), channel_id=1, source_target_pairs={{0,4},{1,5},{2,6},{3,7},{4,0},{5,1},{6,2},{7,3},{8,12},{9,13},{10,... | collective-permute-start | bytes 884744 | tf_op jit(solution)/shard_map/ppermute | solution.py:714
  32.2 17.0 %collective-permute-start.21 = (f32[2,48,512]{2,1,0:T(8,128)S(1)}, f32[2,48,512]{2,1,0:T(8,128)S(1)}, u32[]{:S(2)}, u32[]{:S(2)}) collective-permute-start(f32[2,48,512]{2,1,0:T(8,128)S(1)} %pad_maximum_fusion.6), channel_id=1, source_target_pairs={{0,16},{8,24},{16,0},{24,8},{1,17},{9,25},{17,1},{25,9},{2,18},{10... | collective-permute-start | bytes 589832 | tf_op jit(solution)/shard_map/ppermute | solution.py:714
  34.1 15.2 %collective-permute-start.18 = (f32[3,3,16,512]{3,2,1,0:T(8,128)S(1)}, f32[3,3,16,512]{3,2,1,0:T(8,128)S(1)}, u32[]{:S(2)}, u32[]{:S(2)}) collective-permute-start(f32[3,3,16,512]{3,2,1,0:T(8,128)S(1)} %pad_maximum_fusion.2.refs_11_), channel_id=1, source_target_pairs={{0,6},{1,7},{2,4},{3,5},{4,2},{5,3},{6,0},{7,1},{8,14},{9,15},{10,... | collective-permute-start | bytes 884744 | tf_op jit(solution)/shard_map/ppermute | solution.py:714
  35.1 15.0 %collective-permute-start.13 = (f32[3,3,16,512]{3,2,1,0:T(8,128)S(1)}, f32[3,3,16,512]{3,2,1,0:T(8,128)S(1)}, u32[]{:S(2)}, u32[]{:S(2)}) collective-permute-start(f32[3,3,16,512]{3,2,1,0:T(8,128)S(1)} %pad_maximum_fusion.2.refs_11_), channel_id=1, source_target_pairs={{0,1},{1,0},{2,3},{3,2},{4,5},{5,4},{6,7},{7,6},{8,9},{9,8},{10,11... | collective-permute-start | bytes 884744 | tf_op jit(solution)/shard_map/ppermute | solution.py:714
  49.5 12.9 %collective-permute-start.22 = (f32[3,3,16,512]{3,2,1,0:T(8,128)S(1)}, f32[3,3,16,512]{3,2,1,0:T(8,128)S(1)}, u32[]{:S(2)}, u32[]{:S(2)}) collective-permute-start(f32[3,3,16,512]{3,2,1,0:T(8,128)S(1)} %pad_maximum_fusion.3.refs_3_), channel_id=1, source_target_pairs={{0,2},{1,3},{2,0},{3,1},{4,6},{5,7},{6,4},{7,5},{8,10},{9,11},{10,... | collective-permute-start | bytes 884744 | tf_op jit(solution)/shard_map/ppermute | solution.py:714
  50.1 12.3 %collective-permute-start.23 = (f32[3,3,16,512]{3,2,1,0:T(8,128)S(1)}, f32[3,3,16,512]{3,2,1,0:T(8,128)S(1)}, u32[]{:S(2)}, u32[]{:S(2)}) collective-permute-start(f32[3,3,16,512]{3,2,1,0:T(8,128)S(1)} %pad_maximum_fusion.3.refs_3_), channel_id=1, source_target_pairs={{0,4},{1,5},{2,6},{3,7},{4,0},{5,1},{6,2},{7,3},{8,12},{9,13},{10,... | collective-permute-start | bytes 884744 | tf_op jit(solution)/shard_map/ppermute | solution.py:714
  50.8 13.9 %collective-permute-start.24 = (f32[3,3,16,512]{3,2,1,0:T(8,128)S(1)}, f32[3,3,16,512]{3,2,1,0:T(8,128)S(1)}, u32[]{:S(2)}, u32[]{:S(2)}) collective-permute-start(f32[3,3,16,512]{3,2,1,0:T(8,128)S(1)} %pad_maximum_fusion.3.refs_3_), channel_id=1, source_target_pairs={{0,6},{1,7},{2,4},{3,5},{4,2},{5,3},{6,0},{7,1},{8,14},{9,15},{10,... | collective-permute-start | bytes 884744 | tf_op jit(solution)/shard_map/ppermute | solution.py:714
  64.7 10.8 %collective-permute-start.25 = (f32[3,3,16,512]{3,2,1,0:T(8,128)S(1)}, f32[3,3,16,512]{3,2,1,0:T(8,128)S(1)}, u32[]{:S(2)}, u32[]{:S(2)}) collective-permute-start(f32[3,3,16,512]{3,2,1,0:T(8,128)S(1)} %pad_maximum_fusion.3.refs_3_), channel_id=1, source_target_pairs={{0,1},{1,0},{2,3},{3,2},{4,5},{5,4},{6,7},{7,6},{8,9},{9,8},{10,11... | collective-permute-start | bytes 884744 | tf_op jit(solution)/shard_map/ppermute | solution.py:714
  103.4 19.0 %collective-permute-start.30 = (f32[4,48,512]{2,1,0:T(8,128)S(1)}, f32[4,48,512]{2,1,0:T(8,128)S(1)}, u32[]{:S(2)}, u32[]{:S(2)}) collective-permute-start(f32[4,48,512]{2,1,0:T(8,128)S(1)} %get-tuple-element.168), channel_id=1, source_target_pairs={{0,2},{1,3},{2,0},{3,1},{4,6},{5,7},{6,4},{7,5},{8,10},{9,11},{10,... | collective-permute-start | bytes 1179656 | tf_op jit(solution)/shard_map/ppermute | solution.py:714
  104.0 18.4 %collective-permute-start.31 = (f32[4,48,512]{2,1,0:T(8,128)S(1)}, f32[4,48,512]{2,1,0:T(8,128)S(1)}, u32[]{:S(2)}, u32[]{:S(2)}) collective-permute-start(f32[4,48,512]{2,1,0:T(8,128)S(1)} %get-tuple-element.169), channel_id=1, source_target_pairs={{0,4},{1,5},{2,6},{3,7},{4,0},{5,1},{6,2},{7,3},{8,12},{9,13},{10,... | collective-permute-start | bytes 1179656 | tf_op jit(solution)/shard_map/ppermute | solution.py:714
  104.9 17.8 %collective-permute-start.32 = (f32[4,48,512]{2,1,0:T(8,128)S(1)}, f32[4,48,512]{2,1,0:T(8,128)S(1)}, u32[]{:S(2)}, u32[]{:S(2)}) collective-permute-start(f32[4,48,512]{2,1,0:T(8,128)S(1)} %get-tuple-element.170), channel_id=1, source_target_pairs={{0,6},{1,7},{2,4},{3,5},{4,2},{5,3},{6,0},{7,1},{8,14},{9,15},{10,... | collective-permute-start | bytes 1179656 | tf_op jit(solution)/shard_map/ppermute | solution.py:714
  122.9 10.1 %collective-permute-start.33 = (f32[4,4,64,512]{3,2,1,0:T(8,128)S(1)}, f32[4,4,64,512]{3,2,1,0:T(8,128)S(1)}, u32[]{:S(2)}, u32[]{:S(2)}) collective-permute-start(f32[4,4,64,512]{3,2,1,0:T(8,128)S(1)} %get-tuple-element.173), channel_id=1, source_target_pairs={{0,1},{1,0},{2,3},{3,2},{4,5},{5,4},{6,7},{7,6},{8,9},{9,8},{10,11... | collective-permute-start | bytes 6291464 | tf_op jit(solution)/shard_map/ppermute | solution.py:714
  133.7 13.4 %collective-permute-start.48 = (f32[2,2,64,512]{3,2,1,0:T(8,128)S(1)}, f32[2,2,64,512]{3,2,1,0:T(8,128)S(1)}, u32[]{:S(2)}, u32[]{:S(2)}) collective-permute-start(f32[2,2,64,512]{3,2,1,0:T(8,128)S(1)} %pad_maximum_fusion), channel_id=1, source_target_pairs={{0,2},{1,3},{2,0},{3,1},{4,6},{5,7},{6,4},{7,5},{8,10},{9,11},{10,... | collective-permute-start | bytes 1572872 | tf_op jit(solution)/shard_map/ppermute | solution.py:714
  134.9 10.0 %collective-permute-start.39 = (f32[48,512]{1,0:T(8,128)S(1)}, f32[48,512]{1,0:T(8,128)S(1)}, u32[]{:S(2)}, u32[]{:S(2)}) collective-permute-start(f32[48,512]{1,0:T(8,128)S(1)} %get-tuple-element.186), channel_id=1, source_target_pairs={{0,16},{8,24},{16,0},{24,8},{1,17},{9,25},{17,1},{25,9},{2,18},{10... | collective-permute-start | bytes 294920 | tf_op jit(solution)/shard_map/ppermute | solution.py:714
  137.0 12.1 %collective-permute-start.51 = (f32[2,2,64,512]{3,2,1,0:T(8,128)S(1)}, f32[2,2,64,512]{3,2,1,0:T(8,128)S(1)}, u32[]{:S(2)}, u32[]{:S(2)}) collective-permute-start(f32[2,2,64,512]{3,2,1,0:T(8,128)S(1)} %pad_maximum_fusion.1), channel_id=1, source_target_pairs={{0,4},{1,5},{2,6},{3,7},{4,0},{5,1},{6,2},{7,3},{8,12},{9,13},{10,... | collective-permute-start | bytes 1572872 | tf_op jit(solution)/shard_map/ppermute | solution.py:714
  156.4 16.0 %collective-permute-start.53 = (f32[64,512]{1,0:T(8,128)S(1)}, f32[64,512]{1,0:T(8,128)S(1)}, u32[]{:S(2)}, u32[]{:S(2)}) collective-permute-start(f32[64,512]{1,0:T(8,128)S(1)} %get-tuple-element.227), channel_id=1, source_target_pairs={{0,16},{8,24},{16,0},{24,8},{1,17},{9,25},{17,1},{25,9},{2,18},{10... | collective-permute-start | bytes 393224 | tf_op jit(solution)/shard_map/ppermute | solution.py:714
  158.2 20.3 %collective-permute-start.54 = (f32[64,512]{1,0:T(8,128)S(1)}, f32[64,512]{1,0:T(8,128)S(1)}, u32[]{:S(2)}, u32[]{:S(2)}) collective-permute-start(f32[64,512]{1,0:T(8,128)S(1)} %get-tuple-element.228), channel_id=1, source_target_pairs={{0,24},{8,16},{16,8},{24,0},{1,25},{9,17},{17,9},{25,1},{2,26},{10... | collective-permute-start | bytes 393224 | tf_op jit(solution)/shard_map/ppermute | solution.py:714
  162.3 16.8 %collective-permute-start.42 = (f32[120,512]{1,0:T(8,128)S(1)}, f32[120,512]{1,0:T(8,128)S(1)}, u32[]{:S(2)}, u32[]{:S(2)}) collective-permute-start(f32[120,512]{1,0:T(8,128)S(1)} %pad_maximum_fusion.4.refs_0_), channel_id=1, source_target_pairs={{0,2},{1,3},{2,0},{3,1},{4,6},{5,7},{6,4},{7,5},{8,10},{9,11},{10,... | collective-permute-start | bytes 737288 | tf_op jit(solution)/shard_map/ppermute | solution.py:714
  162.9 17.1 %collective-permute-start.44 = (f32[120,512]{1,0:T(8,128)S(1)}, f32[120,512]{1,0:T(8,128)S(1)}, u32[]{:S(2)}, u32[]{:S(2)}) collective-permute-start(f32[120,512]{1,0:T(8,128)S(1)} %pad_maximum_fusion.4.refs_0_), channel_id=1, source_target_pairs={{0,4},{1,5},{2,6},{3,7},{4,0},{5,1},{6,2},{7,3},{8,12},{9,13},{10,... | collective-permute-start | bytes 737288 | tf_op jit(solution)/shard_map/ppermute | solution.py:714
  163.8 17.4 %collective-permute-start.46 = (f32[120,512]{1,0:T(8,128)S(1)}, f32[120,512]{1,0:T(8,128)S(1)}, u32[]{:S(2)}, u32[]{:S(2)}) collective-permute-start(f32[120,512]{1,0:T(8,128)S(1)} %pad_maximum_fusion.4.refs_0_), channel_id=1, source_target_pairs={{0,6},{1,7},{2,4},{3,5},{4,2},{5,3},{6,0},{7,1},{8,14},{9,15},{10,... | collective-permute-start | bytes 737288 | tf_op jit(solution)/shard_map/ppermute | solution.py:714
  172.4 15.6 %collective-permute-start.41 = (f32[120,512]{1,0:T(8,128)S(1)}, f32[120,512]{1,0:T(8,128)S(1)}, u32[]{:S(2)}, u32[]{:S(2)}) collective-permute-start(f32[120,512]{1,0:T(8,128)S(1)} %pad_maximum_fusion.4.refs_0_), channel_id=1, source_target_pairs={{0,1},{1,0},{2,3},{3,2},{4,5},{5,4},{6,7},{7,6},{8,9},{9,8},{10,11... | collective-permute-start | bytes 737288 | tf_op jit(solution)/shard_map/ppermute | solution.py:714
  180.1 10.2 %collective-permute-start.60 = (f32[64,512]{1,0:T(8,128)S(1)}, f32[64,512]{1,0:T(8,128)S(1)}, u32[]{:S(2)}, u32[]{:S(2)}) collective-permute-start(f32[64,512]{1,0:T(8,128)S(1)} %fusion.18.refs_8_), channel_id=1, source_target_pairs={{0,6},{1,7},{2,4},{3,5},{4,2},{5,3},{6,0},{7,1},{8,14},{9,15},{10,... | collective-permute-start | bytes 393224 | tf_op jit(solution)/shard_map/ppermute | solution.py:714
  (64 other events, 466.5 us)

commit v6 on v5

--- a/solution.py
+++ b/solution.py
@@ -191,7 +191,7 @@
     return th
 
 
-def back(dim, table, drive, cf, g, xhat, w_out, w_gv, w_gg, en, states, mixed, active, v, s, ah, al, wh, wl):
+def back(dim, table, drive, cf, g, xhat, w_out, w_gv, w_gg, en, states, mixed, v, s, sh, sl, ch, cl, wh, wl):
     entries_of(dim, table, cf, g, en, False)
     lr, li = lam_of(dim, table, LAM, False)
     lr = jnp.broadcast_to(lr, (dim.R, dim.N))
@@ -202,27 +202,26 @@
         mr, mi = cmul(lr, li, *carry)
         both = jnp.concatenate([mr + d[:, : dim.N], mi + d[:, dim.N :]], 1)
         states[rows, :] = both
-        ah[rows, :], al[rows, :] = split(both)
+        sh[rows, :], sl[rows, :] = split(both)
         return both[:, : dim.N], both[:, dim.N :]
 
     each_step(dim, scan, 4, False, (en[:, : dim.N], en[:, dim.N :]))
     w_out.fill(wh, wl)
-    product(ah, al, wh, wl, mixed)
+    product(sh, sl, wh, wl, mixed)
 
     def gelu(j, rows, _):
         normed = xhat[rows, :] * row(table, GAIN) + row(table, BIAS)
         m = mixed[rows, :] + row(table, SKIP) * normed
         mixed[rows, :] = m
         a = (0.5 * m) * (1.0 + gelu_parts(m))
-        active[rows, :] = a
-        ah[rows, :], al[rows, :] = split(a)
+        ch[rows, :], cl[rows, :] = split(a)
         return 0
 
     each_step(dim, gelu, 4)
     w_gv.fill(wh, wl)
-    product(ah, al, wh, wl, v)
+    product(ch, cl, wh, wl, v)
     w_gg.fill(wh, wl)
-    product(ah, al, wh, wl, s)
+    product(ch, cl, wh, wl, s)
 
 
 def gate(dim, table, v, s, rows):
@@ -233,14 +232,12 @@
     return vv * ss
 
 
-def top(dim, table, load_dact, v, s, mixed, xhat, w_gv, w_gg, w_out, dv, dg, dmixed, ds, rcf, rfin, sums, ah, al, bh, bl, wh, wl):
+def top(dim, table, load_dact, v, s, mixed, xhat, w_gv, w_gg, w_out, dmixed, ds, rcf, rfin, sums, ah, al, bh, bl, mh, ml, wh, wl):
     def dgate(j, rows, carry):
         dact = load_dact(j, rows)
         ss, vv = s[rows, :], v[rows, :]
         a = dact * ss
         b = a * vv * (1.0 - ss)
-        dv[rows, :] = a
-        dg[rows, :] = b
         ah[rows, :], al[rows, :] = split(a)
         bh[rows, :], bl[rows, :] = split(b)
         return carry[0] + a, carry[1] + b
@@ -260,17 +257,17 @@
         slope = 0.5 * (1.0 + th) + (0.5 * m) * (1.0 - th * th) * (GELU_C * (1.0 + (3 * 0.044715) * (m * m)))
         d = dmixed[rows, :] * slope
         dmixed[rows, :] = d
-        ah[rows, :], al[rows, :] = split(d)
+        mh[rows, :], ml[rows, :] = split(d)
         normed = xhat[rows, :] * row(table, GAIN) + row(table, BIAS)
         return carry + d * normed
 
     sums[SKIP : SKIP + 1, :] = jnp.sum(each_step(dim, dgelu, 2, False, zero), 0, keepdims=True)
     w_out.fill(wh, wl)
-    product(ah, al, wh, wl, ds, True)
+    product(mh, ml, wh, wl, ds, True)
     local_finals(dim, table, ds, rcf, rfin, True)
 
 
-def bottom(dim, table, ds, rcf, gr, states, en, drive, xhat, rstd, dmixed, w_in, load_dact, store, dproj, buf, adj_en, sums, ah, al, wh, wl):
+def bottom(dim, table, ds, rcf, gr, states, en, drive, xhat, rstd, dmixed, w_in, load_dact, store, buf, adj_en, sums, ah, al, wh, wl):
     entries_of(dim, table, rcf, gr, adj_en, True)
     lr, li = lam_of(dim, table, LAM, True)
     lr = jnp.broadcast_to(lr, (dim.R, dim.N))
@@ -290,7 +287,6 @@
         u = drive[rows, :]
         dgam = dgam + (ar * u[:, : dim.N] + ai * u[:, dim.N :])
         dp = jnp.concatenate([ar, ai], 1) * row(table, GAMMA)
-        dproj[rows, :] = dp
         ah[rows, :], al[rows, :] = split(dp)
         return ar, ai, dr, di, dgam
 
@@ -450,10 +446,6 @@
 
 def f32(*shape):
     return jax.ShapeDtypeStruct(shape, F32)
-
-
-def halves(dim, n):
-    return [pltpu.VMEM((dim.T, dim.H), BF16)] * (2 * n) + [pltpu.VMEM((dim.H, dim.H), BF16)] * 2
 
 
 def prep_kernel(dim, small, table):
@@ -611,14 +603,14 @@
     return lambda j, rows: ref[rows, :]
 
 
-def k_a0(dim, weights, x, table, xhat, rstd, drive, cf, fin, ah, al, wh, wl):
-    front(dim, strided(dim, x), table, weights[0], xhat, rstd, drive, cf, fin, ah, al, wh, wl)
+def k_a0(dim, weights, x, table, xhat, rstd, drive, cf, fin, nh, nl, wh, wl):
+    front(dim, strided(dim, x), table, weights[0], xhat, rstd, drive, cf, fin, nh, nl, wh, wl)
 
 
 def k_b0(dim, weights, x, t, t1, drive, cf, g, xhat,
-         en, states, mixed, active, v, s, act1, xhat1, rstd1, drive1, cf1, fin1, ah, al, wh, wl):
+         en, states, mixed, v, s, sh, sl, ch, cl, act1, xhat1, rstd1, drive1, cf1, fin1, nh, nl, wh, wl):
     w_out, w_gv, w_gg, w_in1 = weights
-    back(dim, t, drive, cf, g, xhat, w_out, w_gv, w_gg, en, states, mixed, active, v, s, ah, al, wh, wl)
+    back(dim, t, drive, cf, g, xhat, w_out, w_gv, w_gg, en, states, mixed, v, s, sh, sl, ch, cl, wh, wl)
     load = strided(dim, x)
 
     def residual(steps, rows):
@@ -626,13 +618,13 @@
         act1[rows, :] = act
         return act
 
-    front(dim, residual, t1, w_in1, xhat1, rstd1, drive1, cf1, fin1, ah, al, wh, wl)
+    front(dim, residual, t1, w_in1, xhat1, rstd1, drive1, cf1, fin1, nh, nl, wh, wl)
 
 
 def k_b1(dim, weights, act1, out_grad, t, drive, cf, g, xhat,
-         out, en, states, active, dv, dg, dmixed, ds, rcf, rfin, sums, ah, al, bh, bl, wh, wl, mixed, v, s):
+         out, en, states, dmixed, ds, rcf, rfin, sums, sh, sl, ch, cl, dvh, dvl, dgh, dgl, mh, ml, wh, wl, mixed, v, s):
     w_out, w_gv, w_gg = weights
-    back(dim, t, drive, cf, g, xhat, w_out, w_gv, w_gg, en, states, mixed, active, v, s, ah, al, wh, wl)
+    back(dim, t, drive, cf, g, xhat, w_out, w_gv, w_gg, en, states, mixed, v, s, sh, sl, ch, cl, wh, wl)
 
     def residual(j, rows, _):
         out.near[:, j, :] = act1[rows, :] + gate(dim, t, v, s, rows)
@@ -641,53 +633,45 @@
     each_step(dim, residual, 2)
     out.flush()
     sums[...] = jnp.zeros((SMALL, dim.H), F32)
-    top(dim, t, strided(dim, out_grad), v, s, mixed, xhat, w_gv, w_gg, w_out, dv, dg, dmixed, ds, rcf, rfin, sums,
-        ah, al, bh, bl, wh, wl)
-
-
-def k_w1(dim, share, active, dv, dg, states, dmixed, keep, send, ah, al, bh, bl, tile):
-    split_rows(dim, lambda rows: active[rows, :], ah, al)
-    for m, ref in ((0, dv), (1, dg)):
-        split_rows(dim, lambda rows: ref[rows, :], bh, bl)
+    top(dim, t, strided(dim, out_grad), v, s, mixed, xhat, w_gv, w_gg, w_out, dmixed, ds, rcf, rfin, sums,
+        dvh, dvl, dgh, dgl, mh, ml, wh, wl)
+
+
+def k_w1(dim, share, ch, cl, dvh, dvl, dgh, dgl, sh, sl, mh, ml, keep, send, tile):
+    for m, (ah, al, bh, bl) in enumerate(((ch, cl, dvh, dvl), (ch, cl, dgh, dgl), (sh, sl, mh, ml))):
         weight_grad(dim, share, m, ah, al, bh, bl, tile, keep, send)
-    split_rows(dim, lambda rows: states[rows, :], ah, al)
-    split_rows(dim, lambda rows: dmixed[rows, :], bh, bl)
-    weight_grad(dim, share, 2, ah, al, bh, bl, tile, keep, send)
-
-
-def k_w2(dim, share, active, dv, dg, states, dmixed, xhat1, dproj1, t, keep, send, ah, al, bh, bl, tile):
-    k_w1(dim, share, active, dv, dg, states, dmixed, keep, send, ah, al, bh, bl, tile)
-    split_rows(dim, lambda rows: xhat1[rows, :] * row(t, GAIN) + row(t, BIAS), ah, al)
-    split_rows(dim, lambda rows: dproj1[rows, :], bh, bl)
-    weight_grad(dim, share, 3, ah, al, bh, bl, tile, keep, send)
+
+
+def k_w2(dim, share, ch, cl, dvh, dvl, dgh, dgl, sh, sl, mh, ml, nh, nl, dph, dpl, keep, send, tile):
+    k_w1(dim, share, ch, cl, dvh, dvl, dgh, dgl, sh, sl, mh, ml, keep, send, tile)
+    weight_grad(dim, share, 3, nh, nl, dph, dpl, tile, keep, send)
 
 
 def k_c1(dim, weights, out_grad, t, t0, ds, rcf, gr, states, en, drive, xhat, rstd, dmixed,
          xhat0, mixed0, v0, s0,
-         dproj, dmid, dv0, dg0, dmixed0, ds0, rcf0, rfin0, sums1, sums0, ah, al, bh, bl, wh, wl, adj_en):
+         dmid, dmixed0, ds0, rcf0, rfin0, sums1, sums0, dph, dpl, dvh, dvl, dgh, dgl, mh, ml, wh, wl, adj_en):
     w_in, w_gv, w_gg, w_out = weights
 
     def store(j, rows, value):
         dmid[rows, :] = value
 
     bottom(dim, t, ds, rcf, gr, states, en, drive, xhat, rstd, dmixed, w_in, strided(dim, out_grad), store,
-           dproj, ds0, adj_en, sums1, ah, al, wh, wl)
+           ds0, adj_en, sums1, dph, dpl, wh, wl)
     sums0[...] = jnp.zeros((SMALL, dim.H), F32)
-    top(dim, t0, plain(dmid), v0, s0, mixed0, xhat0, w_gv, w_gg, w_out, dv0, dg0, dmixed0, ds0, rcf0, rfin0,
-        sums0, ah, al, bh, bl, wh, wl)
-
-
-def k_c0(share, dim, weights, t, ds, rcf, gr, states, en, drive, xhat, rstd, dmixed, dmid, sums1a, sums1b, sums0a,
-         input_grad, keep, send, ah, al, bh, bl, wh, wl, adj_en, dproj, buf, sums0, tile):
+    top(dim, t0, plain(dmid), v0, s0, mixed0, xhat0, w_gv, w_gg, w_out, dmixed0, ds0, rcf0, rfin0,
+        sums0, dvh, dvl, dgh, dgl, mh, ml, wh, wl)
+
+
+def k_c0(share, dim, weights, t, ds, rcf, gr, states, en, drive, xhat, rstd, dmixed, dmid, sums1a, sums1b, sums0a, nh, nl,
+         input_grad, keep, send, ah, al, wh, wl, adj_en, buf, sums0, tile):
     def store(steps, rows, value):
         for u, j in enumerate(steps):
             input_grad.near[:, j, :] = value[u * dim.R : (u + 1) * dim.R, :]
 
-    bottom(dim, t, ds, rcf, gr, states, en, drive, xhat, rstd, dmixed, weights[0], plain(dmid), store, dproj, buf, adj_en,
+    bottom(dim, t, ds, rcf, gr, states, en, drive, xhat, rstd, dmixed, weights[0], plain(dmid), store, buf, adj_en,
            sums0, ah, al, wh, wl)
     input_grad.flush()
-    split_rows(dim, lambda rows: xhat[rows, :] * row(t, GAIN) + row(t, BIAS), bh, bl)
-    weight_grad(dim, share, 0, bh, bl, ah, al, tile, keep, send)
+    weight_grad(dim, share, 0, nh, nl, ah, al, tile, keep, send)
     place = lax.broadcasted_iota(jnp.int32, (SMALL, dim.H), 0)
     upper = (place >= SKIP) & (place <= BIAS_G)
     tile[0:SMALL, :] = jnp.where(upper, sums0a[...], sums0[...])
@@ -900,17 +884,19 @@
     def carried(fin):
         return lax.all_gather(fin, "seq")
 
-    xhat0, rstd0, drive0, cf0, fin0 = k(
-        k_a0, [(0, 0)], [big, stat, big, ent, fins], halves(dim, 1), x, table0, us=3.4
+    part = [pltpu.VMEM((T, H), BF16)] * 2
+    split_weight = [pltpu.VMEM((H, H), BF16)] * 2
+    xhat0, rstd0, drive0, cf0, fin0, *normed0 = k(
+        k_a0, [(0, 0)], [big, stat, big, ent, fins] + part, split_weight, x, table0, us=2.8
     )
     g0 = carried(fin0)
     joined2, (g0,) = tie(joined2, [g0])
     chips2 = chips_gather(dim, joined2)
-    en0, states0, mixed0, active0, v0, s0, act1, xhat1, rstd1, drive1, cf1, fin1 = k(
+    en0, states0, mixed0, v0, s0, sh0, sl0, ch0, cl0, act1, xhat1, rstd1, drive1, cf1, fin1, *normed1 = k(
         k_b0,
         [(0, 1), (0, 2), (0, 3), (1, 0)],
-        [ent, big, big, big, big, big, big, big, stat, big, ent, fins],
-        halves(dim, 1),
+        [ent, big, big, big, big] + part * 2 + [big, big, stat, big, ent, fins] + part,
+        split_weight,
         x, table0, table1, drive0, cf0, g0, xhat0,
         us=9.0,
     )
@@ -918,36 +904,35 @@
     g1 = carried(fin1)
     pieces[2] = cores_gather(chips2)
     spare = [pltpu.VMEM((T, H), F32)]
-    out, en1, states1, active1, dv1, dg1, dmixed1, ds1, rcf1, rfin1, sums1a = k(
+    out, en1, states1, dmixed1, ds1, rcf1, rfin1, sums1a, sh1, sl1, ch1, cl1, dvh1, dvl1, dgh1, dgl1, mh1, ml1 = k(
         k_b1,
         [(1, 1), (1, 2), (1, 3)],
-        [f32(R, dim.L, H), ent, big, big, big, big, big, big, ent, fins, vec],
-        halves(dim, 2) + spare * 3,
+        [f32(R, dim.L, H), ent, big, big, big, ent, fins, vec] + part * 5,
+        split_weight + spare * 3,
         act1, og, table1, drive1, cf1, g1, xhat1,
         us=12.5, sinks=[0],
     )
     share1, share2, share3 = Share(dim, 3), Share(dim, 4), Halves(dim)
     tile = [pltpu.VMEM((WIDE, H), F32)]
-    pair = [pltpu.VMEM((T, H), BF16)] * 4
     keep1, send1 = call(
-        functools.partial(k_w1, dim, share1), [f32(*share1.shape)] * 2, pair + tile,
-        active1, dv1, dg1, states1, dmixed1, us=5.0,
+        functools.partial(k_w1, dim, share1), [f32(*share1.shape)] * 2, tile,
+        ch1, cl1, dvh1, dvl1, dgh1, dgl1, sh1, sl1, mh1, ml1, us=4.0,
     )
     rfin1, (send1,) = tie(rfin1, [send1])
     gr1 = carried(rfin1)
     gr1, half1 = tie(gr1, half_sums(dim, keep1, send1))
-    dproj1, dmid, dv0, dg0, dmixed0, ds0, rcf0, rfin0, sums1b, sums0a = k(
+    dmid, dmixed0, ds0, rcf0, rfin0, sums1b, sums0a, dph1, dpl1, dvh0, dvl0, dgh0, dgl0, mh0, ml0 = k(
         k_c1,
         [(1, 0), (0, 2), (0, 3), (0, 1)],
-        [big, big, big, big, big, big, ent, fins, vec, vec],
-        halves(dim, 2) + [pltpu.VMEM((R, H), F32)],
+        [big, big, big, ent, fins, vec, vec] + part * 4,
+        split_weight + [pltpu.VMEM((R, H), F32)],
         og, table1, table0, ds1, rcf1, gr1, states1, en1, drive1, xhat1, rstd1, dmixed1,
         xhat0, mixed0, v0, s0,
         us=9.5,
     )
     keep2, send2 = call(
-        functools.partial(k_w2, dim, share2), [f32(*share2.shape)] * 2, pair + tile,
-        active0, dv0, dg0, states0, dmixed0, xhat1, dproj1, table1, us=6.4,
+        functools.partial(k_w2, dim, share2), [f32(*share2.shape)] * 2, tile,
+        ch0, cl0, dvh0, dvl0, dgh0, dgl0, sh0, sl0, mh0, ml0, *normed1, dph1, dpl1, us=5.3,
     )
     rfin0, (send2, *sums1) = tie(rfin0, [send2, *plane_sums(dim, half1)])
     gr0 = carried(rfin0)
@@ -958,8 +943,8 @@
         functools.partial(k_c0, share3),
         [(0, 0)],
         [f32(R, dim.L, H)] + [f32(*share3.shape)] * 2,
-        halves(dim, 2) + [pltpu.VMEM((R, H), F32)] + spare * 2 + [pltpu.VMEM((SMALL, H), F32)] + tile,
-        table0, ds0, rcf0, gr0, states0, en0, drive0, xhat0, rstd0, dmixed0, dmid, sums1a, sums1b, sums0a,
+        part + split_weight + [pltpu.VMEM((R, H), F32)] + spare + [pltpu.VMEM((SMALL, H), F32)] + tile,
+        table0, ds0, rcf0, gr0, states0, en0, drive0, xhat0, rstd0, dmixed0, dmid, sums1a, sums1b, sums0a, *normed0,
         us=6.0, sinks=[0],
     )
     sums2 = two_step_sums(dim, half2) if two_steps else plane_sums(dim, half2)

time: 195 us -> 193 us (0.990)
  Pallas kernels: 54.4 us -> 52.2 us
    pallas_call x11, Pallas kernels: 54.4 us -> 52.2 us  [call(): pl.pallas_call(fn, out_shape=outs, in_specs=[pl.BlockSpec(memory_space=sp...]
where the time goes in v6:
time: 193 us
  starting transfers between devices  63.7 us (33%)
  Pallas kernels  52.2 us (27%)
  waiting for transfers between devices  36.2 us (19%)
  blocking collectives  36.2 us (19%)
  local copies, waits for them, and re-layouts  2 us (1%)
    ppermute x62, starting transfers between devices, swap(): return lax.ppermute(x, axis, [(i, i ^ mask) for i in range(count)])  63.7 us
    pallas_call x11, Pallas kernels, call(): pl.pallas_call(fn, out_shape=outs, in_specs=[pl.BlockSpec(memory_space=sp...  52.2 us
    ppermute x62, waiting for transfers between devices, swap(): return lax.ppermute(x, axis, [(i, i ^ mask) for i in range(count)])  36.2 us
    all_gather x4, blocking collectives, carried(): return lax.all_gather(fin, 'seq')  36.2 us
  transfers between devices with their start and end apart: 62, of which 15 were waited for; matrix products, arithmetic and copies ran while one was open for 0% of the time, Pallas kernels for 17%

profile of v6, /device:TPU:9, one launch (start us, length us, event | category | flops | bytes accessed | tf_op | source)
XLA Modules:
  0.0 193.1 jit_solution(6112155901136915254)
XLA Ops:
  1.9 2.5 %collective-permute-start.1 = (f32[40,512]{1,0:T(8,128)S(1)}, f32[40,512]{1,0:T(8,128)S(1)}, u32[]{:S(2)}, u32[]{:S(2)}) collective-permute-start(f32[40,512]{1,0:T(8,128)S(1)} %get-tuple-element.128), channel_id=1, source_target_pairs={{0,16},{8,24},{16,0},{24,8},{1,17},{9,25},{17,1},{25,9},{2,18},{10... | collective-permute-start | bytes 245768 | tf_op jit(solution)/shard_map/ppermute | solution.py:698
  5.2 2.5 %collective-permute-done.1 = f32[40,512]{1,0:T(8,128)S(1)} collective-permute-done((f32[40,512]{1,0:T(8,128)S(1)}, f32[40,512]{1,0:T(8,128)S(1)}, u32[]{:S(2)}, u32[]{:S(2)}) %collective-permute-start.1) | collective-permute-done | bytes 81952 | tf_op jit(solution)/shard_map/ppermute | solution.py:698
  7.7 3.9 %collective-permute-done.2 = f32[40,512]{1,0:T(8,128)S(1)} collective-permute-done((f32[40,512]{1,0:T(8,128)S(1)}, f32[40,512]{1,0:T(8,128)S(1)}, u32[]{:S(2)}, u32[]{:S(2)}) %collective-permute-start.2) | collective-permute-done | bytes 81952 | tf_op jit(solution)/shard_map/ppermute | solution.py:698
  11.6 2.3 %collective-permute-start.4 = (f32[56,512]{1,0:T(8,128)S(1)}, f32[56,512]{1,0:T(8,128)S(1)}, u32[]{:S(2)}, u32[]{:S(2)}) collective-permute-start(f32[56,512]{1,0:T(8,128)S(1)} %get-tuple-element.129), channel_id=1, source_target_pairs={{0,16},{8,24},{16,0},{24,8},{1,17},{9,25},{17,1},{25,9},{2,18},{10... | collective-permute-start | bytes 344072 | tf_op jit(solution)/shard_map/ppermute | solution.py:698
  17.7 6.4 %collective-permute-done.5 = f32[56,512]{1,0:T(8,128)S(1)} collective-permute-done((f32[56,512]{1,0:T(8,128)S(1)}, f32[56,512]{1,0:T(8,128)S(1)}, u32[]{:S(2)}, u32[]{:S(2)}) %collective-permute-start.5) | collective-permute-done | bytes 114720 | tf_op jit(solution)/shard_map/ppermute | solution.py:698
  24.7 4.0 %collective-permute-start.10 = (f32[2,3,16,512]{3,2,1,0:T(8,128)S(1)}, f32[2,3,16,512]{3,2,1,0:T(8,128)S(1)}, u32[]{:S(2)}, u32[]{:S(2)}) collective-permute-start(f32[2,3,16,512]{3,2,1,0:T(8,128)S(1)} %collective-permute-done.6.refs_5_), channel_id=1, source_target_pairs={{0,1},{1,0},{2,3},{3,2},{4,5},{5,4},{6,7},{7,6},{8,9},{9,8},{10,11... | collective-permute-start | bytes 589832 | tf_op jit(solution)/shard_map/ppermute | solution.py:698
  29.8 2.3 %collective-permute-start.12 = (f32[2,3,16,512]{3,2,1,0:T(8,128)S(1)}, f32[2,3,16,512]{3,2,1,0:T(8,128)S(1)}, u32[]{:S(2)}, u32[]{:S(2)}) collective-permute-start(f32[2,3,16,512]{3,2,1,0:T(8,128)S(1)} %collective-permute-done.8.refs_9_), channel_id=1, source_target_pairs={{0,1},{1,0},{2,3},{3,2},{4,5},{5,4},{6,7},{7,6},{8,9},{9,8},{10,11... | collective-permute-start | bytes 589832 | tf_op jit(solution)/shard_map/ppermute | solution.py:698
  36.1 2.8 %shard_map.214 = (f32[512,512]{1,0:T(8,128)S(1)}, f32[512,128]{1,0:T(8,128)S(1)}, f32[512,512]{1,0:T(8,128)S(1)}, f32[16,512]{1,0:T(8,128)S(1)}, f32[2,512]{1,0:...) custom-call(f32[2,128,512]{2,1,0:T(8,128)} %refs_0_.9, f32[2,128,512]{2,1,0:T(8,128)} %refs_1_.9, ...), custom_call_target="tpu_custom_call" | custom-call | flops 1 | bytes 10080000 | tf_op jit(solution)/shard_map/pallas_call | solution.py:435
  39.0 9.7 %all-gather.4.refs_24_ = f32[8,2,512]{2,1,0:T(2,128)S(1)} all-gather(f32[1,2,512]{2,1,0:T(2,128)S(1)} %bitcast.97), channel_id=2, replica_groups=mesh['dp'=4,'seq'=8] {'seq'}, dimensions={0}, use_global_device_ids=true | all-gather | bytes 36864 | tf_op jit(solution)/shard_map/all_gather | solution.py:885
  53.1 9.3 %shard_map.215 = (f32[16,512]{1,0:T(8,128)S(1)}, f32[512,512]{1,0:T(8,128)S(1)}, f32[512,512]{1,0:T(8,128)S(1)}, f32[512,512]{1,0:T(8,128)S(1)}, f32[512,512]{1,...) custom-call(f32[2,128,512]{2,1,0:T(8,128)} %refs_0_.9, ...), custom_call_target="tpu_custom_call" | custom-call | flops 1 | bytes 32400000 | tf_op jit(solution)/shard_map/pallas_call | solution.py:435
  62.4 2.3 %collective-permute-done.24.refs_9_ = f32[3,3,16,512]{3,2,1,0:T(8,128)S(1)} collective-permute-done((f32[3,3,16,512]{3,2,1,0:T(8,128)S(1)}, f32[3,3,16,512]{3,2,1,0:T(8,128)S(1)}, u32[]{:S(2)}, u32[]{:S(2)}) %collective-permute-start.24) | collective-permute-done | bytes 294944 | tf_op jit(solution)/shard_map/ppermute | solution.py:698
  66.5 9.0 %all-gather.5.refs_16_ = f32[8,2,512]{2,1,0:T(2,128)S(1)} all-gather(f32[1,2,512]{2,1,0:T(2,128)S(1)} %bitcast.95), channel_id=3, replica_groups=mesh['dp'=4,'seq'=8] {'seq'}, dimensions={0}, use_global_device_ids=true | all-gather | bytes 36864 | tf_op jit(solution)/shard_map/all_gather | solution.py:885
  76.5 12.5 %shard_map.216 = (f32[16,32,512]{2,1,0:T(8,128)}, f32[16,512]{1,0:T(8,128)S(1)}, f32[512,512]{1,0:T(8,128)S(1)}, f32[512,512]{1,0:T(8,128)S(1)}, f32[512,512]{1,...) custom-call(f32[2,128,512]{2,1,0:T(8,128)} %refs_0_.9, ...), custom_call_target="tpu_custom_call" | custom-call | flops 1 | bytes 45000000 | tf_op jit(solution)/shard_map/pallas_call | solution.py:435
  89.0 4.0 %shard_map.217 = (f32[4,4,48,512]{3,2,1,0:T(8,128)S(1)}, f32[4,4,48,512]{3,2,1,0:T(8,128)S(1)}) custom-call(bf16[512,512]{1,0:T(8,128)(2,1)S(1)} %get-tuple-element.161.ch, bf16[512,512]{1,0:T(8,128)(2,1)S(1)} %get-tuple-element.162.cl, bf16[512,512]{1,0:T(8,128)(2,1)S(1)} %get-tuple-element.163.dvh, bf16[512,512]{1,0:T(8,128)(2,1)S(1)} %get-tuple-element.164.dvl, ...), custom_call_target="tpu_custom_call" | custom-call | flops 1 | bytes 14400000 | tf_op jit(solution)/shard_map/pallas_call | solution.py:435
  93.3 8.9 %all-gather.6.refs_24_ = f32[8,2,512]{2,1,0:T(2,128)S(1)} all-gather(f32[1,2,512]{2,1,0:T(2,128)S(1)} %bitcast.96), channel_id=4, replica_groups=mesh['dp'=4,'seq'=8] {'seq'}, dimensions={0}, use_global_device_ids=true | all-gather | bytes 36864 | tf_op jit(solution)/shard_map/all_gather | solution.py:885
  105.2 9.9 %shard_map.218 = (f32[512,512]{1,0:T(8,128)S(1)}, f32[512,512]{1,0:T(8,128)S(1)}, f32[512,512]{1,0:T(8,128)S(1)}, f32[16,512]{1,0:T(8,128)S(1)}, f32[2,512]{1,0:...) custom-call(f32[2,128,512]{2,1,0:T(8,128)} %refs_0_.9, ...), custom_call_target="tpu_custom_call" | custom-call | flops 1 | bytes 34200000 | tf_op jit(solution)/shard_map/pallas_call | solution.py:435
  115.1 5.1 %shard_map.219 = (f32[4,4,64,512]{3,2,1,0:T(8,128)S(1)}, f32[4,4,64,512]{3,2,1,0:T(8,128)S(1)}) custom-call(bf16[512,512]{1,0:T(8,128)(2,1)S(1)} %get-tuple-element.186.ch, bf16[512,512]{1,0:T(8,128)(2,1)S(1)} %get-tuple-element.187.cl, bf16[512,512]{1,0:T(8,128)(2,1)S(1)} %get-tuple-element.188.dvh, bf16[512,512]{1,0:T(8,128)(2,1)S(1)} %get-tuple-element.189.dvl, ...), custom_call_target="tpu_custom_call" | custom-call | flops 1 | bytes 19080000 | tf_op jit(solution)/shard_map/pallas_call | solution.py:435
  123.3 8.6 %all-gather.7.refs_14_ = f32[8,2,512]{2,1,0:T(2,128)S(1)} all-gather(f32[1,2,512]{2,1,0:T(2,128)S(1)} %bitcast.94), channel_id=5, replica_groups=mesh['dp'=4,'seq'=8] {'seq'}, dimensions={0}, use_global_device_ids=true | all-gather | bytes 36864 | tf_op jit(solution)/shard_map/all_gather | solution.py:885
  136.8 5.3 %shard_map.220 = (f32[16,32,512]{2,1,0:T(8,128)}, f32[4,72,512]{2,1,0:T(8,128)S(1)}, f32[4,72,512]{2,1,0:T(8,128)S(1)}) custom-call(f32[2,128,512]{2,1,0:T(8,128)} %refs_0_.9, f32[2,128,512]{2,1,0:T(8,128)} %refs_1_.9, f32[2,128,1024]{2,1,0:T(8,128)} %refs_2_.9, f32[2,3,16,512]{3,2,1,0:T(8,128)} %copy-done.2, f32[2,3,16,512]{3,2,1,0:T(8,128)} %copy-done.9, ...), custom_call_target="tpu_custom_call" | custom-call | flops 1 | bytes 21600000 | tf_op jit(solution)/shard_map/pallas_call | solution.py:435
  151.9 2.7 %collective-permute-done.49 = f32[2,64,512]{2,1,0:T(8,128)S(1)} collective-permute-done((f32[2,64,512]{2,1,0:T(8,128)S(1)}, f32[2,64,512]{2,1,0:T(8,128)S(1)}, u32[]{:S(2)}, u32[]{:S(2)}) %collective-permute-start.49) | collective-permute-done | bytes 262176 | tf_op jit(solution)/shard_map/ppermute | solution.py:698
  157.5 3.6 %collective-permute-done.37 = f32[72,512]{1,0:T(8,128)S(1)} collective-permute-done((f32[72,512]{1,0:T(8,128)S(1)}, f32[72,512]{1,0:T(8,128)S(1)}, u32[]{:S(2)}, u32[]{:S(2)}) %collective-permute-start.37) | collective-permute-done | bytes 147488 | tf_op jit(solution)/shard_map/ppermute | solution.py:698
  163.9 7.4 %collective-permute-done.53 = f32[64,512]{1,0:T(8,128)S(1)} collective-permute-done((f32[64,512]{1,0:T(8,128)S(1)}, f32[64,512]{1,0:T(8,128)S(1)}, u32[]{:S(2)}, u32[]{:S(2)}) %collective-permute-start.53) | collective-permute-done | bytes 131104 | tf_op jit(solution)/shard_map/ppermute | solution.py:698
  171.3 6.1 %collective-permute-start.41 = (f32[120,512]{1,0:T(8,128)S(1)}, f32[120,512]{1,0:T(8,128)S(1)}, u32[]{:S(2)}, u32[]{:S(2)}) collective-permute-start(f32[120,512]{1,0:T(8,128)S(1)} %pad_maximum_fusion.4.refs_0_), channel_id=1, source_target_pairs={{0,1},{1,0},{2,3},{3,2},{4,5},{5,4},{6,7},{7,6},{8,9},{9,8},{10,11... | collective-permute-start | bytes 737288 | tf_op jit(solution)/shard_map/ppermute | solution.py:698
  180.2 5.1 %collective-permute-start.55 = (f32[64,512]{1,0:T(8,128)S(1)}, f32[64,512]{1,0:T(8,128)S(1)}, u32[]{:S(2)}, u32[]{:S(2)}) collective-permute-start(f32[64,512]{1,0:T(8,128)S(1)} %fusion.18.refs_8_), channel_id=1, source_target_pairs={{0,1},{1,0},{2,3},{3,2},{4,5},{5,4},{6,7},{7,6},{8,9},{9,8},{10,11... | collective-permute-start | bytes 393224 | tf_op jit(solution)/shard_map/ppermute | solution.py:698
  (199 shorter events, 55.8 us)
Async XLA Ops:
  13.9 10.3 %collective-permute-start.5 = (f32[56,512]{1,0:T(8,128)S(1)}, f32[56,512]{1,0:T(8,128)S(1)}, u32[]{:S(2)}, u32[]{:S(2)}) collective-permute-start(f32[56,512]{1,0:T(8,128)S(1)} %get-tuple-element.129), channel_id=1, source_target_pairs={{0,24},{8,16},{16,8},{24,0},{1,25},{9,17},{17,9},{25,1},{2,26},{10... | collective-permute-start | bytes 344072 | tf_op jit(solution)/shard_map/ppermute | solution.py:698
  28.7 20.0 %collective-permute-start.14 = (f32[3,3,16,512]{3,2,1,0:T(8,128)S(1)}, f32[3,3,16,512]{3,2,1,0:T(8,128)S(1)}, u32[]{:S(2)}, u32[]{:S(2)}) collective-permute-start(f32[3,3,16,512]{3,2,1,0:T(8,128)S(1)} %pad_maximum_fusion.2.refs_11_), channel_id=1, source_target_pairs={{0,2},{1,3},{2,0},{3,1},{4,6},{5,7},{6,4},{7,5},{8,10},{9,11},{10,... | collective-permute-start | bytes 884744 | tf_op jit(solution)/shard_map/ppermute | solution.py:698
  29.2 19.6 %collective-permute-start.16 = (f32[3,3,16,512]{3,2,1,0:T(8,128)S(1)}, f32[3,3,16,512]{3,2,1,0:T(8,128)S(1)}, u32[]{:S(2)}, u32[]{:S(2)}) collective-permute-start(f32[3,3,16,512]{3,2,1,0:T(8,128)S(1)} %pad_maximum_fusion.2.refs_11_), channel_id=1, source_target_pairs={{0,4},{1,5},{2,6},{3,7},{4,0},{5,1},{6,2},{7,3},{8,12},{9,13},{10,... | collective-permute-start | bytes 884744 | tf_op jit(solution)/shard_map/ppermute | solution.py:698
  32.2 17.0 %collective-permute-start.21 = (f32[2,48,512]{2,1,0:T(8,128)S(1)}, f32[2,48,512]{2,1,0:T(8,128)S(1)}, u32[]{:S(2)}, u32[]{:S(2)}) collective-permute-start(f32[2,48,512]{2,1,0:T(8,128)S(1)} %pad_maximum_fusion.6), channel_id=1, source_target_pairs={{0,16},{8,24},{16,0},{24,8},{1,17},{9,25},{17,1},{25,9},{2,18},{10... | collective-permute-start | bytes 589832 | tf_op jit(solution)/shard_map/ppermute | solution.py:698
  34.1 15.2 %collective-permute-start.18 = (f32[3,3,16,512]{3,2,1,0:T(8,128)S(1)}, f32[3,3,16,512]{3,2,1,0:T(8,128)S(1)}, u32[]{:S(2)}, u32[]{:S(2)}) collective-permute-start(f32[3,3,16,512]{3,2,1,0:T(8,128)S(1)} %pad_maximum_fusion.2.refs_11_), channel_id=1, source_target_pairs={{0,6},{1,7},{2,4},{3,5},{4,2},{5,3},{6,0},{7,1},{8,14},{9,15},{10,... | collective-permute-start | bytes 884744 | tf_op jit(solution)/shard_map/ppermute | solution.py:698
  35.1 15.0 %collective-permute-start.13 = (f32[3,3,16,512]{3,2,1,0:T(8,128)S(1)}, f32[3,3,16,512]{3,2,1,0:T(8,128)S(1)}, u32[]{:S(2)}, u32[]{:S(2)}) collective-permute-start(f32[3,3,16,512]{3,2,1,0:T(8,128)S(1)} %pad_maximum_fusion.2.refs_11_), channel_id=1, source_target_pairs={{0,1},{1,0},{2,3},{3,2},{4,5},{5,4},{6,7},{7,6},{8,9},{9,8},{10,11... | collective-permute-start | bytes 884744 | tf_op jit(solution)/shard_map/ppermute | solution.py:698
  49.5 12.9 %collective-permute-start.22 = (f32[3,3,16,512]{3,2,1,0:T(8,128)S(1)}, f32[3,3,16,512]{3,2,1,0:T(8,128)S(1)}, u32[]{:S(2)}, u32[]{:S(2)}) collective-permute-start(f32[3,3,16,512]{3,2,1,0:T(8,128)S(1)} %pad_maximum_fusion.3.refs_3_), channel_id=1, source_target_pairs={{0,2},{1,3},{2,0},{3,1},{4,6},{5,7},{6,4},{7,5},{8,10},{9,11},{10,... | collective-permute-start | bytes 884744 | tf_op jit(solution)/shard_map/ppermute | solution.py:698
  50.1 12.3 %collective-permute-start.23 = (f32[3,3,16,512]{3,2,1,0:T(8,128)S(1)}, f32[3,3,16,512]{3,2,1,0:T(8,128)S(1)}, u32[]{:S(2)}, u32[]{:S(2)}) collective-permute-start(f32[3,3,16,512]{3,2,1,0:T(8,128)S(1)} %pad_maximum_fusion.3.refs_3_), channel_id=1, source_target_pairs={{0,4},{1,5},{2,6},{3,7},{4,0},{5,1},{6,2},{7,3},{8,12},{9,13},{10,... | collective-permute-start | bytes 884744 | tf_op jit(solution)/shard_map/ppermute | solution.py:698
  50.8 13.9 %collective-permute-start.24 = (f32[3,3,16,512]{3,2,1,0:T(8,128)S(1)}, f32[3,3,16,512]{3,2,1,0:T(8,128)S(1)}, u32[]{:S(2)}, u32[]{:S(2)}) collective-permute-start(f32[3,3,16,512]{3,2,1,0:T(8,128)S(1)} %pad_maximum_fusion.3.refs_3_), channel_id=1, source_target_pairs={{0,6},{1,7},{2,4},{3,5},{4,2},{5,3},{6,0},{7,1},{8,14},{9,15},{10,... | collective-permute-start | bytes 884744 | tf_op jit(solution)/shard_map/ppermute | solution.py:698
  64.7 10.8 %collective-permute-start.25 = (f32[3,3,16,512]{3,2,1,0:T(8,128)S(1)}, f32[3,3,16,512]{3,2,1,0:T(8,128)S(1)}, u32[]{:S(2)}, u32[]{:S(2)}) collective-permute-start(f32[3,3,16,512]{3,2,1,0:T(8,128)S(1)} %pad_maximum_fusion.3.refs_3_), channel_id=1, source_target_pairs={{0,1},{1,0},{2,3},{3,2},{4,5},{5,4},{6,7},{7,6},{8,9},{9,8},{10,11... | collective-permute-start | bytes 884744 | tf_op jit(solution)/shard_map/ppermute | solution.py:698
  102.5 17.7 %collective-permute-start.30 = (f32[4,48,512]{2,1,0:T(8,128)S(1)}, f32[4,48,512]{2,1,0:T(8,128)S(1)}, u32[]{:S(2)}, u32[]{:S(2)}) collective-permute-start(f32[4,48,512]{2,1,0:T(8,128)S(1)} %get-tuple-element.202), channel_id=1, source_target_pairs={{0,2},{1,3},{2,0},{3,1},{4,6},{5,7},{6,4},{7,5},{8,10},{9,11},{10,... | collective-permute-start | bytes 1179656 | tf_op jit(solution)/shard_map/ppermute | solution.py:698
  103.1 17.1 %collective-permute-start.31 = (f32[4,48,512]{2,1,0:T(8,128)S(1)}, f32[4,48,512]{2,1,0:T(8,128)S(1)}, u32[]{:S(2)}, u32[]{:S(2)}) collective-permute-start(f32[4,48,512]{2,1,0:T(8,128)S(1)} %get-tuple-element.203), channel_id=1, source_target_pairs={{0,4},{1,5},{2,6},{3,7},{4,0},{5,1},{6,2},{7,3},{8,12},{9,13},{10,... | collective-permute-start | bytes 1179656 | tf_op jit(solution)/shard_map/ppermute | solution.py:698
  104.1 17.8 %collective-permute-start.32 = (f32[4,48,512]{2,1,0:T(8,128)S(1)}, f32[4,48,512]{2,1,0:T(8,128)S(1)}, u32[]{:S(2)}, u32[]{:S(2)}) collective-permute-start(f32[4,48,512]{2,1,0:T(8,128)S(1)} %get-tuple-element.204), channel_id=1, source_target_pairs={{0,6},{1,7},{2,4},{3,5},{4,2},{5,3},{6,0},{7,1},{8,14},{9,15},{10,... | collective-permute-start | bytes 1179656 | tf_op jit(solution)/shard_map/ppermute | solution.py:698
  122.0 9.9 %collective-permute-start.33 = (f32[4,4,64,512]{3,2,1,0:T(8,128)S(1)}, f32[4,4,64,512]{3,2,1,0:T(8,128)S(1)}, u32[]{:S(2)}, u32[]{:S(2)}) collective-permute-start(f32[4,4,64,512]{3,2,1,0:T(8,128)S(1)} %get-tuple-element.207), channel_id=1, source_target_pairs={{0,1},{1,0},{2,3},{3,2},{4,5},{5,4},{6,7},{7,6},{8,9},{9,8},{10,11... | collective-permute-start | bytes 6291464 | tf_op jit(solution)/shard_map/ppermute | solution.py:698
  132.7 13.4 %collective-permute-start.48 = (f32[2,2,64,512]{3,2,1,0:T(8,128)S(1)}, f32[2,2,64,512]{3,2,1,0:T(8,128)S(1)}, u32[]{:S(2)}, u32[]{:S(2)}) collective-permute-start(f32[2,2,64,512]{3,2,1,0:T(8,128)S(1)} %pad_maximum_fusion), channel_id=1, source_target_pairs={{0,2},{1,3},{2,0},{3,1},{4,6},{5,7},{6,4},{7,5},{8,10},{9,11},{10,... | collective-permute-start | bytes 1572872 | tf_op jit(solution)/shard_map/ppermute | solution.py:698
  133.8 10.0 %collective-permute-start.39 = (f32[48,512]{1,0:T(8,128)S(1)}, f32[48,512]{1,0:T(8,128)S(1)}, u32[]{:S(2)}, u32[]{:S(2)}) collective-permute-start(f32[48,512]{1,0:T(8,128)S(1)} %get-tuple-element.224), channel_id=1, source_target_pairs={{0,16},{8,24},{16,0},{24,8},{1,17},{9,25},{17,1},{25,9},{2,18},{10... | collective-permute-start | bytes 294920 | tf_op jit(solution)/shard_map/ppermute | solution.py:698
  135.9 12.1 %collective-permute-start.51 = (f32[2,2,64,512]{3,2,1,0:T(8,128)S(1)}, f32[2,2,64,512]{3,2,1,0:T(8,128)S(1)}, u32[]{:S(2)}, u32[]{:S(2)}) collective-permute-start(f32[2,2,64,512]{3,2,1,0:T(8,128)S(1)} %pad_maximum_fusion.1), channel_id=1, source_target_pairs={{0,4},{1,5},{2,6},{3,7},{4,0},{5,1},{6,2},{7,3},{8,12},{9,13},{10,... | collective-permute-start | bytes 1572872 | tf_op jit(solution)/shard_map/ppermute | solution.py:698
  155.4 16.0 %collective-permute-start.53 = (f32[64,512]{1,0:T(8,128)S(1)}, f32[64,512]{1,0:T(8,128)S(1)}, u32[]{:S(2)}, u32[]{:S(2)}) collective-permute-start(f32[64,512]{1,0:T(8,128)S(1)} %get-tuple-element.265), channel_id=1, source_target_pairs={{0,16},{8,24},{16,0},{24,8},{1,17},{9,25},{17,1},{25,9},{2,18},{10... | collective-permute-start | bytes 393224 | tf_op jit(solution)/shard_map/ppermute | solution.py:698
  157.2 20.3 %collective-permute-start.54 = (f32[64,512]{1,0:T(8,128)S(1)}, f32[64,512]{1,0:T(8,128)S(1)}, u32[]{:S(2)}, u32[]{:S(2)}) collective-permute-start(f32[64,512]{1,0:T(8,128)S(1)} %get-tuple-element.266), channel_id=1, source_target_pairs={{0,24},{8,16},{16,8},{24,0},{1,25},{9,17},{17,9},{25,1},{2,26},{10... | collective-permute-start | bytes 393224 | tf_op jit(solution)/shard_map/ppermute | solution.py:698
  161.2 16.9 %collective-permute-start.42 = (f32[120,512]{1,0:T(8,128)S(1)}, f32[120,512]{1,0:T(8,128)S(1)}, u32[]{:S(2)}, u32[]{:S(2)}) collective-permute-start(f32[120,512]{1,0:T(8,128)S(1)} %pad_maximum_fusion.4.refs_0_), channel_id=1, source_target_pairs={{0,2},{1,3},{2,0},{3,1},{4,6},{5,7},{6,4},{7,5},{8,10},{9,11},{10,... | collective-permute-start | bytes 737288 | tf_op jit(solution)/shard_map/ppermute | solution.py:698
  161.8 17.1 %collective-permute-start.44 = (f32[120,512]{1,0:T(8,128)S(1)}, f32[120,512]{1,0:T(8,128)S(1)}, u32[]{:S(2)}, u32[]{:S(2)}) collective-permute-start(f32[120,512]{1,0:T(8,128)S(1)} %pad_maximum_fusion.4.refs_0_), channel_id=1, source_target_pairs={{0,4},{1,5},{2,6},{3,7},{4,0},{5,1},{6,2},{7,3},{8,12},{9,13},{10,... | collective-permute-start | bytes 737288 | tf_op jit(solution)/shard_map/ppermute | solution.py:698
  162.7 17.4 %collective-permute-start.46 = (f32[120,512]{1,0:T(8,128)S(1)}, f32[120,512]{1,0:T(8,128)S(1)}, u32[]{:S(2)}, u32[]{:S(2)}) collective-permute-start(f32[120,512]{1,0:T(8,128)S(1)} %pad_maximum_fusion.4.refs_0_), channel_id=1, source_target_pairs={{0,6},{1,7},{2,4},{3,5},{4,2},{5,3},{6,0},{7,1},{8,14},{9,15},{10,... | collective-permute-start | bytes 737288 | tf_op jit(solution)/shard_map/ppermute | solution.py:698
  171.3 15.6 %collective-permute-start.41 = (f32[120,512]{1,0:T(8,128)S(1)}, f32[120,512]{1,0:T(8,128)S(1)}, u32[]{:S(2)}, u32[]{:S(2)}) collective-permute-start(f32[120,512]{1,0:T(8,128)S(1)} %pad_maximum_fusion.4.refs_0_), channel_id=1, source_target_pairs={{0,1},{1,0},{2,3},{3,2},{4,5},{5,4},{6,7},{7,6},{8,9},{9,8},{10,11... | collective-permute-start | bytes 737288 | tf_op jit(solution)/shard_map/ppermute | solution.py:698
  179.0 10.2 %collective-permute-start.60 = (f32[64,512]{1,0:T(8,128)S(1)}, f32[64,512]{1,0:T(8,128)S(1)}, u32[]{:S(2)}, u32[]{:S(2)}) collective-permute-start(f32[64,512]{1,0:T(8,128)S(1)} %fusion.18.refs_8_), channel_id=1, source_target_pairs={{0,6},{1,7},{2,4},{3,5},{4,2},{5,3},{6,0},{7,1},{8,14},{9,15},{10,... | collective-permute-start | bytes 393224 | tf_op jit(solution)/shard_map/ppermute | solution.py:698
  (64 other events, 466.4 us)

commit v7 on v6

--- a/solution.py
+++ b/solution.py
@@ -174,8 +174,7 @@
         return 0
 
     each_span(dim, norm)
-    w_in.fill(wh, wl)
-    product(ah, al, wh, wl, drive)
+    product(ah, al, *w_in.fill(*halves_of(w_in, wh, wl)), drive)
 
     def scale(j, rows, _):
         drive[rows, :] = drive[rows, :] * row(table, GAMMA)
@@ -206,8 +205,7 @@
         return both[:, : dim.N], both[:, dim.N :]
 
     each_step(dim, scan, 4, False, (en[:, : dim.N], en[:, dim.N :]))
-    w_out.fill(wh, wl)
-    product(sh, sl, wh, wl, mixed)
+    product(sh, sl, *w_out.fill(*halves_of(w_out, wh, wl)), mixed)
 
     def gelu(j, rows, _):
         normed = xhat[rows, :] * row(table, GAIN) + row(table, BIAS)
@@ -218,10 +216,8 @@
         return 0
 
     each_step(dim, gelu, 4)
-    w_gv.fill(wh, wl)
-    product(ch, cl, wh, wl, v)
-    w_gg.fill(wh, wl)
-    product(ch, cl, wh, wl, s)
+    product(ch, cl, *w_gv.fill(*halves_of(w_gv, wh, wl)), v)
+    product(ch, cl, *w_gg.fill(*halves_of(w_gg, wh, wl)), s)
 
 
 def gate(dim, table, v, s, rows):
@@ -246,10 +242,8 @@
     sv, sg = each_step(dim, dgate, 2, False, (zero, zero))
     sums[BIAS_V : BIAS_V + 1, :] = jnp.sum(sv, 0, keepdims=True)
     sums[BIAS_G : BIAS_G + 1, :] = jnp.sum(sg, 0, keepdims=True)
-    w_gv.fill(wh, wl)
-    product(ah, al, wh, wl, dmixed, True)
-    w_gg.fill(wh, wl)
-    product(bh, bl, wh, wl, dmixed, True, True)
+    product(ah, al, *w_gv.fill(*halves_of(w_gv, wh, wl)), dmixed, True)
+    product(bh, bl, *w_gg.fill(*halves_of(w_gg, wh, wl)), dmixed, True, True)
 
     def dgelu(j, rows, carry):
         m = mixed[rows, :]
@@ -262,8 +256,7 @@
         return carry + d * normed
 
     sums[SKIP : SKIP + 1, :] = jnp.sum(each_step(dim, dgelu, 2, False, zero), 0, keepdims=True)
-    w_out.fill(wh, wl)
-    product(mh, ml, wh, wl, ds, True)
+    product(mh, ml, *w_out.fill(*halves_of(w_out, wh, wl)), ds, True)
     local_finals(dim, table, ds, rcf, rfin, True)
 
 
@@ -302,8 +295,7 @@
     sums[6:7, dim.N :] = jnp.zeros_like(dgam)
     sums[7:8, :] = jnp.zeros((1, dim.H), F32)
 
-    w_in.fill(wh, wl)
-    product(ah, al, wh, wl, buf, True)
+    product(ah, al, *w_in.fill(*halves_of(w_in, wh, wl)), buf, True)
     wide = jnp.zeros((8, dim.H), F32)
 
     def dnorm(steps, rows, carry):
@@ -517,11 +509,15 @@
         move.wait()
 
 
+def halves_of(weight, wh, wl):
+    return weight.kept or (wh, wl)
+
+
 class Weight:
     def __init__(self, dim, name, place, sources, own, buf, sem):
         self.dim, self.name, self.place = dim, name, place
         self.sources, self.own, self.buf, self.sem = sources, own, buf, sem
-        self.here = False
+        self.here, self.kept, self.halves = False, False, None
 
     def moves(self):
         shard = shard_of(self.sources, self.name, slice(None), self.dim.H)
@@ -534,6 +530,14 @@
             move.start()
 
     def fill(self, wh, wl):
+        if self.halves is None:
+            self.write(wh, wl)
+            if self.kept:
+                self.halves = wh, wl
+            return wh, wl
+        return self.halves
+
+    def write(self, wh, wl):
         dim, q = self.dim, self.dim.q
         if not self.here:
             for move in self.moves():
@@ -622,8 +626,11 @@
 
 
 def k_b1(dim, weights, act1, out_grad, t, drive, cf, g, xhat,
-         out, en, states, dmixed, ds, rcf, rfin, sums, sh, sl, ch, cl, dvh, dvl, dgh, dgl, mh, ml, wh, wl, mixed, v, s):
+         out, en, states, dmixed, ds, rcf, rfin, sums, sh, sl, ch, cl, dvh, dvl, dgh, dgl, mh, ml, *scratch):
     w_out, w_gv, w_gg = weights
+    for i, w in enumerate(weights):
+        w.kept = scratch[2 * i : 2 * i + 2]
+    wh, wl, (mixed, v, s) = None, None, scratch[6:]
     back(dim, t, drive, cf, g, xhat, w_out, w_gv, w_gg, en, states, mixed, v, s, sh, sl, ch, cl, wh, wl)
 
     def residual(j, rows, _):
@@ -908,7 +915,7 @@
         k_b1,
         [(1, 1), (1, 2), (1, 3)],
         [f32(R, dim.L, H), ent, big, big, big, ent, fins, vec] + part * 5,
-        split_weight + spare * 3,
+        split_weight * 3 + spare * 3,
         act1, og, table1, drive1, cf1, g1, xhat1,
         us=12.5, sinks=[0],
     )

time: 193 us -> 193 us (level)
  no operation moved by 1% of the time
where the time goes in v7:
time: 193 us; the launch traced here: 192 us
  starting transfers between devices  63.7 us (33%)
  Pallas kernels  51.6 us (27%)
  waiting for transfers between devices  36.2 us (19%)
  blocking collectives  36.2 us (19%)
  local copies, waits for them, and re-layouts  2 us (1%)
    ppermute x62, starting transfers between devices, swap(): return lax.ppermute(x, axis, [(i, i ^ mask) for i in range(count)])  63.7 us
    pallas_call x11, Pallas kernels, call(): pl.pallas_call(fn, out_shape=outs, in_specs=[pl.BlockSpec(memory_space=sp...  51.6 us
    all_gather x4, blocking collectives, carried(): return lax.all_gather(fin, 'seq')  36.2 us
    ppermute x62, waiting for transfers between devices, swap(): return lax.ppermute(x, axis, [(i, i ^ mask) for i in range(count)])  36.2 us
  transfers between devices with their start and end apart: 62, of which 15 were waited for; matrix products, arithmetic and copies ran while one was open for 0% of the time, Pallas kernels for 17%

profile of v7, /device:TPU:9, one launch (start us, length us, event | category | flops | bytes accessed | tf_op | source)
XLA Modules:
  0.0 192.5 jit_solution(16800956577021223511)
XLA Ops:
  1.9 2.5 %collective-permute-start.1 = (f32[40,512]{1,0:T(8,128)S(1)}, f32[40,512]{1,0:T(8,128)S(1)}, u32[]{:S(2)}, u32[]{:S(2)}) collective-permute-start(f32[40,512]{1,0:T(8,128)S(1)} %get-tuple-element.128), channel_id=1, source_target_pairs={{0,16},{8,24},{16,0},{24,8},{1,17},{9,25},{17,1},{25,9},{2,18},{10... | collective-permute-start | bytes 245768 | tf_op jit(solution)/shard_map/ppermute | solution.py:705
  5.2 2.5 %collective-permute-done.1 = f32[40,512]{1,0:T(8,128)S(1)} collective-permute-done((f32[40,512]{1,0:T(8,128)S(1)}, f32[40,512]{1,0:T(8,128)S(1)}, u32[]{:S(2)}, u32[]{:S(2)}) %collective-permute-start.1) | collective-permute-done | bytes 81952 | tf_op jit(solution)/shard_map/ppermute | solution.py:705
  7.7 3.9 %collective-permute-done.2 = f32[40,512]{1,0:T(8,128)S(1)} collective-permute-done((f32[40,512]{1,0:T(8,128)S(1)}, f32[40,512]{1,0:T(8,128)S(1)}, u32[]{:S(2)}, u32[]{:S(2)}) %collective-permute-start.2) | collective-permute-done | bytes 81952 | tf_op jit(solution)/shard_map/ppermute | solution.py:705
  11.6 2.3 %collective-permute-start.4 = (f32[56,512]{1,0:T(8,128)S(1)}, f32[56,512]{1,0:T(8,128)S(1)}, u32[]{:S(2)}, u32[]{:S(2)}) collective-permute-start(f32[56,512]{1,0:T(8,128)S(1)} %get-tuple-element.129), channel_id=1, source_target_pairs={{0,16},{8,24},{16,0},{24,8},{1,17},{9,25},{17,1},{25,9},{2,18},{10... | collective-permute-start | bytes 344072 | tf_op jit(solution)/shard_map/ppermute | solution.py:705
  17.7 6.4 %collective-permute-done.5 = f32[56,512]{1,0:T(8,128)S(1)} collective-permute-done((f32[56,512]{1,0:T(8,128)S(1)}, f32[56,512]{1,0:T(8,128)S(1)}, u32[]{:S(2)}, u32[]{:S(2)}) %collective-permute-start.5) | collective-permute-done | bytes 114720 | tf_op jit(solution)/shard_map/ppermute | solution.py:705
  24.7 4.0 %collective-permute-start.10 = (f32[2,3,16,512]{3,2,1,0:T(8,128)S(1)}, f32[2,3,16,512]{3,2,1,0:T(8,128)S(1)}, u32[]{:S(2)}, u32[]{:S(2)}) collective-permute-start(f32[2,3,16,512]{3,2,1,0:T(8,128)S(1)} %collective-permute-done.6.refs_5_), channel_id=1, source_target_pairs={{0,1},{1,0},{2,3},{3,2},{4,5},{5,4},{6,7},{7,6},{8,9},{9,8},{10,11... | collective-permute-start | bytes 589832 | tf_op jit(solution)/shard_map/ppermute | solution.py:705
  29.8 2.3 %collective-permute-start.12 = (f32[2,3,16,512]{3,2,1,0:T(8,128)S(1)}, f32[2,3,16,512]{3,2,1,0:T(8,128)S(1)}, u32[]{:S(2)}, u32[]{:S(2)}) collective-permute-start(f32[2,3,16,512]{3,2,1,0:T(8,128)S(1)} %collective-permute-done.8.refs_9_), channel_id=1, source_target_pairs={{0,1},{1,0},{2,3},{3,2},{4,5},{5,4},{6,7},{7,6},{8,9},{9,8},{10,11... | collective-permute-start | bytes 589832 | tf_op jit(solution)/shard_map/ppermute | solution.py:705
  36.1 2.8 %shard_map.214 = (f32[512,512]{1,0:T(8,128)S(1)}, f32[512,128]{1,0:T(8,128)S(1)}, f32[512,512]{1,0:T(8,128)S(1)}, f32[16,512]{1,0:T(8,128)S(1)}, f32[2,512]{1,0:...) custom-call(f32[2,128,512]{2,1,0:T(8,128)} %refs_0_.9, f32[2,128,512]{2,1,0:T(8,128)} %refs_1_.9, ...), custom_call_target="tpu_custom_call" | custom-call | flops 1 | bytes 10080000 | tf_op jit(solution)/shard_map/pallas_call | solution.py:427
  39.0 9.7 %all-gather.4.refs_24_ = f32[8,2,512]{2,1,0:T(2,128)S(1)} all-gather(f32[1,2,512]{2,1,0:T(2,128)S(1)} %bitcast.97), channel_id=2, replica_groups=mesh['dp'=4,'seq'=8] {'seq'}, dimensions={0}, use_global_device_ids=true | all-gather | bytes 36864 | tf_op jit(solution)/shard_map/all_gather | solution.py:892
  53.1 9.3 %shard_map.215 = (f32[16,512]{1,0:T(8,128)S(1)}, f32[512,512]{1,0:T(8,128)S(1)}, f32[512,512]{1,0:T(8,128)S(1)}, f32[512,512]{1,0:T(8,128)S(1)}, f32[512,512]{1,...) custom-call(f32[2,128,512]{2,1,0:T(8,128)} %refs_0_.9, ...), custom_call_target="tpu_custom_call" | custom-call | flops 1 | bytes 32400000 | tf_op jit(solution)/shard_map/pallas_call | solution.py:427
  62.4 2.3 %collective-permute-done.24.refs_9_ = f32[3,3,16,512]{3,2,1,0:T(8,128)S(1)} collective-permute-done((f32[3,3,16,512]{3,2,1,0:T(8,128)S(1)}, f32[3,3,16,512]{3,2,1,0:T(8,128)S(1)}, u32[]{:S(2)}, u32[]{:S(2)}) %collective-permute-start.24) | collective-permute-done | bytes 294944 | tf_op jit(solution)/shard_map/ppermute | solution.py:705
  66.5 9.0 %all-gather.5.refs_16_ = f32[8,2,512]{2,1,0:T(2,128)S(1)} all-gather(f32[1,2,512]{2,1,0:T(2,128)S(1)} %bitcast.95), channel_id=3, replica_groups=mesh['dp'=4,'seq'=8] {'seq'}, dimensions={0}, use_global_device_ids=true | all-gather | bytes 36864 | tf_op jit(solution)/shard_map/all_gather | solution.py:892
  76.5 11.8 %shard_map.216 = (f32[16,32,512]{2,1,0:T(8,128)}, f32[16,512]{1,0:T(8,128)S(1)}, f32[512,512]{1,0:T(8,128)S(1)}, f32[512,512]{1,0:T(8,128)S(1)}, f32[512,512]{1,...) custom-call(f32[2,128,512]{2,1,0:T(8,128)} %refs_0_.9, ...), custom_call_target="tpu_custom_call" | custom-call | flops 1 | bytes 45000000 | tf_op jit(solution)/shard_map/pallas_call | solution.py:427
  88.3 4.0 %shard_map.217 = (f32[4,4,48,512]{3,2,1,0:T(8,128)S(1)}, f32[4,4,48,512]{3,2,1,0:T(8,128)S(1)}) custom-call(bf16[512,512]{1,0:T(8,128)(2,1)S(1)} %get-tuple-element.161.ch, bf16[512,512]{1,0:T(8,128)(2,1)S(1)} %get-tuple-element.162.cl, bf16[512,512]{1,0:T(8,128)(2,1)S(1)} %get-tuple-element.163.dvh, bf16[512,512]{1,0:T(8,128)(2,1)S(1)} %get-tuple-element.164.dvl, ...), custom_call_target="tpu_custom_call" | custom-call | flops 1 | bytes 14400000 | tf_op jit(solution)/shard_map/pallas_call | solution.py:427
  92.6 8.9 %all-gather.6.refs_24_ = f32[8,2,512]{2,1,0:T(2,128)S(1)} all-gather(f32[1,2,512]{2,1,0:T(2,128)S(1)} %bitcast.96), channel_id=4, replica_groups=mesh['dp'=4,'seq'=8] {'seq'}, dimensions={0}, use_global_device_ids=true | all-gather | bytes 36864 | tf_op jit(solution)/shard_map/all_gather | solution.py:892
  104.6 9.9 %shard_map.218 = (f32[512,512]{1,0:T(8,128)S(1)}, f32[512,512]{1,0:T(8,128)S(1)}, f32[512,512]{1,0:T(8,128)S(1)}, f32[16,512]{1,0:T(8,128)S(1)}, f32[2,512]{1,0:...) custom-call(f32[2,128,512]{2,1,0:T(8,128)} %refs_0_.9, ...), custom_call_target="tpu_custom_call" | custom-call | flops 1 | bytes 34200000 | tf_op jit(solution)/shard_map/pallas_call | solution.py:427
  114.5 5.1 %shard_map.219 = (f32[4,4,64,512]{3,2,1,0:T(8,128)S(1)}, f32[4,4,64,512]{3,2,1,0:T(8,128)S(1)}) custom-call(bf16[512,512]{1,0:T(8,128)(2,1)S(1)} %get-tuple-element.186.ch, bf16[512,512]{1,0:T(8,128)(2,1)S(1)} %get-tuple-element.187.cl, bf16[512,512]{1,0:T(8,128)(2,1)S(1)} %get-tuple-element.188.dvh, bf16[512,512]{1,0:T(8,128)(2,1)S(1)} %get-tuple-element.189.dvl, ...), custom_call_target="tpu_custom_call" | custom-call | flops 1 | bytes 19080000 | tf_op jit(solution)/shard_map/pallas_call | solution.py:427
  122.7 8.6 %all-gather.7.refs_14_ = f32[8,2,512]{2,1,0:T(2,128)S(1)} all-gather(f32[1,2,512]{2,1,0:T(2,128)S(1)} %bitcast.94), channel_id=5, replica_groups=mesh['dp'=4,'seq'=8] {'seq'}, dimensions={0}, use_global_device_ids=true | all-gather | bytes 36864 | tf_op jit(solution)/shard_map/all_gather | solution.py:892
  136.2 5.3 %shard_map.220 = (f32[16,32,512]{2,1,0:T(8,128)}, f32[4,72,512]{2,1,0:T(8,128)S(1)}, f32[4,72,512]{2,1,0:T(8,128)S(1)}) custom-call(f32[2,128,512]{2,1,0:T(8,128)} %refs_0_.9, f32[2,128,512]{2,1,0:T(8,128)} %refs_1_.9, f32[2,128,1024]{2,1,0:T(8,128)} %refs_2_.9, f32[2,3,16,512]{3,2,1,0:T(8,128)} %copy-done.2, f32[2,3,16,512]{3,2,1,0:T(8,128)} %copy-done.9, ...), custom_call_target="tpu_custom_call" | custom-call | flops 1 | bytes 21600000 | tf_op jit(solution)/shard_map/pallas_call | solution.py:427
  151.3 2.6 %collective-permute-done.49 = f32[2,64,512]{2,1,0:T(8,128)S(1)} collective-permute-done((f32[2,64,512]{2,1,0:T(8,128)S(1)}, f32[2,64,512]{2,1,0:T(8,128)S(1)}, u32[]{:S(2)}, u32[]{:S(2)}) %collective-permute-start.49) | collective-permute-done | bytes 262176 | tf_op jit(solution)/shard_map/ppermute | solution.py:705
  156.9 3.6 %collective-permute-done.37 = f32[72,512]{1,0:T(8,128)S(1)} collective-permute-done((f32[72,512]{1,0:T(8,128)S(1)}, f32[72,512]{1,0:T(8,128)S(1)}, u32[]{:S(2)}, u32[]{:S(2)}) %collective-permute-start.37) | collective-permute-done | bytes 147488 | tf_op jit(solution)/shard_map/ppermute | solution.py:705
  163.3 7.4 %collective-permute-done.53 = f32[64,512]{1,0:T(8,128)S(1)} collective-permute-done((f32[64,512]{1,0:T(8,128)S(1)}, f32[64,512]{1,0:T(8,128)S(1)}, u32[]{:S(2)}, u32[]{:S(2)}) %collective-permute-start.53) | collective-permute-done | bytes 131104 | tf_op jit(solution)/shard_map/ppermute | solution.py:705
  170.7 6.1 %collective-permute-start.41 = (f32[120,512]{1,0:T(8,128)S(1)}, f32[120,512]{1,0:T(8,128)S(1)}, u32[]{:S(2)}, u32[]{:S(2)}) collective-permute-start(f32[120,512]{1,0:T(8,128)S(1)} %pad_maximum_fusion.4.refs_0_), channel_id=1, source_target_pairs={{0,1},{1,0},{2,3},{3,2},{4,5},{5,4},{6,7},{7,6},{8,9},{9,8},{10,11... | collective-permute-start | bytes 737288 | tf_op jit(solution)/shard_map/ppermute | solution.py:705
  179.5 5.1 %collective-permute-start.55 = (f32[64,512]{1,0:T(8,128)S(1)}, f32[64,512]{1,0:T(8,128)S(1)}, u32[]{:S(2)}, u32[]{:S(2)}) collective-permute-start(f32[64,512]{1,0:T(8,128)S(1)} %fusion.18.refs_8_), channel_id=1, source_target_pairs={{0,1},{1,0},{2,3},{3,2},{4,5},{5,4},{6,7},{7,6},{8,9},{9,8},{10,11... | collective-permute-start | bytes 393224 | tf_op jit(solution)/shard_map/ppermute | solution.py:705
  (199 shorter events, 55.8 us)
Async XLA Ops:
  13.9 10.3 %collective-permute-start.5 = (f32[56,512]{1,0:T(8,128)S(1)}, f32[56,512]{1,0:T(8,128)S(1)}, u32[]{:S(2)}, u32[]{:S(2)}) collective-permute-start(f32[56,512]{1,0:T(8,128)S(1)} %get-tuple-element.129), channel_id=1, source_target_pairs={{0,24},{8,16},{16,8},{24,0},{1,25},{9,17},{17,9},{25,1},{2,26},{10... | collective-permute-start | bytes 344072 | tf_op jit(solution)/shard_map/ppermute | solution.py:705
  28.7 20.0 %collective-permute-start.14 = (f32[3,3,16,512]{3,2,1,0:T(8,128)S(1)}, f32[3,3,16,512]{3,2,1,0:T(8,128)S(1)}, u32[]{:S(2)}, u32[]{:S(2)}) collective-permute-start(f32[3,3,16,512]{3,2,1,0:T(8,128)S(1)} %pad_maximum_fusion.2.refs_11_), channel_id=1, source_target_pairs={{0,2},{1,3},{2,0},{3,1},{4,6},{5,7},{6,4},{7,5},{8,10},{9,11},{10,... | collective-permute-start | bytes 884744 | tf_op jit(solution)/shard_map/ppermute | solution.py:705
  29.2 19.6 %collective-permute-start.16 = (f32[3,3,16,512]{3,2,1,0:T(8,128)S(1)}, f32[3,3,16,512]{3,2,1,0:T(8,128)S(1)}, u32[]{:S(2)}, u32[]{:S(2)}) collective-permute-start(f32[3,3,16,512]{3,2,1,0:T(8,128)S(1)} %pad_maximum_fusion.2.refs_11_), channel_id=1, source_target_pairs={{0,4},{1,5},{2,6},{3,7},{4,0},{5,1},{6,2},{7,3},{8,12},{9,13},{10,... | collective-permute-start | bytes 884744 | tf_op jit(solution)/shard_map/ppermute | solution.py:705
  32.2 17.0 %collective-permute-start.21 = (f32[2,48,512]{2,1,0:T(8,128)S(1)}, f32[2,48,512]{2,1,0:T(8,128)S(1)}, u32[]{:S(2)}, u32[]{:S(2)}) collective-permute-start(f32[2,48,512]{2,1,0:T(8,128)S(1)} %pad_maximum_fusion.6), channel_id=1, source_target_pairs={{0,16},{8,24},{16,0},{24,8},{1,17},{9,25},{17,1},{25,9},{2,18},{10... | collective-permute-start | bytes 589832 | tf_op jit(solution)/shard_map/ppermute | solution.py:705
  34.1 15.2 %collective-permute-start.18 = (f32[3,3,16,512]{3,2,1,0:T(8,128)S(1)}, f32[3,3,16,512]{3,2,1,0:T(8,128)S(1)}, u32[]{:S(2)}, u32[]{:S(2)}) collective-permute-start(f32[3,3,16,512]{3,2,1,0:T(8,128)S(1)} %pad_maximum_fusion.2.refs_11_), channel_id=1, source_target_pairs={{0,6},{1,7},{2,4},{3,5},{4,2},{5,3},{6,0},{7,1},{8,14},{9,15},{10,... | collective-permute-start | bytes 884744 | tf_op jit(solution)/shard_map/ppermute | solution.py:705
  35.1 15.0 %collective-permute-start.13 = (f32[3,3,16,512]{3,2,1,0:T(8,128)S(1)}, f32[3,3,16,512]{3,2,1,0:T(8,128)S(1)}, u32[]{:S(2)}, u32[]{:S(2)}) collective-permute-start(f32[3,3,16,512]{3,2,1,0:T(8,128)S(1)} %pad_maximum_fusion.2.refs_11_), channel_id=1, source_target_pairs={{0,1},{1,0},{2,3},{3,2},{4,5},{5,4},{6,7},{7,6},{8,9},{9,8},{10,11... | collective-permute-start | bytes 884744 | tf_op jit(solution)/shard_map/ppermute | solution.py:705
  49.5 12.9 %collective-permute-start.22 = (f32[3,3,16,512]{3,2,1,0:T(8,128)S(1)}, f32[3,3,16,512]{3,2,1,0:T(8,128)S(1)}, u32[]{:S(2)}, u32[]{:S(2)}) collective-permute-start(f32[3,3,16,512]{3,2,1,0:T(8,128)S(1)} %pad_maximum_fusion.3.refs_3_), channel_id=1, source_target_pairs={{0,2},{1,3},{2,0},{3,1},{4,6},{5,7},{6,4},{7,5},{8,10},{9,11},{10,... | collective-permute-start | bytes 884744 | tf_op jit(solution)/shard_map/ppermute | solution.py:705
  50.1 12.3 %collective-permute-start.23 = (f32[3,3,16,512]{3,2,1,0:T(8,128)S(1)}, f32[3,3,16,512]{3,2,1,0:T(8,128)S(1)}, u32[]{:S(2)}, u32[]{:S(2)}) collective-permute-start(f32[3,3,16,512]{3,2,1,0:T(8,128)S(1)} %pad_maximum_fusion.3.refs_3_), channel_id=1, source_target_pairs={{0,4},{1,5},{2,6},{3,7},{4,0},{5,1},{6,2},{7,3},{8,12},{9,13},{10,... | collective-permute-start | bytes 884744 | tf_op jit(solution)/shard_map/ppermute | solution.py:705
  50.8 13.9 %collective-permute-start.24 = (f32[3,3,16,512]{3,2,1,0:T(8,128)S(1)}, f32[3,3,16,512]{3,2,1,0:T(8,128)S(1)}, u32[]{:S(2)}, u32[]{:S(2)}) collective-permute-start(f32[3,3,16,512]{3,2,1,0:T(8,128)S(1)} %pad_maximum_fusion.3.refs_3_), channel_id=1, source_target_pairs={{0,6},{1,7},{2,4},{3,5},{4,2},{5,3},{6,0},{7,1},{8,14},{9,15},{10,... | collective-permute-start | bytes 884744 | tf_op jit(solution)/shard_map/ppermute | solution.py:705
  64.7 10.8 %collective-permute-start.25 = (f32[3,3,16,512]{3,2,1,0:T(8,128)S(1)}, f32[3,3,16,512]{3,2,1,0:T(8,128)S(1)}, u32[]{:S(2)}, u32[]{:S(2)}) collective-permute-start(f32[3,3,16,512]{3,2,1,0:T(8,128)S(1)} %pad_maximum_fusion.3.refs_3_), channel_id=1, source_target_pairs={{0,1},{1,0},{2,3},{3,2},{4,5},{5,4},{6,7},{7,6},{8,9},{9,8},{10,11... | collective-permute-start | bytes 884744 | tf_op jit(solution)/shard_map/ppermute | solution.py:705
  101.9 17.7 %collective-permute-start.30 = (f32[4,48,512]{2,1,0:T(8,128)S(1)}, f32[4,48,512]{2,1,0:T(8,128)S(1)}, u32[]{:S(2)}, u32[]{:S(2)}) collective-permute-start(f32[4,48,512]{2,1,0:T(8,128)S(1)} %get-tuple-element.202), channel_id=1, source_target_pairs={{0,2},{1,3},{2,0},{3,1},{4,6},{5,7},{6,4},{7,5},{8,10},{9,11},{10,... | collective-permute-start | bytes 1179656 | tf_op jit(solution)/shard_map/ppermute | solution.py:705
  102.5 17.1 %collective-permute-start.31 = (f32[4,48,512]{2,1,0:T(8,128)S(1)}, f32[4,48,512]{2,1,0:T(8,128)S(1)}, u32[]{:S(2)}, u32[]{:S(2)}) collective-permute-start(f32[4,48,512]{2,1,0:T(8,128)S(1)} %get-tuple-element.203), channel_id=1, source_target_pairs={{0,4},{1,5},{2,6},{3,7},{4,0},{5,1},{6,2},{7,3},{8,12},{9,13},{10,... | collective-permute-start | bytes 1179656 | tf_op jit(solution)/shard_map/ppermute | solution.py:705
  103.4 17.8 %collective-permute-start.32 = (f32[4,48,512]{2,1,0:T(8,128)S(1)}, f32[4,48,512]{2,1,0:T(8,128)S(1)}, u32[]{:S(2)}, u32[]{:S(2)}) collective-permute-start(f32[4,48,512]{2,1,0:T(8,128)S(1)} %get-tuple-element.204), channel_id=1, source_target_pairs={{0,6},{1,7},{2,4},{3,5},{4,2},{5,3},{6,0},{7,1},{8,14},{9,15},{10,... | collective-permute-start | bytes 1179656 | tf_op jit(solution)/shard_map/ppermute | solution.py:705
  121.3 9.9 %collective-permute-start.33 = (f32[4,4,64,512]{3,2,1,0:T(8,128)S(1)}, f32[4,4,64,512]{3,2,1,0:T(8,128)S(1)}, u32[]{:S(2)}, u32[]{:S(2)}) collective-permute-start(f32[4,4,64,512]{3,2,1,0:T(8,128)S(1)} %get-tuple-element.207), channel_id=1, source_target_pairs={{0,1},{1,0},{2,3},{3,2},{4,5},{5,4},{6,7},{7,6},{8,9},{9,8},{10,11... | collective-permute-start | bytes 6291464 | tf_op jit(solution)/shard_map/ppermute | solution.py:705
  132.0 13.4 %collective-permute-start.48 = (f32[2,2,64,512]{3,2,1,0:T(8,128)S(1)}, f32[2,2,64,512]{3,2,1,0:T(8,128)S(1)}, u32[]{:S(2)}, u32[]{:S(2)}) collective-permute-start(f32[2,2,64,512]{3,2,1,0:T(8,128)S(1)} %pad_maximum_fusion), channel_id=1, source_target_pairs={{0,2},{1,3},{2,0},{3,1},{4,6},{5,7},{6,4},{7,5},{8,10},{9,11},{10,... | collective-permute-start | bytes 1572872 | tf_op jit(solution)/shard_map/ppermute | solution.py:705
  133.2 10.0 %collective-permute-start.39 = (f32[48,512]{1,0:T(8,128)S(1)}, f32[48,512]{1,0:T(8,128)S(1)}, u32[]{:S(2)}, u32[]{:S(2)}) collective-permute-start(f32[48,512]{1,0:T(8,128)S(1)} %get-tuple-element.224), channel_id=1, source_target_pairs={{0,16},{8,24},{16,0},{24,8},{1,17},{9,25},{17,1},{25,9},{2,18},{10... | collective-permute-start | bytes 294920 | tf_op jit(solution)/shard_map/ppermute | solution.py:705
  135.3 12.1 %collective-permute-start.51 = (f32[2,2,64,512]{3,2,1,0:T(8,128)S(1)}, f32[2,2,64,512]{3,2,1,0:T(8,128)S(1)}, u32[]{:S(2)}, u32[]{:S(2)}) collective-permute-start(f32[2,2,64,512]{3,2,1,0:T(8,128)S(1)} %pad_maximum_fusion.1), channel_id=1, source_target_pairs={{0,4},{1,5},{2,6},{3,7},{4,0},{5,1},{6,2},{7,3},{8,12},{9,13},{10,... | collective-permute-start | bytes 1572872 | tf_op jit(solution)/shard_map/ppermute | solution.py:705
  154.7 16.0 %collective-permute-start.53 = (f32[64,512]{1,0:T(8,128)S(1)}, f32[64,512]{1,0:T(8,128)S(1)}, u32[]{:S(2)}, u32[]{:S(2)}) collective-permute-start(f32[64,512]{1,0:T(8,128)S(1)} %get-tuple-element.265), channel_id=1, source_target_pairs={{0,16},{8,24},{16,0},{24,8},{1,17},{9,25},{17,1},{25,9},{2,18},{10... | collective-permute-start | bytes 393224 | tf_op jit(solution)/shard_map/ppermute | solution.py:705
  156.5 20.3 %collective-permute-start.54 = (f32[64,512]{1,0:T(8,128)S(1)}, f32[64,512]{1,0:T(8,128)S(1)}, u32[]{:S(2)}, u32[]{:S(2)}) collective-permute-start(f32[64,512]{1,0:T(8,128)S(1)} %get-tuple-element.266), channel_id=1, source_target_pairs={{0,24},{8,16},{16,8},{24,0},{1,25},{9,17},{17,9},{25,1},{2,26},{10... | collective-permute-start | bytes 393224 | tf_op jit(solution)/shard_map/ppermute | solution.py:705
  160.6 16.9 %collective-permute-start.42 = (f32[120,512]{1,0:T(8,128)S(1)}, f32[120,512]{1,0:T(8,128)S(1)}, u32[]{:S(2)}, u32[]{:S(2)}) collective-permute-start(f32[120,512]{1,0:T(8,128)S(1)} %pad_maximum_fusion.4.refs_0_), channel_id=1, source_target_pairs={{0,2},{1,3},{2,0},{3,1},{4,6},{5,7},{6,4},{7,5},{8,10},{9,11},{10,... | collective-permute-start | bytes 737288 | tf_op jit(solution)/shard_map/ppermute | solution.py:705
  161.2 17.2 %collective-permute-start.44 = (f32[120,512]{1,0:T(8,128)S(1)}, f32[120,512]{1,0:T(8,128)S(1)}, u32[]{:S(2)}, u32[]{:S(2)}) collective-permute-start(f32[120,512]{1,0:T(8,128)S(1)} %pad_maximum_fusion.4.refs_0_), channel_id=1, source_target_pairs={{0,4},{1,5},{2,6},{3,7},{4,0},{5,1},{6,2},{7,3},{8,12},{9,13},{10,... | collective-permute-start | bytes 737288 | tf_op jit(solution)/shard_map/ppermute | solution.py:705
  162.1 17.4 %collective-permute-start.46 = (f32[120,512]{1,0:T(8,128)S(1)}, f32[120,512]{1,0:T(8,128)S(1)}, u32[]{:S(2)}, u32[]{:S(2)}) collective-permute-start(f32[120,512]{1,0:T(8,128)S(1)} %pad_maximum_fusion.4.refs_0_), channel_id=1, source_target_pairs={{0,6},{1,7},{2,4},{3,5},{4,2},{5,3},{6,0},{7,1},{8,14},{9,15},{10,... | collective-permute-start | bytes 737288 | tf_op jit(solution)/shard_map/ppermute | solution.py:705
  170.7 15.6 %collective-permute-start.41 = (f32[120,512]{1,0:T(8,128)S(1)}, f32[120,512]{1,0:T(8,128)S(1)}, u32[]{:S(2)}, u32[]{:S(2)}) collective-permute-start(f32[120,512]{1,0:T(8,128)S(1)} %pad_maximum_fusion.4.refs_0_), channel_id=1, source_target_pairs={{0,1},{1,0},{2,3},{3,2},{4,5},{5,4},{6,7},{7,6},{8,9},{9,8},{10,11... | collective-permute-start | bytes 737288 | tf_op jit(solution)/shard_map/ppermute | solution.py:705
  178.3 10.2 %collective-permute-start.60 = (f32[64,512]{1,0:T(8,128)S(1)}, f32[64,512]{1,0:T(8,128)S(1)}, u32[]{:S(2)}, u32[]{:S(2)}) collective-permute-start(f32[64,512]{1,0:T(8,128)S(1)} %fusion.18.refs_8_), channel_id=1, source_target_pairs={{0,6},{1,7},{2,4},{3,5},{4,2},{5,3},{6,0},{7,1},{8,14},{9,15},{10,... | collective-permute-start | bytes 393224 | tf_op jit(solution)/shard_map/ppermute | solution.py:705
  (64 other events, 466.4 us)
